TPU v7x, 32 devices: a whole 2x2x4 slice. The times are simulated.
32 devices in a mesh: dp: 8 (over y, x, core), mp: 4 (over z).
Axes of the slice: x: 2, y: 2, z: 4, core: 2. Of those that a mesh axis runs over, the one named last changes fastest.
Arguments:
- features: bfloat16 [16384, 2, 512], P('dp'), may hold values from -27 to 27
- projection: bfloat16 [512, 256], replicated, may hold values from -1 to 1
- prototypes: float32 [3000, 256], P('mp'), may hold values from -7 to 7
Outputs:
- grad_prototypes: float32 [3000, 256], P('mp')
- grad_projection: float32 [512, 256], replicated
- loss: float32 [], replicated
All inputs are finite; a program needn't handle non-finite values.
Results may differ from a plain program's by a relative error of at most 0.0019.
The roundings to bfloat16 on the way count: a program that leaves them out, or rounds other values in their place, can miss the bound.
Values may be sent and summed in bfloat16 or wider, within the bound.
No kernel may reach another device: no remote copies, remote signals or barrier semaphores. Data moves between devices by JAX's collectives and lax.ppermute only.
A program may use at most 128 MiB of HBM per device.

v0:
```python
import jax
import jax.numpy as jnp
from jax import lax
from jax.sharding import PartitionSpec as P

ITERS = 3


EPSILON_CODES = 0.05
SOFTMAX_TEMPER = 0.1
LOSS_FACTOR = 4096.0
TINY = 1e-06


def unit_rows(values):
    inverse = lax.rsqrt(jnp.sum(values * values, axis=-1, keepdims=True) + TINY)
    return (values * inverse, inverse)


def prototype_totals(values):
    return lax.psum(jnp.sum(values, axis=0), "dp")


def code_totals(values):
    return lax.psum(jnp.sum(values, axis=-1), "mp")


def loss_pieces(
    prototype_logits, softmax_exponent, softmax_denominator, assignments, gradient_factor
):
    swapped_targets = assignments[:, ::-1]
    grad_half = (
        (softmax_exponent / softmax_denominator[..., None] - swapped_targets) * gradient_factor
    ).astype(jnp.bfloat16)
    loss_portion = jnp.sum(
        swapped_targets
        * (prototype_logits * (1.0 / SOFTMAX_TEMPER) - jnp.log(softmax_denominator)[..., None])
    )
    return (grad_half, loss_portion)


def embed_backward(grad_unit, embed_unit, embed_inverse, own_feats):
    along_unit = jnp.sum(embed_unit * grad_unit, axis=-1, keepdims=True)
    grad_raw = ((grad_unit - embed_unit * along_unit) * embed_inverse).astype(jnp.bfloat16)
    return jnp.einsum("bve,bvp->ep", own_feats, grad_raw, preferred_element_type=jnp.float32)


def body(features, projection, prototypes):
    local_rows = features.shape[0]
    own_count = local_rows // lax.axis_size("mp")
    batch_row_count = local_rows * lax.axis_size("dp")
    gradient_factor = LOSS_FACTOR / (2.0 * batch_row_count * SOFTMAX_TEMPER)
    proto_unit, proto_inverse = unit_rows(prototypes)
    proto_half = proto_unit.astype(jnp.bfloat16)
    first_row = lax.axis_index("mp") * own_count
    own_feats = lax.dynamic_slice_in_dim(features, first_row, own_count, 0)
    raw_embed = jnp.einsum("bve,ep->bvp", own_feats, projection, preferred_element_type=jnp.float32)
    embed_unit, embed_inverse = unit_rows(raw_embed)
    embed_half = embed_unit.astype(jnp.bfloat16)
    all_embed = lax.all_gather(embed_half, "mp", axis=0, tiled=True)
    prototype_logits = jnp.einsum(
        "bvp,kp->bvk", all_embed, proto_half, preferred_element_type=jnp.float32
    )
    transport = jnp.exp(prototype_logits * (1.0 / EPSILON_CODES))
    softmax_exponent = jnp.exp(prototype_logits * (1.0 / SOFTMAX_TEMPER))
    soft_part = jnp.sum(softmax_exponent, axis=-1)
    for iteration in range(ITERS - 1):
        transport = transport / prototype_totals(transport)[None]
        transport = transport / code_totals(transport)[..., None]
    transport = transport / prototype_totals(transport)[None]
    softmax_denominator = lax.psum(soft_part, "mp")
    row_sums = code_totals(transport)
    assignments = transport / row_sums[..., None]
    grad_half, loss_portion = loss_pieces(
        prototype_logits, softmax_exponent, softmax_denominator, assignments, gradient_factor
    )
    proto_grad = jnp.einsum("bvk,bvp->kp", grad_half, all_embed, preferred_element_type=jnp.float32)
    proto_grad = lax.psum(proto_grad, "dp")
    grad_unit = lax.psum_scatter(
        jnp.einsum("bvk,kp->bvp", grad_half, proto_half, preferred_element_type=jnp.float32),
        "mp",
        scatter_dimension=0,
        tiled=True,
    )
    weight_part = embed_backward(grad_unit, embed_unit, embed_inverse, own_feats)
    weight_grad, loss_total = lax.psum((weight_part, loss_portion), ("dp", "mp"))
    along_proto = jnp.sum(proto_unit * proto_grad, axis=-1, keepdims=True)
    grad_protos = (proto_grad - proto_unit * along_proto) * proto_inverse
    loss_value = -loss_total / (2.0 * batch_row_count)
    return (grad_protos, weight_grad, loss_value)


def solution(mesh):
    return jax.shard_map(
        body,
        mesh=mesh,
        in_specs=(P("dp", None, None), P(), P("mp", None)),
        out_specs=(P("mp", None), P(), P()),
        check_vma=False,
    )
```

profile of v0, /device:TPU:0, one launch (start us, length us, event | category | flops | bytes accessed | tf_op | source)
XLA Modules:
  0.0 487.4 jit_solution(1023003064711756271)
XLA Ops:
  12.1 47.4 %all-gather.2.cloned.1.call-done = bf16[2048,2,256]{0,2,1:T(8,128)(2,1)} async-done(((bf16[512,2,256]{0,2,1:T(8,128)(2,1)}), bf16[2048,2,256]{0,2,1:T(8,128)(2,1)}) %all-gather.2.cloned.1.call-update) | async-done | bytes 2097168 | tf_op jit(solution)/shard_map/all_gather | solution.py:60
  59.5 8.4 %fusion.12 = (f32[2,750]{1,0:T(2,128)S(1)}, f32[2048,2,750]{0,2,1:T(8,128)}) fusion(bf16[2048,2,256]{0,2,1:T(8,128)(2,1)} %all-gather.2.cloned.1.call-done, f32[750,256]{1,0:T(8,128)} %param.5, f32[750]{0:T(1024)S(1)} %add_rsqrt_fusion), kind=kOutput, calls=%fused_computation.19 | convolution fusion | flops 1579390464 | bytes 15162152 | tf_op jit(solution)/shard_map/bvp,kp->bvk/dot_general | solution.py:61
  67.9 13.8 %psum.71 = f32[2,750]{1,0:T(2,128)S(1)} all-reduce(f32[2,750]{1,0:T(2,128)S(1)} %get-tuple-element.11), channel_id=1, replica_groups=mesh['dp'=8,'mp'=4] {'dp'}, use_global_device_ids=true, to_apply=%region_5.0 | all-reduce | flops 1500 | bytes 12000 | tf_op jit(solution)/shard_map/psum | solution.py:21
  81.7 7.0 %exponential_reduce_fusion = (f32[2048,2]{0,1:T(2,128)S(1)}, f32[2048,2]{0,1:T(2,128)S(1)}) fusion(f32[2048,2,750]{0,2,1:T(8,128)} %get-tuple-element.12, f32[2,750]{1,0:T(2,128)S(1)} %psum.71), kind=kLoop, calls=%fused_computation.18 | loop fusion | flops 15351808 | bytes 12326768 | tf_op jit(solution)/shard_map/reduce_sum | solution.py:66
  88.8 16.8 %psum.72 = f32[2048,2]{0,1:T(2,128)S(1)} all-reduce(f32[2048,2]{0,1:T(2,128)S(1)} %get-tuple-element.4), channel_id=1, replica_groups=mesh['dp'=8,'mp'=4] {'mp'}, use_global_device_ids=true, to_apply=%region_7.0 | all-reduce | flops 4096 | bytes 32768 | tf_op jit(solution)/shard_map/psum | solution.py:25
  105.5 6.7 %fusion.8 = f32[2,750]{1,0:T(2,128)S(1)} fusion(f32[2048,2]{0,1:T(2,128)S(1)} %psum.72, f32[2,750]{1,0:T(2,128)S(1)} %psum.71, f32[2048,2,750]{0,2,1:T(8,128)} %get-tuple-element.12), kind=kLoop, calls=%fused_computation.14 | loop fusion | flops 12286500 | bytes 12316384 | tf_op jit(solution)/shard_map/reduce_sum | solution.py:21
  112.2 12.1 %psum.73 = f32[2,750]{1,0:T(2,128)S(1)} all-reduce(f32[2,750]{1,0:T(2,128)S(1)} %fusion.8), channel_id=1, replica_groups=mesh['dp'=8,'mp'=4] {'dp'}, use_global_device_ids=true, to_apply=%region_9.0 | all-reduce | flops 1500 | bytes 12000 | tf_op jit(solution)/shard_map/psum | solution.py:21
  124.4 7.0 %fusion.9 = f32[2048,2]{0,1:T(2,128)S(1)} fusion(f32[2,750]{1,0:T(2,128)S(1)} %psum.73, f32[2048,2]{0,1:T(2,128)S(1)} %psum.72, f32[2,750]{1,0:T(2,128)S(1)} %psum.71, f32[2048,2,750]{0,2,1:T(8,128)} %get-tuple-element.12), kind=kLoop, calls=%fused_computation.15 | loop fusion | flops 15355904 | bytes 12332768 | tf_op jit(solution)/shard_map/reduce_sum | solution.py:25
  131.3 15.5 %psum.74 = f32[2048,2]{0,1:T(2,128)S(1)} all-reduce(f32[2048,2]{0,1:T(2,128)S(1)} %fusion.9), channel_id=1, replica_groups=mesh['dp'=8,'mp'=4] {'mp'}, use_global_device_ids=true, to_apply=%region_11.0 | all-reduce | flops 4096 | bytes 32768 | tf_op jit(solution)/shard_map/psum | solution.py:25
  146.9 7.1 %fusion.10 = f32[2,750]{1,0:T(2,128)S(1)} fusion(f32[2048,2]{0,1:T(2,128)S(1)} %psum.74, f32[2,750]{1,0:T(2,128)S(1)} %psum.73, f32[2048,2]{0,1:T(2,128)S(1)} %psum.72, f32[2,750]{1,0:T(2,128)S(1)} %psum.71, f32[2048,2,750]{0,2,1:T(8,128)} %get-tuple-element.12), kind=kLoop, calls=%fused_computation.16 | loop fusion | flops 18430500 | bytes 12338768 | tf_op jit(solution)/shard_map/reduce_sum | solution.py:21
  153.9 12.3 %psum.75 = f32[2,750]{1,0:T(2,128)S(1)} all-reduce(f32[2,750]{1,0:T(2,128)S(1)} %fusion.10), channel_id=1, replica_groups=mesh['dp'=8,'mp'=4] {'dp'}, use_global_device_ids=true, to_apply=%region_13.0 | all-reduce | flops 1500 | bytes 12000 | tf_op jit(solution)/shard_map/psum | solution.py:21
  166.2 7.8 %fusion.11 = f32[2048,2]{0,1:T(2,128)S(1)} fusion(f32[2,750]{1,0:T(2,128)S(1)} %psum.75, f32[2048,2]{0,1:T(2,128)S(1)} %psum.74, f32[2,750]{1,0:T(2,128)S(1)} %psum.73, f32[2048,2]{0,1:T(2,128)S(1)} %psum.72, f32[2,750]{1,0:T(2,128)S(1)} %psum.71, f32[2048,2,750]{0,2,1:T(8,128)} %get-tuple-element.12), kind=kLoop, calls=%fused_computation.17 | loop fusion | flops 21499904 | bytes 12355152 | tf_op jit(solution)/shard_map/reduce_sum | solution.py:25
  174.0 16.6 %all-reduce = (f32[2048,2]{0,1:T(2,128)S(1)}, f32[2048,2]{0,1:T(2,128)S(1)}) all-reduce(f32[2048,2]{0,1:T(2,128)S(1)} %fusion.11, f32[2048,2]{0,1:T(2,128)S(1)} %get-tuple-element.3), channel_id=1, replica_groups=mesh['dp'=8,'mp'=4] {'mp'}, use_global_device_ids=true, to_apply=%region_15.0 | all-reduce | flops 8192 | bytes 65536 | tf_op jit(solution)/shard_map/psum | solution.py:25
  190.6 8.0 %fusion.7 = f32[2048,2,750]{0,2,1:T(8,128)S(1)} fusion(f32[2048,2]{0,1:T(2,128)S(1)} %get-tuple-element.5, f32[2,750]{1,0:T(2,128)S(1)} %psum.75, f32[2048,2]{0,1:T(2,128)S(1)} %psum.74, f32[2,750]{1,0:T(2,128)S(1)} %psum.73, f32[2048,2]{0,1:T(2,128)S(1)} %psum.72, f32[2,750]{1,0:T(2,128)S(1)} %psum.71, f32[2048,2,750]{0,2,1:T(8,128)} %get-tuple-element.12), kind=kLoop, calls=%fused_computation.9 | loop fusion | flops 21504000 | bytes 24643152 | tf_op jit(solution)/shard_map/div | solution.py:73
  198.7 8.0 %multiply_reduce_fusion = (f32[]{:T(128)}, bf16[2048,2,750]{0,2,1:T(8,128)(2,1)S(1)}) fusion(f32[2048,2,750]{0,2,1:T(8,128)S(1)} %fusion.7, f32[2048,2,750]{0,2,1:T(8,128)} %get-tuple-element.12, f32[2048,2]{0,1:T(2,128)S(1)} %log.3, f32[2048,2]{0,1:T(2,128)S(1)} %get-tuple-element.6), kind=kLoop, calls=%fused_computation.10 | loop fusion | flops 24576000 | bytes 30752772 | tf_op jit(solution)/shard_map/reduce_sum | solution.py:35
  206.7 2.6 copy-done.1
  209.3 2.7 convolution_bitcast_fusion
  212.0 6.9 %fusion.30 = f32[2048,2,256]{0,2,1:T(8,128)} fusion(bf16[2048,2,750]{0,2,1:T(8,128)(2,1)} %copy-done.1, f32[750,256]{1,0:T(8,128)S(1)} %copy-done.2, f32[750]{0:T(1024)S(1)} %add_rsqrt_fusion), kind=kOutput, calls=%fused_computation.42 | convolution fusion | flops 1573248000 | bytes 11109304 | tf_op jit(solution)/shard_map/bvk,kp->bvp/dot_general | solution.py:80
  219.1 37.7 %psum.79 = f32[]{:T(128)} all-reduce(f32[]{:T(128)} %get-tuple-element.7), channel_id=1, replica_groups=mesh['dp'=8,'mp'=4] {'dp','mp'}, use_global_device_ids=true, to_apply=%region_22.0 | all-reduce | flops 1 | bytes 8 | tf_op jit(solution)/shard_map/psum | solution.py:86
  257.4 7.1 %all-reduce.4.cloned.1.call-done = f32[750,256]{1,0:T(8,128)} async-done(((f32[750,256]{1,0:T(8,128)}), f32[750,256]{1,0:T(8,128)}) %all-reduce.4.cloned.1.call-update) | async-done | bytes 768016 | tf_op jit(solution)/shard_map/psum | solution.py:78
  265.9 77.1 %reduce-scatter.2.cloned.1.call-done = f32[512,2,256]{0,2,1:T(8,128)} async-done(((f32[2048,2,256]{0,2,1:T(8,128)}), f32[512,2,256]{0,2,1:T(8,128)}) %reduce-scatter.2.cloned.1.call-update) | async-done | bytes 1048592 | tf_op jit(solution)/shard_map/reduce_scatter | solution.py:79
  343.0 3.2 fusion.18
  346.2 2.3 subtract_multiply_fusion
  348.4 129.5 %all-reduce.6.cloned.1.call-done = f32[512,256]{1,0:T(8,128)} async-done(((f32[512,256]{1,0:T(8,128)}), f32[512,256]{1,0:T(8,128)}) %all-reduce.6.cloned.1.call-update) | async-done | bytes 524304 | tf_op jit(solution)/shard_map/psum | solution.py:86
  (24 shorter events, 8.3 us)
Async XLA Ops:
  7.2 2.1 copy-start
  7.2 52.3 %all-gather.2.cloned.1.call-start = ((), (), s32[]{:S(2)}) async-start(), calls=%async_computation.1 | async-start | bytes 2621440 | tf_op jit(solution)/shard_map/all_gather | solution.py:60
  10.7 253.8 %all-reduce.4.cloned.1.call-start = ((), (), s32[]{:S(2)}) async-start(), calls=%async_computation.2 | async-start | bytes 1540096 | tf_op jit(solution)/shard_map/psum | solution.py:78
  198.6 10.6 %copy-start.3 = (bf16[2048,2,256]{0,2,1:T(8,128)(2,1)S(1)}, bf16[2048,2,256]{0,2,1:T(8,128)(2,1)}, u32[]{:S(2)}) copy-start(bf16[2048,2,256]{0,2,1:T(8,128)(2,1)} %all-gather.2.cloned.1.call-done) | copy-start | bytes 6291460
  206.7 2.6 copy-start.1
  206.7 5.4 %copy-start.2 = (f32[750,256]{1,0:T(8,128)S(1)}, f32[750,256]{1,0:T(8,128)}, u32[]{:S(2)}) copy-start(f32[750,256]{1,0:T(8,128)} %param.5) | copy-start | bytes 2304004
  212.0 131.0 %reduce-scatter.2.cloned.1.call-start = ((), (), s32[]{:S(2)}) async-start(), calls=%async_computation.3 | async-start | bytes 5242880 | tf_op jit(solution)/shard_map/reduce_scatter | solution.py:79
  219.0 258.9 %all-reduce.6.cloned.1.call-start = ((), (), s32[]{:S(2)}) async-start(), calls=%async_computation.4 | async-start | bytes 1048576 | tf_op jit(solution)/shard_map/psum | solution.py:86
Sparse Core Ops, SparseCore 0:
  10.8 48.6 all-gather.1
  212.1 52.3 all-reduce.3
  266.8 76.1 reduce-scatter.1
  349.5 128.3 all-reduce.5
where the time goes:
time: 488 us; the launch traced here: 487 us
  waiting for transfers between devices  261 us (53%)
  blocking collectives  125 us (26%)
  other arithmetic  57.5 us (12%)
  matrix products  21.7 us (4%)
  between operations  15.7 us (3%)
  local copies, waits for them, and re-layouts  6.48 us (1%)
    psum x1, waiting for transfers between devices, body(): lax.psum((weight_part, loss_portion), ('dp', 'mp'))  129 us
    reduce_scatter x1, waiting for transfers between devices, body(): lax.psum_scatter(jnp.einsum('bvk,kp->bvp', grad_half, proto_half, preferr...  77.1 us
    psum x3, blocking collectives, code_totals(): return lax.psum(jnp.sum(values, axis=-1), 'mp')  48.9 us
    all_gather x1, waiting for transfers between devices, body(): all_embed = lax.all_gather(embed_half, 'mp', axis=0, tiled=True)  47.4 us
    psum x3, blocking collectives, prototype_totals(): return lax.psum(jnp.sum(values, axis=0), 'dp')  38.2 us
    psum x1, blocking collectives, body(): lax.psum((weight_part, loss_portion), ('dp', 'mp'))  37.7 us
    reduce_sum x2, other arithmetic, code_totals(): return lax.psum(jnp.sum(values, axis=-1), 'mp')  14.8 us
    reduce_sum x2, other arithmetic, prototype_totals(): return lax.psum(jnp.sum(values, axis=0), 'dp')  13.8 us
  transfers between devices with their start and end apart: 4, of which 4 were waited for; matrix products, arithmetic and copies ran while one was open for 2% of the time, Pallas kernels for 0%

commit v1 on v0

v1 whole, which is shorter than its diff:
```python
import functools

import jax
import jax.numpy as jnp
from jax import lax
from jax.experimental import pallas as pl
from jax.experimental.pallas import tpu as pltpu
from jax.sharding import PartitionSpec as P

ITERS = 3
EPSILON_CODES = 0.05
SOFTMAX_TEMPER = 0.1
LOSS_FACTOR = 4096.0
TINY = 1e-06
LANES = 128
VMEM_LIMIT = 48 * 1024 * 1024


def swap(values, axis, size, offset):
    return lax.ppermute(values, axis, [(i, i ^ offset) for i in range(size)])


def stages(size, first):
    bits = size.bit_length() - 1
    groups, done = [], 0
    while done < bits:
        width = min(first if not groups else 2, bits - done)
        groups.append((done, width))
        done += width
    return groups


def sum_over(values, axis, first):
    size = lax.axis_size(axis)
    for low, width in stages(size, first):
        parts = [swap(values, axis, size, k << low) for k in range(1, 1 << width)]
        values = functools.reduce(jnp.add, parts, values)
    return values


def scatter_sum(values, axis, first):
    size = lax.axis_size(axis)
    me = lax.axis_index(axis)
    block = values.shape[1:]
    values = values[None]
    for low, width in stages(size, first):
        ways = 1 << width
        rest = values.shape[1] // ways
        values = values.reshape((rest, ways) + block)
        mine = (me >> low) & (ways - 1)
        own = lax.dynamic_index_in_dim(values, mine, 1, keepdims=False)
        for k in range(1, ways):
            out = lax.dynamic_index_in_dim(values, mine ^ k, 1, keepdims=False)
            own = own + swap(out, axis, size, k << low)
        values = own[None]
    return values.reshape(block)


def gather_blocks(values, axis, first):
    size = lax.axis_size(axis)
    me = lax.axis_index(axis)
    block = values.shape
    values = values[None]
    for low, width in reversed(stages(size, first)):
        ways = 1 << width
        mine = (me >> low) & (ways - 1)
        parts = [values] + [swap(values, axis, size, k << low) for k in range(1, ways)]
        out = jnp.zeros((values.shape[0], ways) + block, values.dtype)
        for k, part in enumerate(parts):
            out = lax.dynamic_update_slice_in_dim(out, part[:, None], mine ^ k, 1)
        values = out.reshape((-1,) + block)
    return values


def gather_over(values, axis):
    size = lax.axis_size(axis)
    me = lax.axis_index(axis)
    parts = [values] + [swap(values, axis, size, k) for k in range(1, size)]
    out = jnp.zeros((size,) + values.shape, values.dtype)
    for k, part in enumerate(parts):
        out = lax.dynamic_update_slice_in_dim(out, part[None], me ^ k, 0)
    return out


def logits_of(proto_ref, rows):
    return lax.dot_general(
        proto_ref[...], rows, (((1,), (1,)), ((), ())), preferred_element_type=jnp.float32
    )


def lane_sums(values):
    total = values[:, :LANES]
    for start in range(LANES, values.shape[1], LANES):
        total = total + values[:, start : start + LANES]
    return total


def as_column(row):
    return jnp.transpose(jnp.broadcast_to(row, (LANES, row.shape[1])))


def widen(column, width):
    return jnp.concatenate([column] * (width // LANES), axis=1)


def first_kernel(valid, proto_ref, rows_ref, col_ref, soft_ref, acc_ref):
    view, tile = pl.program_id(0), pl.program_id(1)
    logits = logits_of(proto_ref, rows_ref[0])
    soft = jnp.exp(logits * (1.0 / SOFTMAX_TEMPER))
    keep = lax.broadcasted_iota(jnp.int32, soft.shape, 0) < valid
    soft_ref[...] = jnp.sum(jnp.where(keep, soft, 0.0), axis=0)[None, None]
    part = lane_sums(soft * soft)

    @pl.when(tile == 0)
    def _():
        acc_ref[...] = part

    @pl.when(tile > 0)
    def _():
        acc_ref[...] += part

    @pl.when(tile == pl.num_programs(1) - 1)
    def _():
        col_ref[...] = jnp.sum(jnp.transpose(acc_ref[...]), axis=0)[None, None]


def col_kernel(proto_ref, rows_ref, sums_ref, col_ref, acc_ref):
    view, tile = pl.program_id(0), pl.program_id(1)
    logits = logits_of(proto_ref, rows_ref[0])
    transport = jnp.exp(logits * (1.0 / EPSILON_CODES))
    part = lane_sums(transport * (1.0 / sums_ref[0]))

    @pl.when(tile == 0)
    def _():
        acc_ref[...] = part

    @pl.when(tile > 0)
    def _():
        acc_ref[...] += part

    @pl.when(tile == pl.num_programs(1) - 1)
    def _():
        col_ref[...] = jnp.sum(jnp.transpose(acc_ref[...]), axis=0)[None, None]


def row_kernel(valid, proto_ref, rows_ref, sums_ref, row_ref, scale_ref):
    tile = pl.program_id(1)

    @pl.when(tile == 0)
    def _():
        sums = sums_ref[0]
        keep = lax.broadcasted_iota(jnp.int32, sums.shape, 1) < valid
        scale_ref[...] = as_column(jnp.where(keep, 1.0 / sums, 0.0))

    logits = logits_of(proto_ref, rows_ref[0])
    transport = jnp.exp(logits * (1.0 / EPSILON_CODES))
    scaled = transport * widen(scale_ref[...], transport.shape[1])
    row_ref[...] = jnp.sum(scaled, axis=0)[None, None]


def grad_of(factor, proto_ref, rows_ref, denoms_ref, sums_ref, scale_ref):
    soft, target, logits = [], [], []
    for view in range(2):
        scores = logits_of(proto_ref, rows_ref[view])
        value = jnp.exp(scores * (1.0 / SOFTMAX_TEMPER))
        scaled = value * value * widen(scale_ref[view], scores.shape[1])
        soft.append(value * (factor / denoms_ref[view]))
        target.append(scaled * (1.0 / sums_ref[view]))
        logits.append(scores)
    grads, loss = [], 0.0
    for view in range(2):
        swapped = target[1 - view]
        grads.append((soft[view] - swapped * factor).astype(jnp.bfloat16))
        terms = logits[view] * (1.0 / SOFTMAX_TEMPER) - jnp.log(denoms_ref[view])
        loss = loss + jnp.sum(swapped * terms, axis=0, keepdims=True)
    return grads, loss


def set_scales(valid, block, cols_ref, scale_ref):
    @pl.when(pl.program_id(0) == 0)
    def _():
        for view in range(2):
            sums = cols_ref[view]
            place = lax.broadcasted_iota(jnp.int32, sums.shape, 1)
            keep = lax.rem(place, block) < valid
            scale_ref[view] = as_column(jnp.where(keep, 1.0 / sums, 0.0))


def proto_grad_kernel(
    valid, block, factor, proto_ref, rows_ref, denoms_ref, sums_ref, cols_ref, out_ref, loss_ref, scale_ref
):
    set_scales(valid, block, cols_ref, scale_ref)
    grads, loss = grad_of(factor, proto_ref, rows_ref, denoms_ref, sums_ref, scale_ref)
    part = sum(
        lax.dot_general(
            grads[view], rows_ref[view], (((1,), (0,)), ((), ())), preferred_element_type=jnp.float32
        )
        for view in range(2)
    )
    loss_ref[...] = loss

    @pl.when(pl.program_id(0) == 0)
    def _():
        out_ref[...] = part

    @pl.when(pl.program_id(0) > 0)
    def _():
        out_ref[...] += part


def embed_grad_kernel(
    valid, block, factor, proto_ref, rows_ref, denoms_ref, sums_ref, cols_ref, out_ref, scale_ref
):
    set_scales(valid, block, cols_ref, scale_ref)
    grads, _ = grad_of(factor, proto_ref, rows_ref, denoms_ref, sums_ref, scale_ref)
    for view in range(2):
        out_ref[view] = lax.dot_general(
            grads[view], proto_ref[...], (((0,), (0,)), ((), ())), preferred_element_type=jnp.float32
        )


def whole(shape):
    return pl.BlockSpec(shape, lambda *_: (0,) * len(shape))


def params(grid):
    return pltpu.CompilerParams(
        dimension_semantics=("arbitrary",) * grid, vmem_limit_bytes=VMEM_LIMIT
    )


def cost(protos, rows, products):
    return pl.CostEstimate(
        flops=2 * protos * rows * 256 * products, bytes_accessed=2 * 256 * (protos + rows),
        transcendentals=protos * rows,
    )


def sinkhorn_calls(valid, proto_half, embed_half):
    protos, width = proto_half.shape
    views, rows, _ = embed_half.shape
    tile = min(512, rows)
    grid = (views, rows // tile)
    proto_spec = whole((protos, width))
    rows_spec = pl.BlockSpec((1, tile, width), lambda v, t: (v, t, 0))
    row_spec = pl.BlockSpec((1, 1, tile), lambda v, t: (v, 0, t))
    col_spec = pl.BlockSpec((1, 1, protos), lambda v, t: (v, 0, 0))
    row_shape = jax.ShapeDtypeStruct((views, 1, rows), jnp.float32)
    col_shape = jax.ShapeDtypeStruct((views, 1, protos), jnp.float32)
    column = pltpu.VMEM((protos, LANES), jnp.float32)
    common = dict(grid=grid, compiler_params=params(2), cost_estimate=cost(protos, 2 * rows, 1))
    first = pl.pallas_call(
        functools.partial(first_kernel, valid), in_specs=[proto_spec, rows_spec],
        out_specs=[col_spec, row_spec], out_shape=[col_shape, row_shape],
        scratch_shapes=[column], name="first_totals", **common,
    )
    col = pl.pallas_call(
        col_kernel, in_specs=[proto_spec, rows_spec, row_spec], out_specs=col_spec,
        out_shape=col_shape, scratch_shapes=[column], name="column_totals", **common,
    )
    row = pl.pallas_call(
        functools.partial(row_kernel, valid), in_specs=[proto_spec, rows_spec, col_spec],
        out_specs=row_spec, out_shape=row_shape, scratch_shapes=[column], name="row_totals", **common,
    )
    return (
        lambda: first(proto_half, embed_half),
        lambda sums: col(proto_half, embed_half, sums),
        lambda sums: row(proto_half, embed_half, sums),
    )


def grad_call(kernel, tile, loss, proto_half, embed_half, denoms, row_sums, col_sums, **names):
    protos, width = proto_half.shape
    views, rows, _ = embed_half.shape
    tile = min(tile, rows)
    row_spec = pl.BlockSpec((views, 1, tile), lambda t: (0, 0, t))
    rows_spec = pl.BlockSpec((views, tile, width), lambda t: (0, t, 0))
    if loss:
        out_specs = [whole((protos, width)), pl.BlockSpec((1, tile), lambda t: (0, t))]
        out_shape = [
            jax.ShapeDtypeStruct((protos, width), jnp.float32),
            jax.ShapeDtypeStruct((1, rows), jnp.float32),
        ]
    else:
        out_specs = rows_spec
        out_shape = jax.ShapeDtypeStruct((views, rows, width), jnp.float32)
    return pl.pallas_call(
        kernel, grid=(rows // tile,),
        in_specs=[
            whole((protos, width)), rows_spec, row_spec, row_spec, whole((views, 1, protos)),
        ],
        out_specs=out_specs, out_shape=out_shape,
        scratch_shapes=[pltpu.VMEM((views, protos, LANES), jnp.float32)],
        compiler_params=params(1), cost_estimate=cost(protos, 2 * rows, 2), **names,
    )(proto_half, embed_half, denoms, row_sums, col_sums)


def unit_rows(values):
    inverse = lax.rsqrt(jnp.sum(values * values, axis=-1, keepdims=True) + TINY)
    return (values * inverse, inverse)


def body(features, projection, prototypes):
    local_rows = features.shape[0]
    shards = lax.axis_size("dp")
    own_count = local_rows // lax.axis_size("mp")
    batch_row_count = local_rows * shards
    factor = LOSS_FACTOR / (2.0 * batch_row_count * SOFTMAX_TEMPER)
    valid, width = prototypes.shape
    block = -(-valid // LANES) * LANES
    first_row = lax.axis_index("mp") * own_count

    proto_unit, proto_inverse = unit_rows(prototypes)
    proto_half = jnp.pad(proto_unit.astype(jnp.bfloat16), ((0, block - valid), (0, 0)))
    all_proto = lax.all_gather(proto_half, "mp", axis=0, tiled=True)

    raw_embed = jnp.einsum("bve,ep->vbp", features, projection, preferred_element_type=jnp.float32)
    embed_unit, embed_inverse = unit_rows(raw_embed)
    embed_half = embed_unit.astype(jnp.bfloat16)

    first, col, row = sinkhorn_calls(valid, proto_half, embed_half)
    col_part, soft_part = first()
    col_sums = sum_over(col_part, "dp", 1)
    both = sum_over(jnp.concatenate([row(col_sums), soft_part]), "mp", 2)
    row_sums, denoms = both[:2], both[2:]
    for iteration in range(1, ITERS):
        col_sums = sum_over(col(row_sums), "dp", 1)
        row_sums = sum_over(row(col_sums), "mp", 2)

    own = functools.partial(lax.dynamic_slice_in_dim, start_index=first_row, slice_size=own_count)
    all_cols = gather_over(col_sums, "mp")
    all_cols = jnp.transpose(all_cols, (1, 2, 0, 3)).reshape(2, 1, -1)
    grad_unit = grad_call(
        functools.partial(embed_grad_kernel, valid, block, factor), 128, False,
        all_proto, own(embed_half, axis=1), own(denoms, axis=2), own(row_sums, axis=2), all_cols,
        name="embed_gradient",
    )
    own_unit, own_inverse = own(embed_unit, axis=1), own(embed_inverse, axis=1)
    along_unit = jnp.sum(own_unit * grad_unit, axis=-1, keepdims=True)
    grad_raw = ((grad_unit - own_unit * along_unit) * own_inverse).astype(jnp.bfloat16)
    weight_part = jnp.einsum(
        "bve,vbp->ep", own(features, axis=0), grad_raw, preferred_element_type=jnp.float32
    )

    proto_part, loss_rows = grad_call(
        functools.partial(proto_grad_kernel, valid, block, factor), 256, True,
        proto_half, embed_half, denoms, row_sums, col_sums, name="proto_gradient",
    )
    loss_row = jnp.broadcast_to(jnp.sum(loss_rows), (shards, 8, width))

    weight_part = jnp.concatenate([weight_part.reshape(shards, -1, width), loss_row], axis=1)
    weight_sum = sum_over(scatter_sum(weight_part, "dp", 1), "mp", 2)
    loss_value = -weight_sum[-1, 0] / (2.0 * batch_row_count)
    weight_grad = gather_blocks(weight_sum[:-8], "dp", 1).reshape(projection.shape)

    proto_sum = scatter_sum(proto_part.reshape(shards, -1, width), "dp", 1)
    proto_grad = gather_blocks(proto_sum, "dp", 1).reshape(block, width)[:valid]
    along_proto = jnp.sum(proto_unit * proto_grad, axis=-1, keepdims=True)
    grad_protos = (proto_grad - proto_unit * along_proto) * proto_inverse
    return (grad_protos, weight_grad, loss_value)


def solution(mesh):
    return jax.shard_map(
        body,
        mesh=mesh,
        in_specs=(P("dp", None, None), P(), P("mp", None)),
        out_specs=(P("mp", None), P(), P()),
        check_vma=False,
    )
```

time: 488 us -> 175 us (0.36)
  waiting for transfers between devices: 261 us -> 42.6 us
  blocking collectives: 125 us -> 0 us
  other arithmetic: 57.5 us -> 6.15 us
  starting transfers between devices: 0.16 us -> 49.3 us
  Pallas kernels: 0 us -> 42.2 us
  matrix products: 21.7 us -> 7.68 us
    psum x2 -> x0, waiting for transfers between devices: 137 us -> none  [the longest x1 129 us: body(): lax.psum((weight_part, loss_portion), ('dp', 'mp'))]
    psum x7 -> x0, blocking collectives: 125 us -> none  [the longest x3 48.9 us: code_totals(): return lax.psum(jnp.sum(values, axis=-1), 'mp')]
    reduce_scatter x1 -> x0, waiting for transfers between devices: 77.1 us -> none  [body(): lax.psum_scatter(jnp.einsum('bvk,kp->bvp', grad_half, proto_half, preferr...]
    ppermute x0 -> x43, starting transfers between devices: none -> 49.3 us  [swap(): return lax.ppermute(values, axis, [(i, i ^ offset) for i in range(size)])]
    all_gather x1, waiting for transfers between devices: 47.4 us -> 0.02 us  [body(): all_proto = lax.all_gather(proto_half, 'mp', axis=0, tiled=True)]
    reduce_sum x6 -> x1, other arithmetic: 43.6 us -> 0.62 us  [body(): loss_row = jnp.broadcast_to(jnp.sum(loss_rows), (shards, 8, width))]
    ppermute x0 -> x43, waiting for transfers between devices: none -> 42.5 us  [swap(): return lax.ppermute(values, axis, [(i, i ^ offset) for i in range(size)])]
    pallas_call x0 -> x8, Pallas kernels: none -> 42.2 us  [the longest x2 16.1 us: grad_call(): pl.pallas_call(kernel, grid=(rows // tile,), in_specs=[whole((protos, wid...]
  transfers between devices with their start and end apart: 4 -> 44, of which waited for: 4 -> 29; matrix products, arithmetic and copies ran while one was open for 2% -> 8% of each run, Pallas kernels for 0% -> 9%
where the time goes in v1:
time: 175 us
  starting transfers between devices  49.3 us (28%)
  waiting for transfers between devices  42.6 us (24%)
  Pallas kernels  42.2 us (24%)
  between operations  16.4 us (9%)
  local copies, waits for them, and re-layouts  10.9 us (6%)
  matrix products  7.68 us (4%)
  other arithmetic  6.15 us (4%)
    ppermute x43, starting transfers between devices, swap(): return lax.ppermute(values, axis, [(i, i ^ offset) for i in range(size)])  49.3 us
    ppermute x43, waiting for transfers between devices, swap(): return lax.ppermute(values, axis, [(i, i ^ offset) for i in range(size)])  42.5 us
    pallas_call x2, Pallas kernels, grad_call(): pl.pallas_call(kernel, grid=(rows // tile,), in_specs=[whole((protos, wid...  16.1 us
    pallas_call x3, Pallas kernels, sinkhorn_calls(): row(proto_half, embed_half, sums)  12.7 us
    pallas_call x2, Pallas kernels, sinkhorn_calls(): col(proto_half, embed_half, sums)  8.67 us
    pallas_call x1, Pallas kernels, sinkhorn_calls(): first(proto_half, embed_half)  4.76 us
    dot_general x1, matrix products, body(): jnp.einsum('bve,vbp->ep', own(features, axis=0), grad_raw, preferred_elem...  4.15 us
    unnamed x16, local copies, waits for them, and re-layouts  4.09 us
  transfers between devices with their start and end apart: 44, of which 29 were waited for; matrix products, arithmetic and copies ran while one was open for 8% of the time, Pallas kernels for 9%

profile of v1, /device:TPU:0, one launch (start us, length us, event | category | flops | bytes accessed | tf_op | source)
XLA Modules:
  0.0 175.1 jit_solution(16288625229662161376)
XLA Ops:
  8.1 3.5 %fusion.1 = (f32[2,2048]{1,0:T(2,128)S(1)}, f32[256,2048,2]{0,1,2:T(8,128)S(1)}) fusion(bf16[2048,2,512]{2,1,0:T(2,128)(2,1)} %param.3, bf16[512,256]{1,0:T(8,128)(2,1)S(1)} %copy-done), kind=kOutput, calls=%fused_computation.3 | convolution fusion | flops 1075834880 | bytes 8667136 | tf_op jit(solution)/shard_map/bve,ep->vbp/dot_general | solution.py:317
  12.1 2.3 %fusion.19 = (bf16[2,2048,256]{2,1,0:T(8,128)(2,1)S(1)}, f32[2,2048,256]{2,1,0:T(8,128)}) fusion(f32[2,2048]{1,0:T(2,128)S(1)} %add_rsqrt_fusion, f32[256,2048,2]{0,1,2:T(8,128)S(1)} %get-tuple-element.24), kind=kLoop, calls=%fused_computation.63 | loop fusion | flops 2097152 | bytes 10502144 | tf_op jit(solution)/shard_map/convert_element_type | solution.py:319
  14.4 4.8 %first_totals.1 = (f32[2,1,768]{2,1,0:T(1,128)S(1)}, f32[2,1,2048]{2,1,0:T(1,128)S(1)}) custom-call(bf16[768,256]{1,0:T(8,128)(2,1)S(1)} %pad.5.proto_ref, bf16[2,2048,256]{2,1,0:T(8,128)(2,1)S(1)} %get-tuple-element.13.rows_ref), custom_call_target="tpu_custom_call" | custom-call | flops 1610612736 | bytes 2490368 | tf_op jit(solution)/shard_map/first_totals/pallas_call | solution.py:266
  20.6 2.9 %collective-permute-start.1 = (f32[2,1,768]{2,1,0:T(1,128)S(1)}, f32[2,1,768]{2,1,0:T(1,128)S(1)}, u32[]{:S(2)}, u32[]{:S(2)}) collective-permute-start(f32[2,1,768]{2,1,0:T(1,128)S(1)} %add.191), channel_id=1, source_target_pairs={{0,8},{4,12},{8,0},{12,4},{16,24},{20,28},{24,16},{28,20},{1,9},{5... | collective-permute-start | bytes 18440 | tf_op jit(solution)/shard_map/ppermute | solution.py:20
  27.1 2.4 %collective-permute-done.3 = f32[2,1,768]{2,1,0:T(1,128)S(1)} collective-permute-done((f32[2,1,768]{2,1,0:T(1,128)S(1)}, f32[2,1,768]{2,1,0:T(1,128)S(1)}, u32[]{:S(2)}, u32[]{:S(2)}) %collective-permute-start.3) | collective-permute-done | bytes 6176 | tf_op jit(solution)/shard_map/ppermute | solution.py:20
  29.5 4.2 %row_totals.3 = f32[2,1,2048]{2,1,0:T(1,128)S(1)} custom-call(bf16[768,256]{1,0:T(8,128)(2,1)S(1)} %pad.5.proto_ref, bf16[2,2048,256]{2,1,0:T(8,128)(2,1)S(1)} %get-tuple-element.13.rows_ref, f32[2,1,768]{2,1,0:T(1,128)S(1)} %add_add_fusion.7.sums_ref), custom_call_target="tpu_custom_call" | custom-call | flops 1610612736 | bytes 2490368 | tf_op jit(solution)/shard_map/row_totals/pallas_call | solution.py:268
  35.4 2.6 %collective-permute-start.5 = (f32[4,1,2048]{2,1,0:T(1,128)S(1)}, f32[4,1,2048]{2,1,0:T(1,128)S(1)}, u32[]{:S(2)}, u32[]{:S(2)}) collective-permute-start(f32[4,1,2048]{2,1,0:T(1,128)S(1)} %pad_maximum_fusion), channel_id=1, source_target_pairs={{0,2},{1,3},{2,0},{3,1},{4,6},{5,7},{6,4},{7,5},{8,10},{9,11},{10,... | collective-permute-start | bytes 98312 | tf_op jit(solution)/shard_map/ppermute | solution.py:20
  38.2 2.6 %collective-permute-done.5 = f32[4,1,2048]{2,1,0:T(1,128)S(1)} collective-permute-done((f32[4,1,2048]{2,1,0:T(1,128)S(1)}, f32[4,1,2048]{2,1,0:T(1,128)S(1)}, u32[]{:S(2)}, u32[]{:S(2)}) %collective-permute-start.5) | collective-permute-done | bytes 32800 | tf_op jit(solution)/shard_map/ppermute | solution.py:20
  40.8 2.9 %collective-permute-done.6 = f32[4,1,2048]{2,1,0:T(1,128)S(1)} collective-permute-done((f32[4,1,2048]{2,1,0:T(1,128)S(1)}, f32[4,1,2048]{2,1,0:T(1,128)S(1)}, u32[]{:S(2)}, u32[]{:S(2)}) %collective-permute-start.6) | collective-permute-done | bytes 32800 | tf_op jit(solution)/shard_map/ppermute | solution.py:20
  43.8 4.3 %column_totals.2 = f32[2,1,768]{2,1,0:T(1,128)S(1)} custom-call(bf16[768,256]{1,0:T(8,128)(2,1)S(1)} %pad.5.proto_ref, bf16[2,2048,256]{2,1,0:T(8,128)(2,1)S(1)} %get-tuple-element.13.rows_ref, f32[2,1,2048]{2,1,0:T(1,128)S(1)} %get-tuple-element.21.sums_ref), custom_call_target="tpu_custom_call" | custom-call | flops 1610612736 | bytes 2490368 | tf_op jit(solution)/shard_map/column_totals/pallas_call | solution.py:267
  55.1 4.2 %row_totals.4 = f32[2,1,2048]{2,1,0:T(1,128)S(1)} custom-call(bf16[768,256]{1,0:T(8,128)(2,1)S(1)} %pad.5.proto_ref, bf16[2,2048,256]{2,1,0:T(8,128)(2,1)S(1)} %get-tuple-element.13.rows_ref, f32[2,1,768]{2,1,0:T(1,128)S(1)} %add_add_fusion.6.sums_ref), custom_call_target="tpu_custom_call" | custom-call | flops 1610612736 | bytes 2490368 | tf_op jit(solution)/shard_map/row_totals/pallas_call | solution.py:268
  60.3 3.5 %collective-permute-start.13 = (f32[2,1,2048]{2,1,0:T(1,128)S(1)}, f32[2,1,2048]{2,1,0:T(1,128)S(1)}, u32[]{:S(2)}, u32[]{:S(2)}) collective-permute-start(f32[2,1,2048]{2,1,0:T(1,128)S(1)} %row_totals.4), channel_id=1, source_target_pairs={{0,3},{1,2},{2,1},{3,0},{4,7},{5,6},{6,5},{7,4},{8,11},{9,10},{10,... | collective-permute-start | bytes 49160 | tf_op jit(solution)/shard_map/ppermute | solution.py:20
  65.9 4.3 %column_totals.3 = f32[2,1,768]{2,1,0:T(1,128)S(1)} custom-call(bf16[768,256]{1,0:T(8,128)(2,1)S(1)} %pad.5.proto_ref, bf16[2,2048,256]{2,1,0:T(8,128)(2,1)S(1)} %get-tuple-element.13.rows_ref, f32[2,1,2048]{2,1,0:T(1,128)S(1)} %add_add_fusion.4.sums_ref), custom_call_target="tpu_custom_call" | custom-call | flops 1610612736 | bytes 2490368 | tf_op jit(solution)/shard_map/column_totals/pallas_call | solution.py:267
  75.7 2.4 %collective-permute-done.17 = f32[2,1,768]{2,1,0:T(1,128)S(1)} collective-permute-done((f32[2,1,768]{2,1,0:T(1,128)S(1)}, f32[2,1,768]{2,1,0:T(1,128)S(1)}, u32[]{:S(2)}, u32[]{:S(2)}) %collective-permute-start.17) | collective-permute-done | bytes 6176 | tf_op jit(solution)/shard_map/ppermute | solution.py:20
  78.1 4.2 %row_totals.5 = f32[2,1,2048]{2,1,0:T(1,128)S(1)} custom-call(bf16[768,256]{1,0:T(8,128)(2,1)S(1)} %pad.5.proto_ref, bf16[2,2048,256]{2,1,0:T(8,128)(2,1)S(1)} %get-tuple-element.13.rows_ref, f32[2,1,768]{2,1,0:T(1,128)S(1)} %add_add_fusion.5.sums_ref.cols_ref), custom_call_target="tpu_custom_call" | custom-call | flops 1610612736 | bytes 2490368 | tf_op jit(solution)/shard_map/row_totals/pallas_call | solution.py:268
  82.6 3.8 %collective-permute-start.19 = (f32[2,1,2048]{2,1,0:T(1,128)S(1)}, f32[2,1,2048]{2,1,0:T(1,128)S(1)}, u32[]{:S(2)}, u32[]{:S(2)}) collective-permute-start(f32[2,1,2048]{2,1,0:T(1,128)S(1)} %row_totals.5), channel_id=1, source_target_pairs={{0,2},{1,3},{2,0},{3,1},{4,6},{5,7},{6,4},{7,5},{8,10},{9,11},{10,... | collective-permute-start | bytes 49160 | tf_op jit(solution)/shard_map/ppermute | solution.py:20
  88.2 3.8 %collective-permute-done.20 = f32[2,1,2048]{2,1,0:T(1,128)S(1)} collective-permute-done((f32[2,1,2048]{2,1,0:T(1,128)S(1)}, f32[2,1,2048]{2,1,0:T(1,128)S(1)}, u32[]{:S(2)}, u32[]{:S(2)}) %collective-permute-start.20) | collective-permute-done | bytes 16416 | tf_op jit(solution)/shard_map/ppermute | solution.py:20
  93.0 8.9 %proto_gradient.1 = (f32[768,256]{1,0:T(8,128)S(1)}, f32[1,2048]{1,0:T(1,128)S(1)}) custom-call(bf16[768,256]{1,0:T(8,128)(2,1)S(1)} %copy-done.2, bf16[2,2048,256]{2,1,0:T(8,128)(2,1)S(1)} %get-tuple-element.13.rows_ref, f32[2,1,2048]{2,1,0:T(1,128)S(1)} %get-tuple-element.22.denoms_ref, f32[2,1,2048]{2,1,0:T(1,128)S(1)} %add_add_fusion.3.sums_ref, ...), custom_call_target="tpu_custom_call" | custom-call | flops 3221225472 | bytes 2490368 | tf_op jit(solution)/shard_map/proto_gradient/pallas_call | solution.py:287
  103.6 3.0 %constant_dynamic-slice_fusion.7 = bf16[512,2,512]{2,1,0:T(2,128)(2,1)} fusion(bf16[2048,2,512]{2,1,0:T(2,128)(2,1)} %param.3, s32[]{:T(128)S(6)} %select_n.66), kind=kLoop, calls=%fused_computation.54 | loop fusion | bytes 2097156 | tf_op jit(solution)/shard_map/dynamic_slice | solution.py:342
  107.5 3.5 %collective-permute-start.31 = (f32[2,1,768]{2,1,0:T(1,128)S(1)}, f32[2,1,768]{2,1,0:T(1,128)S(1)}, u32[]{:S(2)}, u32[]{:S(2)}) collective-permute-start(f32[2,1,768]{2,1,0:T(1,128)S(1)} %add_add_fusion.5.sums_ref.cols_ref), channel_id=1, source_target_pairs={{0,3},{1,2},{2,1},{3,0},{4,7},{5,6},{6,5},{7,4},{8,11},{9,10},{10,... | collective-permute-start | bytes 18440 | tf_op jit(solution)/shard_map/ppermute | solution.py:20
  116.8 3.1 %collective-permute-done.23 = f32[1,96,256]{2,1,0:T(8,128)S(1)} collective-permute-done((f32[1,96,256]{2,1,0:T(8,128)S(1)}, f32[1,96,256]{2,1,0:T(8,128)S(1)}, u32[]{:S(2)}, u32[]{:S(2)}) %collective-permute-start.23) | collective-permute-done | bytes 98336 | tf_op jit(solution)/shard_map/ppermute | solution.py:20
  127.7 7.2 %embed_gradient.1 = f32[2,512,256]{2,1,0:T(8,128)S(1)} custom-call(bf16[3072,256]{1,0:T(8,128)(2,1)S(1)} %copy-done.4, bf16[2,512,256]{2,1,0:T(8,128)(2,1)S(1)} %copy-done.3, f32[2,1,512]{2,1,0:T(1,128)S(1)} %constant_dynamic-slice_fusion.5.denoms_ref, f32[2,1,512]{2,1,0:T(1,128)S(1)} %constant_dynamic-slice_fusion.4.sums_ref, ...), custom_call_target="tpu_custom_call" | custom-call | flops 3221225472 | bytes 2097152 | tf_op jit(solution)/shard_map/embed_gradient/pallas_call | solution.py:287
  134.9 4.2 %fusion.8 = f32[512,256,1]{1,0,2:T(8,128)S(1)} fusion(f32[2,512,256]{2,1,0:T(8,128)S(1)} %embed_gradient.1, bf16[512,2,512]{2,1,0:T(2,128)(2,1)} %constant_dynamic-slice_fusion.7, f32[2,2048,256]{2,1,0:T(8,128)} %get-tuple-element.14, s32[]{:T(128)S(6)} %select_n.66, f32[2,512]{1,0:T(2,128)S(1)} %constant_dynamic-slice_fusion.3), kind=kOutput, calls=%fused_computation.10 | convolution fusion | flops 269747456 | bytes 5772288 | tf_op jit(solution)/shard_map/bve,vbp->ep/dot_general | solution.py:341
  150.1 2.9 %collective-permute-start.38 = (f32[72,256]{1,0:T(8,128)S(1)}, f32[72,256]{1,0:T(8,128)S(1)}, u32[]{:S(2)}, u32[]{:S(2)}) collective-permute-start(f32[72,256]{1,0:T(8,128)S(1)} %add_bitcast_fusion), channel_id=1, source_target_pairs={{0,3},{1,2},{2,1},{3,0},{4,7},{5,6},{6,5},{7,4},{8,11},{9,10},{10,... | collective-permute-start | bytes 221192 | tf_op jit(solution)/shard_map/ppermute | solution.py:20
  (149 shorter events, 67.1 us)
Async XLA Ops:
  7.2 119.1 %all-gather.2.cloned.1.call-start = ((), (), s32[]{:S(2)}) async-start(), calls=%async_computation | async-start | bytes 1966080 | tf_op jit(solution)/shard_map/all_gather | solution.py:315
  35.4 5.4 %collective-permute-start.5 = (f32[4,1,2048]{2,1,0:T(1,128)S(1)}, f32[4,1,2048]{2,1,0:T(1,128)S(1)}, u32[]{:S(2)}, u32[]{:S(2)}) collective-permute-start(f32[4,1,2048]{2,1,0:T(1,128)S(1)} %pad_maximum_fusion), channel_id=1, source_target_pairs={{0,2},{1,3},{2,0},{3,1},{4,6},{5,7},{6,4},{7,5},{8,10},{9,11},{10,... | collective-permute-start | bytes 98312 | tf_op jit(solution)/shard_map/ppermute | solution.py:20
  38.0 5.7 %collective-permute-start.6 = (f32[4,1,2048]{2,1,0:T(1,128)S(1)}, f32[4,1,2048]{2,1,0:T(1,128)S(1)}, u32[]{:S(2)}, u32[]{:S(2)}) collective-permute-start(f32[4,1,2048]{2,1,0:T(1,128)S(1)} %pad_maximum_fusion), channel_id=1, source_target_pairs={{0,3},{1,2},{2,1},{3,0},{4,7},{5,6},{6,5},{7,4},{8,11},{9,10},{10,... | collective-permute-start | bytes 98312 | tf_op jit(solution)/shard_map/ppermute | solution.py:20
  59.4 4.7 %collective-permute-start.12 = (f32[2,1,2048]{2,1,0:T(1,128)S(1)}, f32[2,1,2048]{2,1,0:T(1,128)S(1)}, u32[]{:S(2)}, u32[]{:S(2)}) collective-permute-start(f32[2,1,2048]{2,1,0:T(1,128)S(1)} %row_totals.4), channel_id=1, source_target_pairs={{0,2},{1,3},{2,0},{3,1},{4,6},{5,7},{6,4},{7,5},{8,10},{9,11},{10,... | collective-permute-start | bytes 49160 | tf_op jit(solution)/shard_map/ppermute | solution.py:20
  60.3 5.5 %collective-permute-start.13 = (f32[2,1,2048]{2,1,0:T(1,128)S(1)}, f32[2,1,2048]{2,1,0:T(1,128)S(1)}, u32[]{:S(2)}, u32[]{:S(2)}) collective-permute-start(f32[2,1,2048]{2,1,0:T(1,128)S(1)} %row_totals.4), channel_id=1, source_target_pairs={{0,3},{1,2},{2,1},{3,0},{4,7},{5,6},{6,5},{7,4},{8,11},{9,10},{10,... | collective-permute-start | bytes 49160 | tf_op jit(solution)/shard_map/ppermute | solution.py:20
  82.6 5.5 %collective-permute-start.19 = (f32[2,1,2048]{2,1,0:T(1,128)S(1)}, f32[2,1,2048]{2,1,0:T(1,128)S(1)}, u32[]{:S(2)}, u32[]{:S(2)}) collective-permute-start(f32[2,1,2048]{2,1,0:T(1,128)S(1)} %row_totals.5), channel_id=1, source_target_pairs={{0,2},{1,3},{2,0},{3,1},{4,6},{5,7},{6,4},{7,5},{8,10},{9,11},{10,... | collective-permute-start | bytes 49160 | tf_op jit(solution)/shard_map/ppermute | solution.py:20
  86.5 5.5 %collective-permute-start.20 = (f32[2,1,2048]{2,1,0:T(1,128)S(1)}, f32[2,1,2048]{2,1,0:T(1,128)S(1)}, u32[]{:S(2)}, u32[]{:S(2)}) collective-permute-start(f32[2,1,2048]{2,1,0:T(1,128)S(1)} %row_totals.5), channel_id=1, source_target_pairs={{0,3},{1,2},{2,1},{3,0},{4,7},{5,6},{6,5},{7,4},{8,11},{9,10},{10,... | collective-permute-start | bytes 49160 | tf_op jit(solution)/shard_map/ppermute | solution.py:20
  102.7 8.2 %collective-permute-start.21 = (f32[4,96,256]{2,1,0:T(8,128)}, f32[4,96,256]{2,1,0:T(8,128)}, u32[]{:S(2)}, u32[]{:S(2)}) collective-permute-start(f32[4,96,256]{2,1,0:T(8,128)} %dynamic-slice_bitcast_fusion), channel_id=1, source_target_pairs={{0,4},{4,0},{8,12},{12,8},{16,20},{20,16},{24,28},{28,24},{1,5},{5... | collective-permute-start | bytes 1179656 | tf_op jit(solution)/shard_map/ppermute | solution.py:20
  106.6 7.5 %collective-permute-start.29 = (f32[2,1,768]{2,1,0:T(1,128)S(1)}, f32[2,1,768]{2,1,0:T(1,128)S(1)}, u32[]{:S(2)}, u32[]{:S(2)}) collective-permute-start(f32[2,1,768]{2,1,0:T(1,128)S(1)} %add_add_fusion.5.sums_ref.cols_ref), channel_id=1, source_target_pairs={{0,1},{1,0},{2,3},{3,2},{4,5},{5,4},{6,7},{7,6},{8,9},{9,8},{10,11... | collective-permute-start | bytes 18440 | tf_op jit(solution)/shard_map/ppermute | solution.py:20
  106.6 9.2 %collective-permute-start.30 = (f32[2,1,768]{2,1,0:T(1,128)S(1)}, f32[2,1,768]{2,1,0:T(1,128)S(1)}, u32[]{:S(2)}, u32[]{:S(2)}) collective-permute-start(f32[2,1,768]{2,1,0:T(1,128)S(1)} %add_add_fusion.5.sums_ref.cols_ref), channel_id=1, source_target_pairs={{0,2},{1,3},{2,0},{3,1},{4,6},{5,7},{6,4},{7,5},{8,10},{9,11},{10,... | collective-permute-start | bytes 18440 | tf_op jit(solution)/shard_map/ppermute | solution.py:20
  107.5 8.4 %collective-permute-start.31 = (f32[2,1,768]{2,1,0:T(1,128)S(1)}, f32[2,1,768]{2,1,0:T(1,128)S(1)}, u32[]{:S(2)}, u32[]{:S(2)}) collective-permute-start(f32[2,1,768]{2,1,0:T(1,128)S(1)} %add_add_fusion.5.sums_ref.cols_ref), channel_id=1, source_target_pairs={{0,3},{1,2},{2,1},{3,0},{4,7},{5,6},{6,5},{7,4},{8,11},{9,10},{10,... | collective-permute-start | bytes 18440 | tf_op jit(solution)/shard_map/ppermute | solution.py:20
  112.1 4.7 %collective-permute-start.22 = (f32[1,96,256]{2,1,0:T(8,128)S(1)}, f32[1,96,256]{2,1,0:T(8,128)S(1)}, u32[]{:S(2)}, u32[]{:S(2)}) collective-permute-start(f32[1,96,256]{2,1,0:T(8,128)S(1)} %get-tuple-element.15), channel_id=1, source_target_pairs={{0,8},{4,12},{8,0},{12,4},{16,24},{20,28},{24,16},{28,20},{1,9},{5... | collective-permute-start | bytes 294920 | tf_op jit(solution)/shard_map/ppermute | solution.py:20
  113.6 6.3 %collective-permute-start.23 = (f32[1,96,256]{2,1,0:T(8,128)S(1)}, f32[1,96,256]{2,1,0:T(8,128)S(1)}, u32[]{:S(2)}, u32[]{:S(2)}) collective-permute-start(f32[1,96,256]{2,1,0:T(8,128)S(1)} %get-tuple-element.17), channel_id=1, source_target_pairs={{0,16},{4,20},{8,24},{12,28},{16,0},{20,4},{24,8},{28,12},{1,17},{... | collective-permute-start | bytes 294920 | tf_op jit(solution)/shard_map/ppermute | solution.py:20
  114.1 5.8 %collective-permute-start.24 = (f32[1,96,256]{2,1,0:T(8,128)S(1)}, f32[1,96,256]{2,1,0:T(8,128)S(1)}, u32[]{:S(2)}, u32[]{:S(2)}) collective-permute-start(f32[1,96,256]{2,1,0:T(8,128)S(1)} %get-tuple-element.16), channel_id=1, source_target_pairs={{0,24},{4,28},{8,16},{12,20},{16,8},{20,12},{24,0},{28,4},{1,25},{... | collective-permute-start | bytes 294920 | tf_op jit(solution)/shard_map/ppermute | solution.py:20
  119.9 5.2 %collective-permute-start.25 = (f32[1,96,256]{2,1,0:T(8,128)S(1)}, f32[1,96,256]{2,1,0:T(8,128)S(1)}, u32[]{:S(2)}, u32[]{:S(2)}) collective-permute-start(f32[1,96,256]{2,1,0:T(8,128)S(1)} %get-tuple-element.12), channel_id=1, source_target_pairs={{0,8},{4,12},{8,0},{12,4},{16,24},{20,28},{24,16},{28,20},{1,9},{5... | collective-permute-start | bytes 294920 | tf_op jit(solution)/shard_map/ppermute | solution.py:20
  120.8 5.4 %collective-permute-start.26 = (f32[1,96,256]{2,1,0:T(8,128)S(1)}, f32[1,96,256]{2,1,0:T(8,128)S(1)}, u32[]{:S(2)}, u32[]{:S(2)}) collective-permute-start(f32[1,96,256]{2,1,0:T(8,128)S(1)} %get-tuple-element.12), channel_id=1, source_target_pairs={{0,16},{4,20},{8,24},{12,28},{16,0},{20,4},{24,8},{28,12},{1,17},{... | collective-permute-start | bytes 294920 | tf_op jit(solution)/shard_map/ppermute | solution.py:20
  121.9 17.9 %collective-permute-start.27 = (f32[1,96,256]{2,1,0:T(8,128)S(1)}, f32[1,96,256]{2,1,0:T(8,128)S(1)}, u32[]{:S(2)}, u32[]{:S(2)}) collective-permute-start(f32[1,96,256]{2,1,0:T(8,128)S(1)} %get-tuple-element.12), channel_id=1, source_target_pairs={{0,24},{4,28},{8,16},{12,20},{16,8},{20,12},{24,0},{28,4},{1,25},{... | collective-permute-start | bytes 294920 | tf_op jit(solution)/shard_map/ppermute | solution.py:20
  139.9 5.2 %collective-permute-start.28 = (f32[4,96,256]{2,1,0:T(8,128)S(1)}, f32[4,96,256]{2,1,0:T(8,128)S(1)}, u32[]{:S(2)}, u32[]{:S(2)}) collective-permute-start(f32[4,96,256]{2,1,0:T(8,128)S(1)} %bitcast.83), channel_id=1, source_target_pairs={{0,4},{4,0},{8,12},{12,8},{16,20},{20,16},{24,28},{28,24},{1,5},{5... | collective-permute-start | bytes 1179656 | tf_op jit(solution)/shard_map/ppermute | solution.py:20
  142.4 5.1 %collective-permute-start.34 = (f32[1,72,256]{2,1,0:T(8,128)S(1)}, f32[1,72,256]{2,1,0:T(8,128)S(1)}, u32[]{:S(2)}, u32[]{:S(2)}) collective-permute-start(f32[1,72,256]{2,1,0:T(8,128)S(1)} %get-tuple-element.20), channel_id=1, source_target_pairs={{0,16},{4,20},{8,24},{12,28},{16,0},{20,4},{24,8},{28,12},{1,17},{... | collective-permute-start | bytes 221192 | tf_op jit(solution)/shard_map/ppermute | solution.py:20
  143.3 5.3 %collective-permute-start.35 = (f32[1,72,256]{2,1,0:T(8,128)S(1)}, f32[1,72,256]{2,1,0:T(8,128)S(1)}, u32[]{:S(2)}, u32[]{:S(2)}) collective-permute-start(f32[1,72,256]{2,1,0:T(8,128)S(1)} %get-tuple-element.19), channel_id=1, source_target_pairs={{0,24},{4,28},{8,16},{12,20},{16,8},{20,12},{24,0},{28,4},{1,25},{... | collective-permute-start | bytes 221192 | tf_op jit(solution)/shard_map/ppermute | solution.py:20
  148.6 4.8 %collective-permute-start.36 = (f32[72,256]{1,0:T(8,128)S(1)}, f32[72,256]{1,0:T(8,128)S(1)}, u32[]{:S(2)}, u32[]{:S(2)}) collective-permute-start(f32[72,256]{1,0:T(8,128)S(1)} %add_bitcast_fusion), channel_id=1, source_target_pairs={{0,1},{1,0},{2,3},{3,2},{4,5},{5,4},{6,7},{7,6},{8,9},{9,8},{10,11... | collective-permute-start | bytes 221192 | tf_op jit(solution)/shard_map/ppermute | solution.py:20
  148.7 6.8 %collective-permute-start.37 = (f32[72,256]{1,0:T(8,128)S(1)}, f32[72,256]{1,0:T(8,128)S(1)}, u32[]{:S(2)}, u32[]{:S(2)}) collective-permute-start(f32[72,256]{1,0:T(8,128)S(1)} %add_bitcast_fusion), channel_id=1, source_target_pairs={{0,2},{1,3},{2,0},{3,1},{4,6},{5,7},{6,4},{7,5},{8,10},{9,11},{10,... | collective-permute-start | bytes 221192 | tf_op jit(solution)/shard_map/ppermute | solution.py:20
  150.1 6.2 %collective-permute-start.38 = (f32[72,256]{1,0:T(8,128)S(1)}, f32[72,256]{1,0:T(8,128)S(1)}, u32[]{:S(2)}, u32[]{:S(2)}) collective-permute-start(f32[72,256]{1,0:T(8,128)S(1)} %add_bitcast_fusion), channel_id=1, source_target_pairs={{0,3},{1,2},{2,1},{3,0},{4,7},{5,6},{6,5},{7,4},{8,11},{9,10},{10,... | collective-permute-start | bytes 221192 | tf_op jit(solution)/shard_map/ppermute | solution.py:20
  158.7 5.2 %collective-permute-start.41 = (f32[1,64,256]{2,1,0:T(8,128)S(1)}, f32[1,64,256]{2,1,0:T(8,128)S(1)}, u32[]{:S(2)}, u32[]{:S(2)}) collective-permute-start(f32[1,64,256]{2,1,0:T(8,128)S(1)} %slice_bitcast_fusion), channel_id=1, source_target_pairs={{0,24},{4,28},{8,16},{12,20},{16,8},{20,12},{24,0},{28,4},{1,25},{... | collective-permute-start | bytes 196616 | tf_op jit(solution)/shard_map/ppermute | solution.py:20
  (28 other events, 184.4 us)
Sparse Core Ops, SparseCore 0:
  86.9 37.7 all-gather.1

commit v2 on v0

v2 whole, which is shorter than its diff:
```python
import functools

import jax
import jax.numpy as jnp
from jax import lax
from jax.experimental import pallas as pl
from jax.experimental.pallas import tpu as pltpu
from jax.sharding import PartitionSpec as P

ITERS = 3
EPSILON_CODES = 0.05
SOFTMAX_TEMPER = 0.1
LOSS_FACTOR = 4096.0
TINY = 1e-06
LOG2_E = 1.4426950408889634
LANES = 128
CHUNK = 256
VMEM_LIMIT = 20 * 1024 * 1024


def swap(values, axis, size, offset):
    return lax.ppermute(values, axis, [(i, i ^ offset) for i in range(size)])


def stages(size, first):
    bits = size.bit_length() - 1
    groups, done = [], 0
    while done < bits:
        width = min(first if not groups else 2, bits - done)
        groups.append((done, width))
        done += width
    return groups


def sum_over(values, axis, first):
    size = lax.axis_size(axis)
    for low, width in stages(size, first):
        parts = [swap(values, axis, size, k << low) for k in range(1, 1 << width)]
        values = functools.reduce(jnp.add, parts, values)
    return values


def scatter_sum(values, axis, first):
    size = lax.axis_size(axis)
    me = lax.axis_index(axis)
    block = values.shape[1:]
    values = values[None]
    for low, width in stages(size, first):
        ways = 1 << width
        rest = values.shape[1] // ways
        values = values.reshape((rest, ways) + block)
        mine = (me >> low) & (ways - 1)
        own = lax.dynamic_index_in_dim(values, mine, 1, keepdims=False)
        for k in range(1, ways):
            out = lax.dynamic_index_in_dim(values, mine ^ k, 1, keepdims=False)
            own = own + swap(out, axis, size, k << low)
        values = own[None]
    return values.reshape(block)


def gather_blocks(values, axis, first):
    size = lax.axis_size(axis)
    me = lax.axis_index(axis)
    block = values.shape
    values = values[None]
    for low, width in reversed(stages(size, first)):
        ways = 1 << width
        mine = (me >> low) & (ways - 1)
        parts = [values] + [swap(values, axis, size, k << low) for k in range(1, ways)]
        out = jnp.zeros((values.shape[0], ways) + block, values.dtype)
        for k, part in enumerate(parts):
            out = lax.dynamic_update_slice_in_dim(out, part[:, None], mine ^ k, 1)
        values = out.reshape((-1,) + block)
    return values


NN = (((1,), (0,)), ((), ()))
NT = (((1,), (1,)), ((), ()))


def product(left, right, dims):
    return lax.dot_general(left, right, dims, preferred_element_type=jnp.float32)


def lane_sums(values):
    total = values[:, :LANES]
    for start in range(LANES, values.shape[1], LANES):
        total = total + values[:, start : start + LANES]
    return total


def as_row(column):
    return jnp.sum(jnp.transpose(column), axis=0, keepdims=True)


def as_column(row):
    return jnp.transpose(jnp.broadcast_to(row, (LANES, row.shape[1])))


def widen(column, width):
    return jnp.concatenate([column] * (width // LANES), axis=1)


def column_scale(valid, sums):
    keep = lax.broadcasted_iota(jnp.int32, sums.shape, 1) < valid
    return as_column(jnp.where(keep, 1.0 / sums, 0.0))


def tiles(ref, width, step):
    count = ref.shape[-1] // width

    def one(index, _):
        step(index // count, pl.ds(pl.multiple_of(lax.rem(index, count) * width, width), width))
        return 0

    lax.fori_loop(0, 2 * count, one, 0)


def first_kernel(
    valid, width, feats_ref, proj_ref, proto_ref, soft_ref, raw_ref, half_ref, col_ref, denom_ref, acc_ref
):
    acc_ref[...] = jnp.zeros_like(acc_ref)
    edge = valid // 8 * 8

    def step(view, lanes):
        raw = product(proj_ref[...], feats_ref[view, lanes, :], NT)
        raw_ref[view, :, lanes] = raw
        inverse = lax.rsqrt(jnp.sum(raw * raw, axis=0, keepdims=True) + TINY)
        half = (raw * inverse).astype(jnp.bfloat16)
        half_ref[view, :, lanes] = half
        denom = jnp.zeros((8, width), jnp.float32)
        for start in range(0, proto_ref.shape[0], CHUNK):
            logits = product(proto_ref[start : start + CHUNK], half, NN)
            soft = jnp.exp2(logits * (LOG2_E / SOFTMAX_TEMPER))
            if start + CHUNK > edge:
                place = lax.broadcasted_iota(jnp.int32, soft.shape, 0) + start
                soft = jnp.where(place < valid, soft, 0.0)
            soft_ref[view, start : start + CHUNK, lanes] = soft
            denom = denom + jnp.sum(soft.reshape(-1, 8, width), axis=0)
            acc_ref[view, start : start + CHUNK] += lane_sums(soft * soft)
        denom_ref[view, :, lanes] = jnp.sum(denom, axis=0, keepdims=True)

    tiles(denom_ref, width, step)
    for view in range(2):
        col_ref[view] = as_row(acc_ref[view])


def row_kernel(valid, width, soft_ref, sums_ref, row_ref, scale_ref):
    for view in range(2):
        scale_ref[view] = column_scale(valid, sums_ref[view])

    def step(view, lanes):
        total = jnp.zeros((8, width), jnp.float32)
        for start in range(0, soft_ref.shape[1], 8):
            soft = soft_ref[view, start : start + 8, lanes]
            total = total + soft * soft * widen(scale_ref[view, start : start + 8], width)
        row_ref[view, :, lanes] = jnp.sum(total, axis=0, keepdims=True)

    tiles(row_ref, width, step)


def col_kernel(width, soft_ref, sums_ref, col_ref, acc_ref):
    acc_ref[...] = jnp.zeros_like(acc_ref)

    def step(view, lanes):
        scale = jnp.broadcast_to(1.0 / sums_ref[view, :, lanes], (8, width))
        for start in range(0, soft_ref.shape[1], 8):
            soft = soft_ref[view, start : start + 8, lanes]
            acc_ref[view, start : start + 8] += lane_sums(soft * soft * scale)

    tiles(sums_ref, width, step)
    for view in range(2):
        col_ref[view] = as_row(acc_ref[view])


def grad_kernel(
    valid, width, factor, feats_ref, proto_ref, turned_ref, soft_ref, raw_ref, half_ref, denom_ref, row_ref,
    col_ref, proto_out, proj_out, loss_ref, scale_ref, grad_ref, turn_ref,
):
    for view in range(2):
        scale_ref[view] = column_scale(valid, col_ref[view])
    proto_out[...] = jnp.zeros_like(proto_out)
    turn_ref[...] = jnp.zeros_like(turn_ref)

    def step(index, loss):
        lanes = pl.ds(index * width, width)
        both = lambda ref: jnp.concatenate([ref[view, :, lanes] for view in range(2)], axis=1)
        rows, denoms = factor / both(row_ref), factor / both(denom_ref)
        halves = both(half_ref)
        for start in range(0, proto_ref.shape[0], CHUNK):
            part = slice(start, start + CHUNK)
            logits = product(proto_ref[part], halves, NN)
            softs = [soft_ref[view, part, lanes] for view in range(2)]
            for view in range(2):
                here, there = (slice(at * width, (at + 1) * width) for at in (view, 1 - view))
                target = softs[1 - view] * softs[1 - view] * widen(scale_ref[1 - view, part], width)
                target = target * rows[:, there]
                loss = loss + jnp.sum((logits[:, here] * target).reshape(-1, 8, width), axis=0)
                grad_ref[part, here] = (softs[view] * denoms[:, here] - target).astype(jnp.bfloat16)
        proto_out[...] += product(grad_ref[...], halves, NT)
        raw = both(raw_ref)
        inverse = lax.rsqrt(jnp.sum(raw * raw, axis=0, keepdims=True) + TINY)
        unit = raw * inverse
        grad_unit = product(turned_ref[...], grad_ref[...], NN)
        along = jnp.sum(unit * grad_unit, axis=0, keepdims=True)
        grad_raw = ((grad_unit - unit * along) * inverse).astype(jnp.bfloat16)
        feats = jnp.concatenate([feats_ref[view, lanes, :] for view in range(2)], axis=0)
        turn_ref[...] += product(grad_raw, feats, NN)
        return loss

    loss = jnp.zeros((8, width), jnp.float32)
    for index in range(row_ref.shape[-1] // width):
        loss = step(index, loss)
    proj_out[...] = jnp.transpose(turn_ref[...])
    logs = jnp.log(denom_ref[0]) + jnp.log(denom_ref[1])
    loss = jnp.sum(loss, axis=0, keepdims=True) * (1.0 / (SOFTMAX_TEMPER * factor))
    loss_ref[...] = jnp.broadcast_to(
        jnp.sum(loss, axis=1, keepdims=True) - jnp.sum(logs, axis=1, keepdims=True) * (1.0 / lax.axis_size("mp")),
        loss_ref.shape,
    )


IN_VMEM = pl.BlockSpec(memory_space=pltpu.VMEM)


def call(kernel, name, out_shapes, scratch, work, *args):
    outs = [jax.ShapeDtypeStruct(shape, dtype) for shape, dtype in out_shapes]
    return pl.pallas_call(
        kernel, in_specs=[IN_VMEM] * len(args), out_specs=[IN_VMEM] * len(outs), out_shape=outs,
        scratch_shapes=[pltpu.VMEM(shape, dtype) for shape, dtype in scratch],
        compiler_params=pltpu.CompilerParams(vmem_limit_bytes=VMEM_LIMIT),
        cost_estimate=pl.CostEstimate(flops=work, bytes_accessed=2**20, transcendentals=0), name=name,
    )(*args)


def unit_rows(values):
    inverse = lax.rsqrt(jnp.sum(values * values, axis=-1, keepdims=True) + TINY)
    return (values * inverse, inverse)


def body(features, projection, prototypes):
    rows = features.shape[0]
    shards = lax.axis_size("dp")
    batch_row_count = rows * shards
    factor = LOSS_FACTOR / (2.0 * batch_row_count * SOFTMAX_TEMPER)
    valid, width = prototypes.shape
    block = -(-valid // LANES) * LANES
    single, half_type = jnp.float32, jnp.bfloat16

    proto_unit, proto_inverse = unit_rows(prototypes)
    proto_half = jnp.pad(proto_unit.astype(half_type), ((0, block - valid), (0, 0)))
    feats = jnp.transpose(features, (1, 0, 2))

    row_shape, col_shape = ((2, 1, rows), single), ((2, 1, block), single)
    column = ((2, block, LANES), single)
    work = 4 * rows * block * width
    soft, raw, half, col_part, soft_part = call(
        functools.partial(first_kernel, valid, min(2048, rows)), "first_totals",
        [((2, block, rows), single), ((2, width, rows), single), ((2, width, rows), half_type), col_shape, row_shape],
        [column], work, feats, projection.T, proto_half,
    )
    row_call = functools.partial(
        call, functools.partial(row_kernel, valid, min(512, rows)), "row_totals", [row_shape], [column], work, soft
    )
    col_call = functools.partial(
        call, functools.partial(col_kernel, min(512, rows)), "column_totals", [col_shape], [column], work, soft
    )

    col_sums = sum_over(col_part, "dp", 1)
    both = sum_over(jnp.concatenate([row_call(col_sums)[0], soft_part]), "mp", 2)
    row_sums, denoms = both[:2], both[2:]
    for iteration in range(1, ITERS):
        col_sums = sum_over(col_call(row_sums)[0], "dp", 1)
        row_sums = sum_over(row_call(col_sums)[0], "mp", 2)

    grad_tile = min(512, rows)
    proto_part, proj_part, loss = call(
        functools.partial(grad_kernel, valid, grad_tile, factor), "gradients",
        [((block, width), single), (projection.shape, single), ((8, width), single)],
        [column, ((block, 2 * grad_tile), half_type), (projection.shape[::-1], single)],
        3 * work, feats, proto_half, proto_half.T, soft, raw, half, denoms, row_sums, col_sums,
    )
    loss_rows = jnp.broadcast_to(loss[None], (shards,) + loss.shape)
    proj_part = jnp.concatenate([proj_part.reshape(shards, -1, width), loss_rows], axis=1)
    proj_sum = sum_over(scatter_sum(proj_part, "dp", 1), "mp", 2)
    loss_value = -proj_sum[-1, 0] / (2.0 * batch_row_count)
    proj_grad = gather_blocks(proj_sum[:-8], "dp", 1).reshape(projection.shape)

    proto_sum = scatter_sum(proto_part.reshape(shards, -1, width), "dp", 1)
    proto_grad = gather_blocks(proto_sum, "dp", 1).reshape(block, width)[:valid]
    along_proto = jnp.sum(proto_unit * proto_grad, axis=-1, keepdims=True)
    grad_protos = (proto_grad - proto_unit * along_proto) * proto_inverse
    return (grad_protos, proj_grad, loss_value)


def solution(mesh):
    return jax.shard_map(
        body,
        mesh=mesh,
        in_specs=(P("dp", None, None), P(), P("mp", None)),
        out_specs=(P("mp", None), P(), P()),
        check_vma=False,
    )
```

time: 488 us -> 132 us (0.27)
  waiting for transfers between devices: 261 us -> 35 us
  blocking collectives: 125 us -> 0 us
  other arithmetic: 57.5 us -> 3.29 us
  starting transfers between devices: 0.16 us -> 45 us
  matrix products: 21.7 us -> 0 us
  Pallas kernels: 0 us -> 21.3 us
  local copies, waits for them, and re-layouts: 6.48 us -> 24 us
  between operations: 15.7 us -> 2.98 us
    psum x2 -> x0, waiting for transfers between devices: 137 us -> none  [the longest x1 129 us: body(): lax.psum((weight_part, loss_portion), ('dp', 'mp'))]
    psum x7 -> x0, blocking collectives: 125 us -> none  [the longest x3 48.9 us: code_totals(): return lax.psum(jnp.sum(values, axis=-1), 'mp')]
    reduce_scatter x1 -> x0, waiting for transfers between devices: 77.1 us -> none  [body(): lax.psum_scatter(jnp.einsum('bvk,kp->bvp', grad_half, proto_half, preferr...]
    all_gather x1 -> x0, waiting for transfers between devices: 47.4 us -> none  [body(): all_embed = lax.all_gather(embed_half, 'mp', axis=0, tiled=True)]
    ppermute x0 -> x40, starting transfers between devices: none -> 45 us  [swap(): return lax.ppermute(values, axis, [(i, i ^ offset) for i in range(size)])]
    reduce_sum x6 -> x0, other arithmetic: 43.6 us -> none  [the longest x2 14.8 us: code_totals(): return lax.psum(jnp.sum(values, axis=-1), 'mp')]
    ppermute x0 -> x40, waiting for transfers between devices: none -> 35 us  [swap(): return lax.ppermute(values, axis, [(i, i ^ offset) for i in range(size)])]
    dot_general x5 -> x0, matrix products: 21.7 us -> none  [the longest x1 8.43 us: body(): jnp.einsum('bvp,kp->bvk', all_embed, proto_half, preferred_element_type=j...]
  transfers between devices with their start and end apart: 4 -> 40, of which waited for: 4 -> 23; matrix products, arithmetic and copies ran while one was open for 2% -> 2% of each run, Pallas kernels for 0% -> 0%
where the time goes in v2:
time: 132 us
  starting transfers between devices  45 us (34%)
  waiting for transfers between devices  35 us (27%)
  local copies, waits for them, and re-layouts  24 us (18%)
  Pallas kernels  21.3 us (16%)
  other arithmetic  3.29 us (2%)
  between operations  2.98 us (2%)
    ppermute x40, starting transfers between devices, swap(): return lax.ppermute(values, axis, [(i, i ^ offset) for i in range(size)])  45 us
    ppermute x40, waiting for transfers between devices, swap(): return lax.ppermute(values, axis, [(i, i ^ offset) for i in range(size)])  35 us
    unnamed x32, local copies, waits for them, and re-layouts  22 us
    pallas_call x7, Pallas kernels, call(): pl.pallas_call(kernel, in_specs=[IN_VMEM] * len(args), out_specs=[IN_VMEM...  21.3 us
  transfers between devices with their start and end apart: 40, of which 23 were waited for; matrix products, arithmetic and copies ran while one was open for 2% of the time, Pallas kernels for 0%

profile of v2, /device:TPU:0, one launch (start us, length us, event | category | flops | bytes accessed | tf_op | source)
XLA Modules:
  0.0 131.6 jit_solution(7033640314642838052)
XLA Ops:
  3.9 4.8 %copy.31 = bf16[2048,2,512]{2,0,1:T(8,128)(2,1)} copy(bf16[2048,2,512]{2,1,0:T(2,128)(2,1)} %param.3) | data formatting | bytes 8388608 | tf_op args[0]
  8.9 2.2 %copy-done.2 = bf16[2048,2,512]{2,0,1:T(8,128)(2,1)S(1)} copy-done((bf16[2048,2,512]{2,0,1:T(8,128)(2,1)S(1)}, bf16[2048,2,512]{2,0,1:T(8,128)(2,1)}, u32[]{:S(2)}) %copy-start.2) | copy-done | bytes 4194328
  11.1 4.4 %first_totals.1 = (f32[2,768,2048]{2,1,0:T(8,128)S(1)}, f32[2,256,2048]{2,1,0:T(8,128)S(1)}, bf16[2,256,2048]{2,1,0:T(8,128)(2,1)S(1)}, f32[2,1,768]{2,1,0:T(1,128)S(1)}, f32[2,1,2048]{2,1,0:T(1,128)S(1)}) custom-call(bf16[2,2048,512]{2,1,0:T(8,128)(2,1)S(1)} %bitcast.55, bf16[256,512]{1,0:T(8,128)(2,1)S(1)} %bitcast.61, bf16[768,256]{1,0:T(8,128)(2,1)S(1)} %pad.4.clone.proto_ref), custom_call_target="tpu_custom_call" | custom-call | flops 1610612736 | bytes 1048576 | tf_op jit(solution)/shard_map/first_totals/pallas_call | solution.py:228
  15.6 2.0 %copy-done.4 = f32[2,256,2048]{2,1,0:T(8,128)} copy-done((f32[2,256,2048]{2,1,0:T(8,128)}, f32[2,256,2048]{2,1,0:T(8,128)S(1)}, u32[]{:S(2)}) %copy-start.4) | copy-done | bytes 4194328
  18.8 2.9 %collective-permute-start.1 = (f32[2,1,768]{2,1,0:T(1,128)S(1)}, f32[2,1,768]{2,1,0:T(1,128)S(1)}, u32[]{:S(2)}, u32[]{:S(2)}) collective-permute-start(f32[2,1,768]{2,1,0:T(1,128)S(1)} %add.151), channel_id=1, source_target_pairs={{0,8},{4,12},{8,0},{12,4},{16,24},{20,28},{24,16},{28,20},{1,9},{5... | collective-permute-start | bytes 18440 | tf_op jit(solution)/shard_map/ppermute | solution.py:22
  23.3 2.0 %collective-permute-done.2 = f32[2,1,768]{2,1,0:T(1,128)S(1)} collective-permute-done((f32[2,1,768]{2,1,0:T(1,128)S(1)}, f32[2,1,768]{2,1,0:T(1,128)S(1)}, u32[]{:S(2)}, u32[]{:S(2)}) %collective-permute-start.2) | collective-permute-done | bytes 6176 | tf_op jit(solution)/shard_map/ppermute | solution.py:22
  25.4 2.4 %collective-permute-done.3 = f32[2,1,768]{2,1,0:T(1,128)S(1)} collective-permute-done((f32[2,1,768]{2,1,0:T(1,128)S(1)}, f32[2,1,768]{2,1,0:T(1,128)S(1)}, u32[]{:S(2)}, u32[]{:S(2)}) %collective-permute-start.3) | collective-permute-done | bytes 6176 | tf_op jit(solution)/shard_map/ppermute | solution.py:22
  31.1 2.6 %collective-permute-start.5 = (f32[4,1,2048]{2,1,0:T(1,128)S(1)}, f32[4,1,2048]{2,1,0:T(1,128)S(1)}, u32[]{:S(2)}, u32[]{:S(2)}) collective-permute-start(f32[4,1,2048]{2,1,0:T(1,128)S(1)} %pad_maximum_fusion), channel_id=1, source_target_pairs={{0,2},{1,3},{2,0},{3,1},{4,6},{5,7},{6,4},{7,5},{8,10},{9,11},{10,... | collective-permute-start | bytes 98312 | tf_op jit(solution)/shard_map/ppermute | solution.py:22
  34.0 2.6 %collective-permute-done.5 = f32[4,1,2048]{2,1,0:T(1,128)S(1)} collective-permute-done((f32[4,1,2048]{2,1,0:T(1,128)S(1)}, f32[4,1,2048]{2,1,0:T(1,128)S(1)}, u32[]{:S(2)}, u32[]{:S(2)}) %collective-permute-start.5) | collective-permute-done | bytes 32800 | tf_op jit(solution)/shard_map/ppermute | solution.py:22
  36.6 2.9 %collective-permute-done.6 = f32[4,1,2048]{2,1,0:T(1,128)S(1)} collective-permute-done((f32[4,1,2048]{2,1,0:T(1,128)S(1)}, f32[4,1,2048]{2,1,0:T(1,128)S(1)}, u32[]{:S(2)}, u32[]{:S(2)}) %collective-permute-start.6) | collective-permute-done | bytes 32800 | tf_op jit(solution)/shard_map/ppermute | solution.py:22
  39.5 1.7 %column_totals.2 = f32[2,1,768]{2,1,0:T(1,128)S(1)} custom-call(f32[2,768,2048]{2,1,0:T(8,128)S(1)} %get-tuple-element.11.soft_ref, f32[2,1,2048]{2,1,0:T(1,128)S(1)} %get-tuple-element.33.sums_ref), custom_call_target="tpu_custom_call" | custom-call | flops 1610612736 | bytes 1048576 | tf_op jit(solution)/shard_map/column_totals/pallas_call | solution.py:228
  50.8 3.5 %collective-permute-start.13 = (f32[2,1,2048]{2,1,0:T(1,128)S(1)}, f32[2,1,2048]{2,1,0:T(1,128)S(1)}, u32[]{:S(2)}, u32[]{:S(2)}) collective-permute-start(f32[2,1,2048]{2,1,0:T(1,128)S(1)} %row_totals.4), channel_id=1, source_target_pairs={{0,3},{1,2},{2,1},{3,0},{4,7},{5,6},{6,5},{7,4},{8,11},{9,10},{10,... | collective-permute-start | bytes 49160 | tf_op jit(solution)/shard_map/ppermute | solution.py:22
  54.6 1.7 %collective-permute-done.13 = f32[2,1,2048]{2,1,0:T(1,128)S(1)} collective-permute-done((f32[2,1,2048]{2,1,0:T(1,128)S(1)}, f32[2,1,2048]{2,1,0:T(1,128)S(1)}, u32[]{:S(2)}, u32[]{:S(2)}) %collective-permute-start.13) | collective-permute-done | bytes 16416 | tf_op jit(solution)/shard_map/ppermute | solution.py:22
  63.5 2.4 %collective-permute-done.17 = f32[2,1,768]{2,1,0:T(1,128)S(1)} collective-permute-done((f32[2,1,768]{2,1,0:T(1,128)S(1)}, f32[2,1,768]{2,1,0:T(1,128)S(1)}, u32[]{:S(2)}, u32[]{:S(2)}) %collective-permute-start.17) | collective-permute-done | bytes 6176 | tf_op jit(solution)/shard_map/ppermute | solution.py:22
  65.9 1.8 %row_totals.5 = f32[2,1,2048]{2,1,0:T(1,128)S(1)} custom-call(f32[2,768,2048]{2,1,0:T(8,128)S(1)} %get-tuple-element.11.soft_ref, f32[2,1,768]{2,1,0:T(1,128)S(1)} %add_add_fusion.5.sums_ref.col_ref), custom_call_target="tpu_custom_call" | custom-call | flops 1610612736 | bytes 1048576 | tf_op jit(solution)/shard_map/row_totals/pallas_call | solution.py:228
  68.1 3.8 %collective-permute-start.19 = (f32[2,1,2048]{2,1,0:T(1,128)S(1)}, f32[2,1,2048]{2,1,0:T(1,128)S(1)}, u32[]{:S(2)}, u32[]{:S(2)}) collective-permute-start(f32[2,1,2048]{2,1,0:T(1,128)S(1)} %row_totals.5), channel_id=1, source_target_pairs={{0,2},{1,3},{2,0},{3,1},{4,6},{5,7},{6,4},{7,5},{8,10},{9,11},{10,... | collective-permute-start | bytes 49160 | tf_op jit(solution)/shard_map/ppermute | solution.py:22
  73.6 3.8 %collective-permute-done.20 = f32[2,1,2048]{2,1,0:T(1,128)S(1)} collective-permute-done((f32[2,1,2048]{2,1,0:T(1,128)S(1)}, f32[2,1,2048]{2,1,0:T(1,128)S(1)}, u32[]{:S(2)}, u32[]{:S(2)}) %collective-permute-start.20) | collective-permute-done | bytes 16416 | tf_op jit(solution)/shard_map/ppermute | solution.py:22
  77.5 4.6 %copy-done.1 = f32[2,768,2048]{2,1,0:T(8,128)S(1)} copy-done((f32[2,768,2048]{2,1,0:T(8,128)S(1)}, f32[2,768,2048]{2,1,0:T(8,128)}, u32[]{:S(2)}) %copy-start.1) | copy-done | bytes 12582936
  82.0 2.2 %copy-done.3 = bf16[2048,2,512]{2,0,1:T(8,128)(2,1)S(1)} copy-done((bf16[2048,2,512]{2,0,1:T(8,128)(2,1)S(1)}, bf16[2048,2,512]{2,0,1:T(8,128)(2,1)}, u32[]{:S(2)}) %copy-start.3) | copy-done | bytes 4194328
  84.2 2.2 %copy-done.5 = f32[2,256,2048]{2,1,0:T(8,128)S(1)} copy-done((f32[2,256,2048]{2,1,0:T(8,128)S(1)}, f32[2,256,2048]{2,1,0:T(8,128)}, u32[]{:S(2)}) %copy-start.5) | copy-done | bytes 4194328
  86.4 8.4 %gradients.1 = (f32[768,256]{1,0:T(8,128)S(1)}, f32[512,256]{1,0:T(8,128)S(1)}, f32[8,256]{1,0:T(8,128)S(1)}) custom-call(bf16[2,2048,512]{2,1,0:T(8,128)(2,1)S(1)} %bitcast.56, bf16[768,256]{1,0:T(8,128)(2,1)S(1)} %pad.4.clone.proto_ref, bf16[256,768]{1,0:T(8,128)(2,1)S(1)} %pad_bitcast_fusion.turned_ref, f32[2,768,2048]{2,1,0:T(8,128)S(1)} %copy-done.1, ...), custom_call_target="tpu_custom_call" | custom-call | flops 4831838208 | bytes 1048576 | tf_op jit(solution)/shard_map/gradients/pallas_call | solution.py:228
  101.9 3.1 %collective-permute-done.31 = f32[1,72,256]{2,1,0:T(8,128)S(1)} collective-permute-done((f32[1,72,256]{2,1,0:T(8,128)S(1)}, f32[1,72,256]{2,1,0:T(8,128)S(1)}, u32[]{:S(2)}, u32[]{:S(2)}) %collective-permute-start.31) | collective-permute-done | bytes 73760 | tf_op jit(solution)/shard_map/ppermute | solution.py:22
  106.0 3.5 %collective-permute-start.35 = (f32[72,256]{1,0:T(8,128)S(1)}, f32[72,256]{1,0:T(8,128)S(1)}, u32[]{:S(2)}, u32[]{:S(2)}) collective-permute-start(f32[72,256]{1,0:T(8,128)S(1)} %add_bitcast_fusion), channel_id=1, source_target_pairs={{0,3},{1,2},{2,1},{3,0},{4,7},{5,6},{6,5},{7,4},{8,11},{9,10},{10,... | collective-permute-start | bytes 221192 | tf_op jit(solution)/shard_map/ppermute | solution.py:22
  117.3 1.7 %collective-permute-start.38 = (f32[1,64,256]{2,1,0:T(8,128)S(1)}, f32[1,64,256]{2,1,0:T(8,128)S(1)}, u32[]{:S(2)}, u32[]{:S(2)}) collective-permute-start(f32[1,64,256]{2,1,0:T(8,128)S(1)} %slice_bitcast_fusion), channel_id=1, source_target_pairs={{0,24},{4,28},{8,16},{12,20},{16,8},{20,12},{24,0},{28,4},{1,25},{... | collective-permute-start | bytes 196616 | tf_op jit(solution)/shard_map/ppermute | solution.py:22
  (141 shorter events, 55.4 us)
Async XLA Ops:
  23.3 4.5 %collective-permute-start.3 = (f32[2,1,768]{2,1,0:T(1,128)S(1)}, f32[2,1,768]{2,1,0:T(1,128)S(1)}, u32[]{:S(2)}, u32[]{:S(2)}) collective-permute-start(f32[2,1,768]{2,1,0:T(1,128)S(1)} %add.151), channel_id=1, source_target_pairs={{0,24},{4,28},{8,16},{12,20},{16,8},{20,12},{24,0},{28,4},{1,25},{... | collective-permute-start | bytes 18440 | tf_op jit(solution)/shard_map/ppermute | solution.py:22
  31.1 5.4 %collective-permute-start.5 = (f32[4,1,2048]{2,1,0:T(1,128)S(1)}, f32[4,1,2048]{2,1,0:T(1,128)S(1)}, u32[]{:S(2)}, u32[]{:S(2)}) collective-permute-start(f32[4,1,2048]{2,1,0:T(1,128)S(1)} %pad_maximum_fusion), channel_id=1, source_target_pairs={{0,2},{1,3},{2,0},{3,1},{4,6},{5,7},{6,4},{7,5},{8,10},{9,11},{10,... | collective-permute-start | bytes 98312 | tf_op jit(solution)/shard_map/ppermute | solution.py:22
  33.7 5.7 %collective-permute-start.6 = (f32[4,1,2048]{2,1,0:T(1,128)S(1)}, f32[4,1,2048]{2,1,0:T(1,128)S(1)}, u32[]{:S(2)}, u32[]{:S(2)}) collective-permute-start(f32[4,1,2048]{2,1,0:T(1,128)S(1)} %pad_maximum_fusion), channel_id=1, source_target_pairs={{0,3},{1,2},{2,1},{3,0},{4,7},{5,6},{6,5},{7,4},{8,11},{9,10},{10,... | collective-permute-start | bytes 98312 | tf_op jit(solution)/shard_map/ppermute | solution.py:22
  42.4 4.6 %collective-permute-start.10 = (f32[2,1,768]{2,1,0:T(1,128)S(1)}, f32[2,1,768]{2,1,0:T(1,128)S(1)}, u32[]{:S(2)}, u32[]{:S(2)}) collective-permute-start(f32[2,1,768]{2,1,0:T(1,128)S(1)} %add.158), channel_id=1, source_target_pairs={{0,24},{4,28},{8,16},{12,20},{16,8},{20,12},{24,0},{28,4},{1,25},{... | collective-permute-start | bytes 18440 | tf_op jit(solution)/shard_map/ppermute | solution.py:22
  49.9 4.7 %collective-permute-start.12 = (f32[2,1,2048]{2,1,0:T(1,128)S(1)}, f32[2,1,2048]{2,1,0:T(1,128)S(1)}, u32[]{:S(2)}, u32[]{:S(2)}) collective-permute-start(f32[2,1,2048]{2,1,0:T(1,128)S(1)} %row_totals.4), channel_id=1, source_target_pairs={{0,2},{1,3},{2,0},{3,1},{4,6},{5,7},{6,4},{7,5},{8,10},{9,11},{10,... | collective-permute-start | bytes 49160 | tf_op jit(solution)/shard_map/ppermute | solution.py:22
  50.8 5.5 %collective-permute-start.13 = (f32[2,1,2048]{2,1,0:T(1,128)S(1)}, f32[2,1,2048]{2,1,0:T(1,128)S(1)}, u32[]{:S(2)}, u32[]{:S(2)}) collective-permute-start(f32[2,1,2048]{2,1,0:T(1,128)S(1)} %row_totals.4), channel_id=1, source_target_pairs={{0,3},{1,2},{2,1},{3,0},{4,7},{5,6},{6,5},{7,4},{8,11},{9,10},{10,... | collective-permute-start | bytes 49160 | tf_op jit(solution)/shard_map/ppermute | solution.py:22
  61.4 4.5 %collective-permute-start.17 = (f32[2,1,768]{2,1,0:T(1,128)S(1)}, f32[2,1,768]{2,1,0:T(1,128)S(1)}, u32[]{:S(2)}, u32[]{:S(2)}) collective-permute-start(f32[2,1,768]{2,1,0:T(1,128)S(1)} %add.165), channel_id=1, source_target_pairs={{0,24},{4,28},{8,16},{12,20},{16,8},{20,12},{24,0},{28,4},{1,25},{... | collective-permute-start | bytes 18440 | tf_op jit(solution)/shard_map/ppermute | solution.py:22
  68.1 5.5 %collective-permute-start.19 = (f32[2,1,2048]{2,1,0:T(1,128)S(1)}, f32[2,1,2048]{2,1,0:T(1,128)S(1)}, u32[]{:S(2)}, u32[]{:S(2)}) collective-permute-start(f32[2,1,2048]{2,1,0:T(1,128)S(1)} %row_totals.5), channel_id=1, source_target_pairs={{0,2},{1,3},{2,0},{3,1},{4,6},{5,7},{6,4},{7,5},{8,10},{9,11},{10,... | collective-permute-start | bytes 49160 | tf_op jit(solution)/shard_map/ppermute | solution.py:22
  71.9 5.5 %collective-permute-start.20 = (f32[2,1,2048]{2,1,0:T(1,128)S(1)}, f32[2,1,2048]{2,1,0:T(1,128)S(1)}, u32[]{:S(2)}, u32[]{:S(2)}) collective-permute-start(f32[2,1,2048]{2,1,0:T(1,128)S(1)} %row_totals.5), channel_id=1, source_target_pairs={{0,3},{1,2},{2,1},{3,0},{4,7},{5,6},{6,5},{7,4},{8,11},{9,10},{10,... | collective-permute-start | bytes 49160 | tf_op jit(solution)/shard_map/ppermute | solution.py:22
  96.9 12.6 %collective-permute-start.21 = (f32[4,96,256]{2,1,0:T(8,128)S(1)}, f32[4,96,256]{2,1,0:T(8,128)S(1)}, u32[]{:S(2)}, u32[]{:S(2)}) collective-permute-start(f32[4,96,256]{2,1,0:T(8,128)S(1)} %dynamic-slice_bitcast_fusion), channel_id=1, source_target_pairs={{0,4},{4,0},{8,12},{12,8},{16,20},{20,16},{24,28},{28,24},{1,5},{5... | collective-permute-start | bytes 1179656 | tf_op jit(solution)/shard_map/ppermute | solution.py:22
  99.0 5.9 %collective-permute-start.31 = (f32[1,72,256]{2,1,0:T(8,128)S(1)}, f32[1,72,256]{2,1,0:T(8,128)S(1)}, u32[]{:S(2)}, u32[]{:S(2)}) collective-permute-start(f32[1,72,256]{2,1,0:T(8,128)S(1)} %get-tuple-element.32), channel_id=1, source_target_pairs={{0,16},{4,20},{8,24},{12,28},{16,0},{20,4},{24,8},{28,12},{1,17},{... | collective-permute-start | bytes 221192 | tf_op jit(solution)/shard_map/ppermute | solution.py:22
  99.5 5.4 %collective-permute-start.32 = (f32[1,72,256]{2,1,0:T(8,128)S(1)}, f32[1,72,256]{2,1,0:T(8,128)S(1)}, u32[]{:S(2)}, u32[]{:S(2)}) collective-permute-start(f32[1,72,256]{2,1,0:T(8,128)S(1)} %get-tuple-element.31), channel_id=1, source_target_pairs={{0,24},{4,28},{8,16},{12,20},{16,8},{20,12},{24,0},{28,4},{1,25},{... | collective-permute-start | bytes 221192 | tf_op jit(solution)/shard_map/ppermute | solution.py:22
  105.0 7.5 %collective-permute-start.33 = (f32[72,256]{1,0:T(8,128)S(1)}, f32[72,256]{1,0:T(8,128)S(1)}, u32[]{:S(2)}, u32[]{:S(2)}) collective-permute-start(f32[72,256]{1,0:T(8,128)S(1)} %add_bitcast_fusion), channel_id=1, source_target_pairs={{0,1},{1,0},{2,3},{3,2},{4,5},{5,4},{6,7},{7,6},{8,9},{9,8},{10,11... | collective-permute-start | bytes 221192 | tf_op jit(solution)/shard_map/ppermute | solution.py:22
  105.1 9.0 %collective-permute-start.34 = (f32[72,256]{1,0:T(8,128)S(1)}, f32[72,256]{1,0:T(8,128)S(1)}, u32[]{:S(2)}, u32[]{:S(2)}) collective-permute-start(f32[72,256]{1,0:T(8,128)S(1)} %add_bitcast_fusion), channel_id=1, source_target_pairs={{0,2},{1,3},{2,0},{3,1},{4,6},{5,7},{6,4},{7,5},{8,10},{9,11},{10,... | collective-permute-start | bytes 221192 | tf_op jit(solution)/shard_map/ppermute | solution.py:22
  106.0 8.1 %collective-permute-start.35 = (f32[72,256]{1,0:T(8,128)S(1)}, f32[72,256]{1,0:T(8,128)S(1)}, u32[]{:S(2)}, u32[]{:S(2)}) collective-permute-start(f32[72,256]{1,0:T(8,128)S(1)} %add_bitcast_fusion), channel_id=1, source_target_pairs={{0,3},{1,2},{2,1},{3,0},{4,7},{5,6},{6,5},{7,4},{8,11},{9,10},{10,... | collective-permute-start | bytes 221192 | tf_op jit(solution)/shard_map/ppermute | solution.py:22
  110.5 6.8 %collective-permute-start.22 = (f32[1,96,256]{2,1,0:T(8,128)S(1)}, f32[1,96,256]{2,1,0:T(8,128)S(1)}, u32[]{:S(2)}, u32[]{:S(2)}) collective-permute-start(f32[1,96,256]{2,1,0:T(8,128)S(1)} %get-tuple-element.27), channel_id=1, source_target_pairs={{0,8},{4,12},{8,0},{12,4},{16,24},{20,28},{24,16},{28,20},{1,9},{5... | collective-permute-start | bytes 294920 | tf_op jit(solution)/shard_map/ppermute | solution.py:22
  111.1 7.9 %collective-permute-start.23 = (f32[1,96,256]{2,1,0:T(8,128)S(1)}, f32[1,96,256]{2,1,0:T(8,128)S(1)}, u32[]{:S(2)}, u32[]{:S(2)}) collective-permute-start(f32[1,96,256]{2,1,0:T(8,128)S(1)} %get-tuple-element.29), channel_id=1, source_target_pairs={{0,16},{4,20},{8,24},{12,28},{16,0},{20,4},{24,8},{28,12},{1,17},{... | collective-permute-start | bytes 294920 | tf_op jit(solution)/shard_map/ppermute | solution.py:22
  112.5 6.5 %collective-permute-start.24 = (f32[1,96,256]{2,1,0:T(8,128)S(1)}, f32[1,96,256]{2,1,0:T(8,128)S(1)}, u32[]{:S(2)}, u32[]{:S(2)}) collective-permute-start(f32[1,96,256]{2,1,0:T(8,128)S(1)} %get-tuple-element.28), channel_id=1, source_target_pairs={{0,24},{4,28},{8,16},{12,20},{16,8},{20,12},{24,0},{28,4},{1,25},{... | collective-permute-start | bytes 294920 | tf_op jit(solution)/shard_map/ppermute | solution.py:22
  114.1 7.2 %collective-permute-start.36 = (f32[1,64,256]{2,1,0:T(8,128)S(1)}, f32[1,64,256]{2,1,0:T(8,128)S(1)}, u32[]{:S(2)}, u32[]{:S(2)}) collective-permute-start(f32[1,64,256]{2,1,0:T(8,128)S(1)} %slice_bitcast_fusion), channel_id=1, source_target_pairs={{0,8},{4,12},{8,0},{12,4},{16,24},{20,28},{24,16},{28,20},{1,9},{5... | collective-permute-start | bytes 196616 | tf_op jit(solution)/shard_map/ppermute | solution.py:22
  114.7 7.9 %collective-permute-start.37 = (f32[1,64,256]{2,1,0:T(8,128)S(1)}, f32[1,64,256]{2,1,0:T(8,128)S(1)}, u32[]{:S(2)}, u32[]{:S(2)}) collective-permute-start(f32[1,64,256]{2,1,0:T(8,128)S(1)} %slice_bitcast_fusion), channel_id=1, source_target_pairs={{0,16},{4,20},{8,24},{12,28},{16,0},{20,4},{24,8},{28,12},{1,17},{... | collective-permute-start | bytes 196616 | tf_op jit(solution)/shard_map/ppermute | solution.py:22
  117.3 5.4 %collective-permute-start.38 = (f32[1,64,256]{2,1,0:T(8,128)S(1)}, f32[1,64,256]{2,1,0:T(8,128)S(1)}, u32[]{:S(2)}, u32[]{:S(2)}) collective-permute-start(f32[1,64,256]{2,1,0:T(8,128)S(1)} %slice_bitcast_fusion), channel_id=1, source_target_pairs={{0,24},{4,28},{8,16},{12,20},{16,8},{20,12},{24,0},{28,4},{1,25},{... | collective-permute-start | bytes 196616 | tf_op jit(solution)/shard_map/ppermute | solution.py:22
  119.1 4.7 %collective-permute-start.25 = (f32[1,96,256]{2,1,0:T(8,128)S(1)}, f32[1,96,256]{2,1,0:T(8,128)S(1)}, u32[]{:S(2)}, u32[]{:S(2)}) collective-permute-start(f32[1,96,256]{2,1,0:T(8,128)S(1)} %get-tuple-element.26), channel_id=1, source_target_pairs={{0,8},{4,12},{8,0},{12,4},{16,24},{20,28},{24,16},{28,20},{1,9},{5... | collective-permute-start | bytes 294920 | tf_op jit(solution)/shard_map/ppermute | solution.py:22
  120.6 4.6 %collective-permute-start.26 = (f32[1,96,256]{2,1,0:T(8,128)S(1)}, f32[1,96,256]{2,1,0:T(8,128)S(1)}, u32[]{:S(2)}, u32[]{:S(2)}) collective-permute-start(f32[1,96,256]{2,1,0:T(8,128)S(1)} %get-tuple-element.26), channel_id=1, source_target_pairs={{0,16},{4,20},{8,24},{12,28},{16,0},{20,4},{24,8},{28,12},{1,17},{... | collective-permute-start | bytes 294920 | tf_op jit(solution)/shard_map/ppermute | solution.py:22
  121.4 5.5 %collective-permute-start.27 = (f32[1,96,256]{2,1,0:T(8,128)S(1)}, f32[1,96,256]{2,1,0:T(8,128)S(1)}, u32[]{:S(2)}, u32[]{:S(2)}) collective-permute-start(f32[1,96,256]{2,1,0:T(8,128)S(1)} %get-tuple-element.26), channel_id=1, source_target_pairs={{0,24},{4,28},{8,16},{12,20},{16,8},{20,12},{24,0},{28,4},{1,25},{... | collective-permute-start | bytes 294920 | tf_op jit(solution)/shard_map/ppermute | solution.py:22
  (29 other events, 151.1 us)

commit v3 on v2

--- a/solution.py
+++ b/solution.py
@@ -82,6 +82,16 @@
     return lax.dot_general(left, right, dims, preferred_element_type=jnp.float32)
 
 
+def unit_rows(values):
+    inverse = lax.rsqrt(jnp.sum(values * values, axis=-1, keepdims=True) + TINY)
+    return (values * inverse, inverse)
+
+
+def unit_columns(values):
+    inverse = lax.rsqrt(jnp.sum(values * values, axis=0, keepdims=True) + TINY)
+    return (values * inverse, inverse)
+
+
 def lane_sums(values):
     total = values[:, :LANES]
     for start in range(LANES, values.shape[1], LANES):
@@ -116,33 +126,60 @@
     lax.fori_loop(0, 2 * count, one, 0)
 
 
+def copies(source_of, target_of, sems, count):
+    return [pltpu.make_async_copy(source_of(at), target_of(at), sems.at[at]) for at in range(count)]
+
+
 def first_kernel(
-    valid, width, feats_ref, proj_ref, proto_ref, soft_ref, raw_ref, half_ref, col_ref, denom_ref, acc_ref
+    valid, width, feats_ref, proj_ref, proto_ref, soft_ref, half_ref, col_ref, denom_ref, proto_half_ref,
+    turned_ref, split_ref, raw_ref, acc_ref, unit_ref, in_ref, out_ref, raw_out_ref, in_sems, out_sems, raw_sems,
 ):
+    count = half_ref.shape[-1] // width
+    spans = [pl.ds(at * width, width) for at in range(count)]
+    loads = copies(lambda at: feats_ref.at[spans[at]], lambda at: in_ref.at[spans[at]], in_sems, count)
+    stores = copies(lambda at: out_ref.at[:, spans[at]], lambda at: split_ref.at[:, spans[at]], out_sems, count)
+    raw_stores = copies(
+        lambda at: raw_out_ref.at[:, :, spans[at]], lambda at: raw_ref.at[:, :, spans[at]], raw_sems, count
+    )
+    for load in loads:
+        load.start()
+
+    edge = valid // 8 * 8
+    unit_ref[edge:] = jnp.zeros_like(unit_ref[edge:])
+    unit_ref[:valid] = proto_ref[...]
+    unit, _ = unit_rows(unit_ref[...])
+    proto_half_ref[...] = unit.astype(jnp.bfloat16)
+    turned_ref[...] = jnp.transpose(unit).astype(jnp.bfloat16)
     acc_ref[...] = jnp.zeros_like(acc_ref)
-    edge = valid // 8 * 8
-
-    def step(view, lanes):
-        raw = product(proj_ref[...], feats_ref[view, lanes, :], NT)
-        raw_ref[view, :, lanes] = raw
-        inverse = lax.rsqrt(jnp.sum(raw * raw, axis=0, keepdims=True) + TINY)
-        half = (raw * inverse).astype(jnp.bfloat16)
-        half_ref[view, :, lanes] = half
-        denom = jnp.zeros((8, width), jnp.float32)
-        for start in range(0, proto_ref.shape[0], CHUNK):
-            logits = product(proto_ref[start : start + CHUNK], half, NN)
-            soft = jnp.exp2(logits * (LOG2_E / SOFTMAX_TEMPER))
-            if start + CHUNK > edge:
-                place = lax.broadcasted_iota(jnp.int32, soft.shape, 0) + start
-                soft = jnp.where(place < valid, soft, 0.0)
-            soft_ref[view, start : start + CHUNK, lanes] = soft
-            denom = denom + jnp.sum(soft.reshape(-1, 8, width), axis=0)
-            acc_ref[view, start : start + CHUNK] += lane_sums(soft * soft)
-        denom_ref[view, :, lanes] = jnp.sum(denom, axis=0, keepdims=True)
-
-    tiles(denom_ref, width, step)
+
+    for at in range(count):
+        lanes = spans[at]
+        loads[at].wait()
+        out_ref[:, lanes] = jnp.transpose(in_ref[lanes], (1, 0, 2))
+        stores[at].start()
+        for view in range(2):
+            raw = product(proj_ref[...], out_ref[view, lanes], NT)
+            raw_out_ref[view, :, lanes] = raw
+            unit, _ = unit_columns(raw)
+            half = unit.astype(jnp.bfloat16)
+            half_ref[view, :, lanes] = half
+            denom = jnp.zeros((8, width), jnp.float32)
+            for start in range(0, proto_half_ref.shape[0], CHUNK):
+                logits = product(proto_half_ref[start : start + CHUNK], half, NN)
+                soft = jnp.exp2(logits * (LOG2_E / SOFTMAX_TEMPER))
+                if start + CHUNK > edge:
+                    place = lax.broadcasted_iota(jnp.int32, soft.shape, 0) + start
+                    soft = jnp.where(place < valid, soft, 0.0)
+                soft_ref[view, start : start + CHUNK, lanes] = soft
+                denom = denom + jnp.sum(soft.reshape(-1, 8, width), axis=0)
+                acc_ref[view, start : start + CHUNK] += lane_sums(soft * soft)
+            denom_ref[view, :, lanes] = jnp.sum(denom, axis=0, keepdims=True)
+        raw_stores[at].start()
+
     for view in range(2):
         col_ref[view] = as_row(acc_ref[view])
+    for store in stores + raw_stores:
+        store.wait()
 
 
 def row_kernel(valid, width, soft_ref, sums_ref, row_ref, scale_ref):
@@ -174,43 +211,52 @@
 
 
 def grad_kernel(
-    valid, width, factor, feats_ref, proto_ref, turned_ref, soft_ref, raw_ref, half_ref, denom_ref, row_ref,
-    col_ref, proto_out, proj_out, loss_ref, scale_ref, grad_ref, turn_ref,
+    valid, width, factor, feats_ref, raw_ref, proto_ref, turned_ref, half_ref, denom_ref, row_ref, col_ref,
+    proto_out, proj_out, loss_ref, scale_ref, grad_ref, turn_ref, in_ref, raw_in_ref, in_sems, raw_sems,
 ):
+    count = half_ref.shape[-1] // width
+    spans = [pl.ds(at * width, width) for at in range(count)]
+    loads = copies(lambda at: feats_ref.at[:, spans[at]], lambda at: in_ref.at[:, spans[at]], in_sems, count)
+    raw_loads = copies(
+        lambda at: raw_ref.at[:, :, spans[at]], lambda at: raw_in_ref.at[:, :, spans[at]], raw_sems, count
+    )
+    for at in range(count):
+        raw_loads[at].start()
+        loads[at].start()
     for view in range(2):
         scale_ref[view] = column_scale(valid, col_ref[view])
-    proto_out[...] = jnp.zeros_like(proto_out)
-    turn_ref[...] = jnp.zeros_like(turn_ref)
-
-    def step(index, loss):
-        lanes = pl.ds(index * width, width)
+    loss = jnp.zeros((8, width), jnp.float32)
+    for at in range(count):
+        lanes = spans[at]
         both = lambda ref: jnp.concatenate([ref[view, :, lanes] for view in range(2)], axis=1)
-        rows, denoms = factor / both(row_ref), factor / both(denom_ref)
-        halves = both(half_ref)
+        halves = [half_ref[view, :, lanes] for view in range(2)]
         for start in range(0, proto_ref.shape[0], CHUNK):
             part = slice(start, start + CHUNK)
-            logits = product(proto_ref[part], halves, NN)
-            softs = [soft_ref[view, part, lanes] for view in range(2)]
+            logits = [product(proto_ref[part], halves[view], NN) for view in range(2)]
+            softs = [jnp.exp2(logits[view] * (LOG2_E / SOFTMAX_TEMPER)) for view in range(2)]
             for view in range(2):
-                here, there = (slice(at * width, (at + 1) * width) for at in (view, 1 - view))
-                target = softs[1 - view] * softs[1 - view] * widen(scale_ref[1 - view, part], width)
-                target = target * rows[:, there]
-                loss = loss + jnp.sum((logits[:, here] * target).reshape(-1, 8, width), axis=0)
-                grad_ref[part, here] = (softs[view] * denoms[:, here] - target).astype(jnp.bfloat16)
-        proto_out[...] += product(grad_ref[...], halves, NT)
-        raw = both(raw_ref)
-        inverse = lax.rsqrt(jnp.sum(raw * raw, axis=0, keepdims=True) + TINY)
-        unit = raw * inverse
+                other = 1 - view
+                target = softs[other] * softs[other] * widen(scale_ref[other, part], width)
+                target = target * (factor / row_ref[other, :, lanes])
+                loss = loss + jnp.sum((logits[view] * target).reshape(-1, 8, width), axis=0)
+                grad = softs[view] * (factor / denom_ref[view, :, lanes]) - target
+                grad_ref[part, view * width : (view + 1) * width] = grad.astype(jnp.bfloat16)
+        proto_part = product(grad_ref[...], jnp.concatenate(halves, axis=1), NT)
         grad_unit = product(turned_ref[...], grad_ref[...], NN)
+        raw_loads[at].wait()
+        unit, inverse = unit_columns(both(raw_in_ref))
         along = jnp.sum(unit * grad_unit, axis=0, keepdims=True)
         grad_raw = ((grad_unit - unit * along) * inverse).astype(jnp.bfloat16)
-        feats = jnp.concatenate([feats_ref[view, lanes, :] for view in range(2)], axis=0)
-        turn_ref[...] += product(grad_raw, feats, NN)
-        return loss
-
-    loss = jnp.zeros((8, width), jnp.float32)
-    for index in range(row_ref.shape[-1] // width):
-        loss = step(index, loss)
+        loads[at].wait()
+        feats = jnp.concatenate([in_ref[view, lanes] for view in range(2)], axis=0)
+        proj_part = product(grad_raw, feats, NN)
+        if at == 0:
+            proto_out[...] = proto_part
+            turn_ref[...] = proj_part
+        else:
+            proto_out[...] += proto_part
+            turn_ref[...] += proj_part
+
     proj_out[...] = jnp.transpose(turn_ref[...])
     logs = jnp.log(denom_ref[0]) + jnp.log(denom_ref[1])
     loss = jnp.sum(loss, axis=0, keepdims=True) * (1.0 / (SOFTMAX_TEMPER * factor))
@@ -221,21 +267,23 @@
 
 
 IN_VMEM = pl.BlockSpec(memory_space=pltpu.VMEM)
-
-
-def call(kernel, name, out_shapes, scratch, work, *args):
-    outs = [jax.ShapeDtypeStruct(shape, dtype) for shape, dtype in out_shapes]
+IN_HBM = pl.BlockSpec(memory_space=pltpu.HBM)
+
+
+def call(kernel, name, out_shapes, scratch, work, *args, far_in=(), far_out=()):
+    outs = [
+        pltpu.HBM(shape, dtype) if at in far_out else jax.ShapeDtypeStruct(shape, dtype)
+        for at, (shape, dtype) in enumerate(out_shapes)
+    ]
     return pl.pallas_call(
-        kernel, in_specs=[IN_VMEM] * len(args), out_specs=[IN_VMEM] * len(outs), out_shape=outs,
-        scratch_shapes=[pltpu.VMEM(shape, dtype) for shape, dtype in scratch],
+        kernel,
+        in_specs=[IN_HBM if at in far_in else IN_VMEM for at in range(len(args))],
+        out_specs=[IN_HBM if at in far_out else IN_VMEM for at in range(len(outs))],
+        out_shape=outs,
+        scratch_shapes=scratch,
         compiler_params=pltpu.CompilerParams(vmem_limit_bytes=VMEM_LIMIT),
         cost_estimate=pl.CostEstimate(flops=work, bytes_accessed=2**20, transcendentals=0), name=name,
     )(*args)
-
-
-def unit_rows(values):
-    inverse = lax.rsqrt(jnp.sum(values * values, axis=-1, keepdims=True) + TINY)
-    return (values * inverse, inverse)
 
 
 def body(features, projection, prototypes):
@@ -247,17 +295,26 @@
     block = -(-valid // LANES) * LANES
     single, half_type = jnp.float32, jnp.bfloat16
 
-    proto_unit, proto_inverse = unit_rows(prototypes)
-    proto_half = jnp.pad(proto_unit.astype(half_type), ((0, block - valid), (0, 0)))
-    feats = jnp.transpose(features, (1, 0, 2))
-
+    tile = min(512, rows)
+    count = rows // tile
     row_shape, col_shape = ((2, 1, rows), single), ((2, 1, block), single)
-    column = ((2, block, LANES), single)
+    column = pltpu.VMEM((2, block, LANES), single)
+    split = (2, rows, features.shape[-1])
     work = 4 * rows * block * width
-    soft, raw, half, col_part, soft_part = call(
-        functools.partial(first_kernel, valid, min(2048, rows)), "first_totals",
-        [((2, block, rows), single), ((2, width, rows), single), ((2, width, rows), half_type), col_shape, row_shape],
-        [column], work, feats, projection.T, proto_half,
+    turned_proj = projection.T
+    sems = pltpu.SemaphoreType.DMA((count,))
+    far = lambda array: pltpu.with_memory_space_constraint(array, pltpu.HBM)
+    soft, half, col_part, soft_part, proto_half, turned, feats, raw = call(
+        functools.partial(first_kernel, valid, tile), "first_totals",
+        [
+            ((2, block, rows), single), ((2, width, rows), half_type), col_shape, row_shape,
+            ((block, width), half_type), ((width, block), half_type), (split, half_type), ((2, width, rows), single),
+        ],
+        [
+            column, pltpu.VMEM((block, width), single), pltpu.VMEM(features.shape, half_type),
+            pltpu.VMEM(split, half_type), pltpu.VMEM((2, width, rows), single), sems, sems, sems,
+        ],
+        work, far(features), turned_proj, prototypes, far_in=(0,), far_out=(6, 7),
     )
     row_call = functools.partial(
         call, functools.partial(row_kernel, valid, min(512, rows)), "row_totals", [row_shape], [column], work, soft
@@ -273,12 +330,14 @@
         col_sums = sum_over(col_call(row_sums)[0], "dp", 1)
         row_sums = sum_over(row_call(col_sums)[0], "mp", 2)
 
-    grad_tile = min(512, rows)
     proto_part, proj_part, loss = call(
-        functools.partial(grad_kernel, valid, grad_tile, factor), "gradients",
+        functools.partial(grad_kernel, valid, tile, factor), "gradients",
         [((block, width), single), (projection.shape, single), ((8, width), single)],
-        [column, ((block, 2 * grad_tile), half_type), (projection.shape[::-1], single)],
-        3 * work, feats, proto_half, proto_half.T, soft, raw, half, denoms, row_sums, col_sums,
+        [
+            column, pltpu.VMEM((block, 2 * tile), half_type), pltpu.VMEM(projection.shape[::-1], single),
+            pltpu.VMEM(split, half_type), pltpu.VMEM((2, width, rows), single), sems, sems,
+        ],
+        3 * work, far(feats), far(raw), proto_half, turned, half, denoms, row_sums, col_sums, far_in=(0, 1),
     )
     loss_rows = jnp.broadcast_to(loss[None], (shards,) + loss.shape)
     proj_part = jnp.concatenate([proj_part.reshape(shards, -1, width), loss_rows], axis=1)
@@ -288,6 +347,7 @@
 
     proto_sum = scatter_sum(proto_part.reshape(shards, -1, width), "dp", 1)
     proto_grad = gather_blocks(proto_sum, "dp", 1).reshape(block, width)[:valid]
+    proto_unit, proto_inverse = unit_rows(prototypes)
     along_proto = jnp.sum(proto_unit * proto_grad, axis=-1, keepdims=True)
     grad_protos = (proto_grad - proto_unit * along_proto) * proto_inverse
     return (grad_protos, proj_grad, loss_value)

time: 132 us -> 120 us (0.909)
  local copies, waits for them, and re-layouts: 24 us -> 4.77 us
  Pallas kernels: 21.3 us -> 29.7 us
    unnamed x32 -> x11, local copies, waits for them, and re-layouts: 22 us -> 3.81 us
    pallas_call x7, Pallas kernels: 21.3 us -> 29.7 us  [call(): pl.pallas_call(kernel, in_specs=[IN_HBM if at in far_in else IN_VMEM for...]
    reduce_sum x1, other arithmetic: 1.59 us -> 0.18 us  [unit_rows(): inverse = lax.rsqrt(jnp.sum(values * values, axis=-1, keepdims=True) + TINY)]
  transfers between devices with their start and end apart: 40 -> 40, of which waited for: 23 -> 24; matrix products, arithmetic and copies ran while one was open for 2% -> 1% of each run, Pallas kernels for 0% -> 0%
where the time goes in v3:
time: 120 us
  starting transfers between devices  45 us (38%)
  waiting for transfers between devices  35.8 us (30%)
  Pallas kernels  29.7 us (25%)
  local copies, waits for them, and re-layouts  4.77 us (4%)
  between operations  2.86 us (2%)
  other arithmetic  2.04 us (2%)
    ppermute x40, starting transfers between devices, swap(): return lax.ppermute(values, axis, [(i, i ^ offset) for i in range(size)])  45 us
    ppermute x40, waiting for transfers between devices, swap(): return lax.ppermute(values, axis, [(i, i ^ offset) for i in range(size)])  35.8 us
    pallas_call x7, Pallas kernels, call(): pl.pallas_call(kernel, in_specs=[IN_HBM if at in far_in else IN_VMEM for...  29.7 us
    unnamed x11, local copies, waits for them, and re-layouts  3.81 us
  transfers between devices with their start and end apart: 40, of which 24 were waited for; matrix products, arithmetic and copies ran while one was open for 1% of the time, Pallas kernels for 0%

profile of v3, /device:TPU:0, one launch (start us, length us, event | category | flops | bytes accessed | tf_op | source)
XLA Modules:
  0.0 120.2 jit_solution(5621216941463353518)
XLA Ops:
  2.9 9.3 %first_totals.1 = (f32[2,768,2048]{2,1,0:T(8,128)S(1)}, bf16[2,256,2048]{2,1,0:T(8,128)(2,1)S(1)}, f32[2,1,768]{2,1,0:T(1,128)S(1)}, f32[2,1,2048]{2,1,0:T(1,128...) custom-call(bf16[2048,2,512]{2,1,0:T(2,128)(2,1)} %feats_ref.1, ...), custom_call_target="tpu_custom_call" | custom-call | flops 1610612736 | bytes 1048576 | tf_op jit(solution)/shard_map/first_totals/pallas_call | solution.py:278
  13.5 2.9 %collective-permute-start.1 = (f32[2,1,768]{2,1,0:T(1,128)S(1)}, f32[2,1,768]{2,1,0:T(1,128)S(1)}, u32[]{:S(2)}, u32[]{:S(2)}) collective-permute-start(f32[2,1,768]{2,1,0:T(1,128)S(1)} %add.147), channel_id=1, source_target_pairs={{0,8},{4,12},{8,0},{12,4},{16,24},{20,28},{24,16},{28,20},{1,9},{5... | collective-permute-start | bytes 18440 | tf_op jit(solution)/shard_map/ppermute | solution.py:22
  18.0 2.0 %collective-permute-done.2 = f32[2,1,768]{2,1,0:T(1,128)S(1)} collective-permute-done((f32[2,1,768]{2,1,0:T(1,128)S(1)}, f32[2,1,768]{2,1,0:T(1,128)S(1)}, u32[]{:S(2)}, u32[]{:S(2)}) %collective-permute-start.2) | collective-permute-done | bytes 6176 | tf_op jit(solution)/shard_map/ppermute | solution.py:22
  20.0 2.4 %collective-permute-done.3 = f32[2,1,768]{2,1,0:T(1,128)S(1)} collective-permute-done((f32[2,1,768]{2,1,0:T(1,128)S(1)}, f32[2,1,768]{2,1,0:T(1,128)S(1)}, u32[]{:S(2)}, u32[]{:S(2)}) %collective-permute-start.3) | collective-permute-done | bytes 6176 | tf_op jit(solution)/shard_map/ppermute | solution.py:22
  22.4 1.8 %row_totals.3 = f32[2,1,2048]{2,1,0:T(1,128)S(1)} custom-call(f32[2,768,2048]{2,1,0:T(8,128)S(1)} %get-tuple-element.19.soft_ref, f32[2,1,768]{2,1,0:T(1,128)S(1)} %add_add_fusion.7.sums_ref), custom_call_target="tpu_custom_call" | custom-call | flops 1610612736 | bytes 1048576 | tf_op jit(solution)/shard_map/row_totals/pallas_call | solution.py:278
  24.3 1.6 %collective-permute-start.4 = (f32[4,1,2048]{2,1,0:T(1,128)S(1)}, f32[4,1,2048]{2,1,0:T(1,128)S(1)}, u32[]{:S(2)}, u32[]{:S(2)}) collective-permute-start(f32[4,1,2048]{2,1,0:T(1,128)S(1)} %pad_maximum_fusion), channel_id=1, source_target_pairs={{0,1},{1,0},{2,3},{3,2},{4,5},{5,4},{6,7},{7,6},{8,9},{9,8},{10,11... | collective-permute-start | bytes 98312 | tf_op jit(solution)/shard_map/ppermute | solution.py:22
  26.0 2.6 %collective-permute-start.5 = (f32[4,1,2048]{2,1,0:T(1,128)S(1)}, f32[4,1,2048]{2,1,0:T(1,128)S(1)}, u32[]{:S(2)}, u32[]{:S(2)}) collective-permute-start(f32[4,1,2048]{2,1,0:T(1,128)S(1)} %pad_maximum_fusion), channel_id=1, source_target_pairs={{0,2},{1,3},{2,0},{3,1},{4,6},{5,7},{6,4},{7,5},{8,10},{9,11},{10,... | collective-permute-start | bytes 98312 | tf_op jit(solution)/shard_map/ppermute | solution.py:22
  28.8 2.6 %collective-permute-done.5 = f32[4,1,2048]{2,1,0:T(1,128)S(1)} collective-permute-done((f32[4,1,2048]{2,1,0:T(1,128)S(1)}, f32[4,1,2048]{2,1,0:T(1,128)S(1)}, u32[]{:S(2)}, u32[]{:S(2)}) %collective-permute-start.5) | collective-permute-done | bytes 32800 | tf_op jit(solution)/shard_map/ppermute | solution.py:22
  31.4 2.9 %collective-permute-done.6 = f32[4,1,2048]{2,1,0:T(1,128)S(1)} collective-permute-done((f32[4,1,2048]{2,1,0:T(1,128)S(1)}, f32[4,1,2048]{2,1,0:T(1,128)S(1)}, u32[]{:S(2)}, u32[]{:S(2)}) %collective-permute-start.6) | collective-permute-done | bytes 32800 | tf_op jit(solution)/shard_map/ppermute | solution.py:22
  34.4 1.8 %column_totals.2 = f32[2,1,768]{2,1,0:T(1,128)S(1)} custom-call(f32[2,768,2048]{2,1,0:T(8,128)S(1)} %get-tuple-element.19.soft_ref, f32[2,1,2048]{2,1,0:T(1,128)S(1)} %get-tuple-element.33.sums_ref), custom_call_target="tpu_custom_call" | custom-call | flops 1610612736 | bytes 1048576 | tf_op jit(solution)/shard_map/column_totals/pallas_call | solution.py:278
  43.1 1.8 %row_totals.4 = f32[2,1,2048]{2,1,0:T(1,128)S(1)} custom-call(f32[2,768,2048]{2,1,0:T(8,128)S(1)} %get-tuple-element.19.soft_ref, f32[2,1,768]{2,1,0:T(1,128)S(1)} %add_add_fusion.6.sums_ref), custom_call_target="tpu_custom_call" | custom-call | flops 1610612736 | bytes 1048576 | tf_op jit(solution)/shard_map/row_totals/pallas_call | solution.py:278
  45.9 3.5 %collective-permute-start.13 = (f32[2,1,2048]{2,1,0:T(1,128)S(1)}, f32[2,1,2048]{2,1,0:T(1,128)S(1)}, u32[]{:S(2)}, u32[]{:S(2)}) collective-permute-start(f32[2,1,2048]{2,1,0:T(1,128)S(1)} %row_totals.4), channel_id=1, source_target_pairs={{0,3},{1,2},{2,1},{3,0},{4,7},{5,6},{6,5},{7,4},{8,11},{9,10},{10,... | collective-permute-start | bytes 49160 | tf_op jit(solution)/shard_map/ppermute | solution.py:22
  49.7 1.7 %collective-permute-done.13 = f32[2,1,2048]{2,1,0:T(1,128)S(1)} collective-permute-done((f32[2,1,2048]{2,1,0:T(1,128)S(1)}, f32[2,1,2048]{2,1,0:T(1,128)S(1)}, u32[]{:S(2)}, u32[]{:S(2)}) %collective-permute-start.13) | collective-permute-done | bytes 16416 | tf_op jit(solution)/shard_map/ppermute | solution.py:22
  51.5 1.8 %column_totals.3 = f32[2,1,768]{2,1,0:T(1,128)S(1)} custom-call(f32[2,768,2048]{2,1,0:T(8,128)S(1)} %get-tuple-element.19.soft_ref, f32[2,1,2048]{2,1,0:T(1,128)S(1)} %add_add_fusion.4.sums_ref), custom_call_target="tpu_custom_call" | custom-call | flops 1610612736 | bytes 1048576 | tf_op jit(solution)/shard_map/column_totals/pallas_call | solution.py:278
  58.8 2.4 %collective-permute-done.17 = f32[2,1,768]{2,1,0:T(1,128)S(1)} collective-permute-done((f32[2,1,768]{2,1,0:T(1,128)S(1)}, f32[2,1,768]{2,1,0:T(1,128)S(1)}, u32[]{:S(2)}, u32[]{:S(2)}) %collective-permute-start.17) | collective-permute-done | bytes 6176 | tf_op jit(solution)/shard_map/ppermute | solution.py:22
  61.2 2.0 %row_totals.5 = f32[2,1,2048]{2,1,0:T(1,128)S(1)} custom-call(f32[2,768,2048]{2,1,0:T(8,128)S(1)} %get-tuple-element.19.soft_ref, f32[2,1,768]{2,1,0:T(1,128)S(1)} %add_add_fusion.5.sums_ref.col_ref), custom_call_target="tpu_custom_call" | custom-call | flops 1610612736 | bytes 1048576 | tf_op jit(solution)/shard_map/row_totals/pallas_call | solution.py:278
  63.5 3.8 %collective-permute-start.19 = (f32[2,1,2048]{2,1,0:T(1,128)S(1)}, f32[2,1,2048]{2,1,0:T(1,128)S(1)}, u32[]{:S(2)}, u32[]{:S(2)}) collective-permute-start(f32[2,1,2048]{2,1,0:T(1,128)S(1)} %row_totals.5), channel_id=1, source_target_pairs={{0,2},{1,3},{2,0},{3,1},{4,6},{5,7},{6,4},{7,5},{8,10},{9,11},{10,... | collective-permute-start | bytes 49160 | tf_op jit(solution)/shard_map/ppermute | solution.py:22
  69.1 3.8 %collective-permute-done.20 = f32[2,1,2048]{2,1,0:T(1,128)S(1)} collective-permute-done((f32[2,1,2048]{2,1,0:T(1,128)S(1)}, f32[2,1,2048]{2,1,0:T(1,128)S(1)}, u32[]{:S(2)}, u32[]{:S(2)}) %collective-permute-start.20) | collective-permute-done | bytes 16416 | tf_op jit(solution)/shard_map/ppermute | solution.py:22
  74.5 11.1 %gradients.1 = (f32[768,256]{1,0:T(8,128)S(1)}, f32[512,256]{1,0:T(8,128)S(1)}, f32[8,256]{1,0:T(8,128)S(1)}) custom-call(bf16[2,2048,512]{2,1,0:T(8,128)(2,1)} %get-tuple-element.14.feats_ref, f32[2,256,2048]{2,1,0:T(8,128)} %get-tuple-element.15.raw_ref, bf16[768,256]{1,0:T(8,128)(2,1)S(1)} %get-tuple-element.16.proto_ref, ...), custom_call_target="tpu_custom_call" | custom-call | flops 4831838208 | bytes 1048576 | tf_op jit(solution)/shard_map/gradients/pallas_call | solution.py:278
  91.8 3.1 %collective-permute-done.31 = f32[1,72,256]{2,1,0:T(8,128)S(1)} collective-permute-done((f32[1,72,256]{2,1,0:T(8,128)S(1)}, f32[1,72,256]{2,1,0:T(8,128)S(1)}, u32[]{:S(2)}, u32[]{:S(2)}) %collective-permute-start.31) | collective-permute-done | bytes 73760 | tf_op jit(solution)/shard_map/ppermute | solution.py:22
  95.9 3.5 %collective-permute-start.35 = (f32[72,256]{1,0:T(8,128)S(1)}, f32[72,256]{1,0:T(8,128)S(1)}, u32[]{:S(2)}, u32[]{:S(2)}) collective-permute-start(f32[72,256]{1,0:T(8,128)S(1)} %add_bitcast_fusion), channel_id=1, source_target_pairs={{0,3},{1,2},{2,1},{3,0},{4,7},{5,6},{6,5},{7,4},{8,11},{9,10},{10,... | collective-permute-start | bytes 221192 | tf_op jit(solution)/shard_map/ppermute | solution.py:22
  101.4 1.6 %collective-permute-start.24 = (f32[1,96,256]{2,1,0:T(8,128)S(1)}, f32[1,96,256]{2,1,0:T(8,128)S(1)}, u32[]{:S(2)}, u32[]{:S(2)}) collective-permute-start(f32[1,96,256]{2,1,0:T(8,128)S(1)} %get-tuple-element.28), channel_id=1, source_target_pairs={{0,24},{4,28},{8,16},{12,20},{16,8},{20,12},{24,0},{28,4},{1,25},{... | collective-permute-start | bytes 294920 | tf_op jit(solution)/shard_map/ppermute | solution.py:22
  106.3 1.7 %collective-permute-start.38 = (f32[1,64,256]{2,1,0:T(8,128)S(1)}, f32[1,64,256]{2,1,0:T(8,128)S(1)}, u32[]{:S(2)}, u32[]{:S(2)}) collective-permute-start(f32[1,64,256]{2,1,0:T(8,128)S(1)} %slice_bitcast_fusion), channel_id=1, source_target_pairs={{0,24},{4,28},{8,16},{12,20},{16,8},{20,12},{24,0},{28,4},{1,25},{... | collective-permute-start | bytes 196616 | tf_op jit(solution)/shard_map/ppermute | solution.py:22
  114.2 1.6 %collective-permute-done.27 = f32[1,96,256]{2,1,0:T(8,128)S(1)} collective-permute-done((f32[1,96,256]{2,1,0:T(8,128)S(1)}, f32[1,96,256]{2,1,0:T(8,128)S(1)}, u32[]{:S(2)}, u32[]{:S(2)}) %collective-permute-start.27) | collective-permute-done | bytes 98336 | tf_op jit(solution)/shard_map/ppermute | solution.py:22
  (116 shorter events, 43.9 us)
Async XLA Ops:
  17.9 4.5 %collective-permute-start.3 = (f32[2,1,768]{2,1,0:T(1,128)S(1)}, f32[2,1,768]{2,1,0:T(1,128)S(1)}, u32[]{:S(2)}, u32[]{:S(2)}) collective-permute-start(f32[2,1,768]{2,1,0:T(1,128)S(1)} %add.147), channel_id=1, source_target_pairs={{0,24},{4,28},{8,16},{12,20},{16,8},{20,12},{24,0},{28,4},{1,25},{... | collective-permute-start | bytes 18440 | tf_op jit(solution)/shard_map/ppermute | solution.py:22
  26.0 5.4 %collective-permute-start.5 = (f32[4,1,2048]{2,1,0:T(1,128)S(1)}, f32[4,1,2048]{2,1,0:T(1,128)S(1)}, u32[]{:S(2)}, u32[]{:S(2)}) collective-permute-start(f32[4,1,2048]{2,1,0:T(1,128)S(1)} %pad_maximum_fusion), channel_id=1, source_target_pairs={{0,2},{1,3},{2,0},{3,1},{4,6},{5,7},{6,4},{7,5},{8,10},{9,11},{10,... | collective-permute-start | bytes 98312 | tf_op jit(solution)/shard_map/ppermute | solution.py:22
  28.6 5.7 %collective-permute-start.6 = (f32[4,1,2048]{2,1,0:T(1,128)S(1)}, f32[4,1,2048]{2,1,0:T(1,128)S(1)}, u32[]{:S(2)}, u32[]{:S(2)}) collective-permute-start(f32[4,1,2048]{2,1,0:T(1,128)S(1)} %pad_maximum_fusion), channel_id=1, source_target_pairs={{0,3},{1,2},{2,1},{3,0},{4,7},{5,6},{6,5},{7,4},{8,11},{9,10},{10,... | collective-permute-start | bytes 98312 | tf_op jit(solution)/shard_map/ppermute | solution.py:22
  37.4 4.6 %collective-permute-start.10 = (f32[2,1,768]{2,1,0:T(1,128)S(1)}, f32[2,1,768]{2,1,0:T(1,128)S(1)}, u32[]{:S(2)}, u32[]{:S(2)}) collective-permute-start(f32[2,1,768]{2,1,0:T(1,128)S(1)} %add.154), channel_id=1, source_target_pairs={{0,24},{4,28},{8,16},{12,20},{16,8},{20,12},{24,0},{28,4},{1,25},{... | collective-permute-start | bytes 18440 | tf_op jit(solution)/shard_map/ppermute | solution.py:22
  45.0 4.7 %collective-permute-start.12 = (f32[2,1,2048]{2,1,0:T(1,128)S(1)}, f32[2,1,2048]{2,1,0:T(1,128)S(1)}, u32[]{:S(2)}, u32[]{:S(2)}) collective-permute-start(f32[2,1,2048]{2,1,0:T(1,128)S(1)} %row_totals.4), channel_id=1, source_target_pairs={{0,2},{1,3},{2,0},{3,1},{4,6},{5,7},{6,4},{7,5},{8,10},{9,11},{10,... | collective-permute-start | bytes 49160 | tf_op jit(solution)/shard_map/ppermute | solution.py:22
  45.9 5.5 %collective-permute-start.13 = (f32[2,1,2048]{2,1,0:T(1,128)S(1)}, f32[2,1,2048]{2,1,0:T(1,128)S(1)}, u32[]{:S(2)}, u32[]{:S(2)}) collective-permute-start(f32[2,1,2048]{2,1,0:T(1,128)S(1)} %row_totals.4), channel_id=1, source_target_pairs={{0,3},{1,2},{2,1},{3,0},{4,7},{5,6},{6,5},{7,4},{8,11},{9,10},{10,... | collective-permute-start | bytes 49160 | tf_op jit(solution)/shard_map/ppermute | solution.py:22
  56.7 4.5 %collective-permute-start.17 = (f32[2,1,768]{2,1,0:T(1,128)S(1)}, f32[2,1,768]{2,1,0:T(1,128)S(1)}, u32[]{:S(2)}, u32[]{:S(2)}) collective-permute-start(f32[2,1,768]{2,1,0:T(1,128)S(1)} %add.161), channel_id=1, source_target_pairs={{0,24},{4,28},{8,16},{12,20},{16,8},{20,12},{24,0},{28,4},{1,25},{... | collective-permute-start | bytes 18440 | tf_op jit(solution)/shard_map/ppermute | solution.py:22
  63.5 5.5 %collective-permute-start.19 = (f32[2,1,2048]{2,1,0:T(1,128)S(1)}, f32[2,1,2048]{2,1,0:T(1,128)S(1)}, u32[]{:S(2)}, u32[]{:S(2)}) collective-permute-start(f32[2,1,2048]{2,1,0:T(1,128)S(1)} %row_totals.5), channel_id=1, source_target_pairs={{0,2},{1,3},{2,0},{3,1},{4,6},{5,7},{6,4},{7,5},{8,10},{9,11},{10,... | collective-permute-start | bytes 49160 | tf_op jit(solution)/shard_map/ppermute | solution.py:22
  67.3 5.5 %collective-permute-start.20 = (f32[2,1,2048]{2,1,0:T(1,128)S(1)}, f32[2,1,2048]{2,1,0:T(1,128)S(1)}, u32[]{:S(2)}, u32[]{:S(2)}) collective-permute-start(f32[2,1,2048]{2,1,0:T(1,128)S(1)} %row_totals.5), channel_id=1, source_target_pairs={{0,3},{1,2},{2,1},{3,0},{4,7},{5,6},{6,5},{7,4},{8,11},{9,10},{10,... | collective-permute-start | bytes 49160 | tf_op jit(solution)/shard_map/ppermute | solution.py:22
  86.0 13.4 %collective-permute-start.21 = (f32[4,96,256]{2,1,0:T(8,128)S(1)}, f32[4,96,256]{2,1,0:T(8,128)S(1)}, u32[]{:S(2)}, u32[]{:S(2)}) collective-permute-start(f32[4,96,256]{2,1,0:T(8,128)S(1)} %dynamic-slice_bitcast_fusion), channel_id=1, source_target_pairs={{0,4},{4,0},{8,12},{12,8},{16,20},{20,16},{24,28},{28,24},{1,5},{5... | collective-permute-start | bytes 1179656 | tf_op jit(solution)/shard_map/ppermute | solution.py:22
  89.0 5.9 %collective-permute-start.31 = (f32[1,72,256]{2,1,0:T(8,128)S(1)}, f32[1,72,256]{2,1,0:T(8,128)S(1)}, u32[]{:S(2)}, u32[]{:S(2)}) collective-permute-start(f32[1,72,256]{2,1,0:T(8,128)S(1)} %get-tuple-element.32), channel_id=1, source_target_pairs={{0,16},{4,20},{8,24},{12,28},{16,0},{20,4},{24,8},{28,12},{1,17},{... | collective-permute-start | bytes 221192 | tf_op jit(solution)/shard_map/ppermute | solution.py:22
  89.5 5.4 %collective-permute-start.32 = (f32[1,72,256]{2,1,0:T(8,128)S(1)}, f32[1,72,256]{2,1,0:T(8,128)S(1)}, u32[]{:S(2)}, u32[]{:S(2)}) collective-permute-start(f32[1,72,256]{2,1,0:T(8,128)S(1)} %get-tuple-element.31), channel_id=1, source_target_pairs={{0,24},{4,28},{8,16},{12,20},{16,8},{20,12},{24,0},{28,4},{1,25},{... | collective-permute-start | bytes 221192 | tf_op jit(solution)/shard_map/ppermute | solution.py:22
  95.0 6.5 %collective-permute-start.33 = (f32[72,256]{1,0:T(8,128)S(1)}, f32[72,256]{1,0:T(8,128)S(1)}, u32[]{:S(2)}, u32[]{:S(2)}) collective-permute-start(f32[72,256]{1,0:T(8,128)S(1)} %add_bitcast_fusion), channel_id=1, source_target_pairs={{0,1},{1,0},{2,3},{3,2},{4,5},{5,4},{6,7},{7,6},{8,9},{9,8},{10,11... | collective-permute-start | bytes 221192 | tf_op jit(solution)/shard_map/ppermute | solution.py:22
  95.0 8.0 %collective-permute-start.34 = (f32[72,256]{1,0:T(8,128)S(1)}, f32[72,256]{1,0:T(8,128)S(1)}, u32[]{:S(2)}, u32[]{:S(2)}) collective-permute-start(f32[72,256]{1,0:T(8,128)S(1)} %add_bitcast_fusion), channel_id=1, source_target_pairs={{0,2},{1,3},{2,0},{3,1},{4,6},{5,7},{6,4},{7,5},{8,10},{9,11},{10,... | collective-permute-start | bytes 221192 | tf_op jit(solution)/shard_map/ppermute | solution.py:22
  95.9 7.1 %collective-permute-start.35 = (f32[72,256]{1,0:T(8,128)S(1)}, f32[72,256]{1,0:T(8,128)S(1)}, u32[]{:S(2)}, u32[]{:S(2)}) collective-permute-start(f32[72,256]{1,0:T(8,128)S(1)} %add_bitcast_fusion), channel_id=1, source_target_pairs={{0,3},{1,2},{2,1},{3,0},{4,7},{5,6},{6,5},{7,4},{8,11},{9,10},{10,... | collective-permute-start | bytes 221192 | tf_op jit(solution)/shard_map/ppermute | solution.py:22
  99.5 6.8 %collective-permute-start.22 = (f32[1,96,256]{2,1,0:T(8,128)S(1)}, f32[1,96,256]{2,1,0:T(8,128)S(1)}, u32[]{:S(2)}, u32[]{:S(2)}) collective-permute-start(f32[1,96,256]{2,1,0:T(8,128)S(1)} %get-tuple-element.27), channel_id=1, source_target_pairs={{0,8},{4,12},{8,0},{12,4},{16,24},{20,28},{24,16},{28,20},{1,9},{5... | collective-permute-start | bytes 294920 | tf_op jit(solution)/shard_map/ppermute | solution.py:22
  100.1 7.8 %collective-permute-start.23 = (f32[1,96,256]{2,1,0:T(8,128)S(1)}, f32[1,96,256]{2,1,0:T(8,128)S(1)}, u32[]{:S(2)}, u32[]{:S(2)}) collective-permute-start(f32[1,96,256]{2,1,0:T(8,128)S(1)} %get-tuple-element.29), channel_id=1, source_target_pairs={{0,16},{4,20},{8,24},{12,28},{16,0},{20,4},{24,8},{28,12},{1,17},{... | collective-permute-start | bytes 294920 | tf_op jit(solution)/shard_map/ppermute | solution.py:22
  101.4 6.5 %collective-permute-start.24 = (f32[1,96,256]{2,1,0:T(8,128)S(1)}, f32[1,96,256]{2,1,0:T(8,128)S(1)}, u32[]{:S(2)}, u32[]{:S(2)}) collective-permute-start(f32[1,96,256]{2,1,0:T(8,128)S(1)} %get-tuple-element.28), channel_id=1, source_target_pairs={{0,24},{4,28},{8,16},{12,20},{16,8},{20,12},{24,0},{28,4},{1,25},{... | collective-permute-start | bytes 294920 | tf_op jit(solution)/shard_map/ppermute | solution.py:22
  103.1 7.2 %collective-permute-start.36 = (f32[1,64,256]{2,1,0:T(8,128)S(1)}, f32[1,64,256]{2,1,0:T(8,128)S(1)}, u32[]{:S(2)}, u32[]{:S(2)}) collective-permute-start(f32[1,64,256]{2,1,0:T(8,128)S(1)} %slice_bitcast_fusion), channel_id=1, source_target_pairs={{0,8},{4,12},{8,0},{12,4},{16,24},{20,28},{24,16},{28,20},{1,9},{5... | collective-permute-start | bytes 196616 | tf_op jit(solution)/shard_map/ppermute | solution.py:22
  103.7 7.9 %collective-permute-start.37 = (f32[1,64,256]{2,1,0:T(8,128)S(1)}, f32[1,64,256]{2,1,0:T(8,128)S(1)}, u32[]{:S(2)}, u32[]{:S(2)}) collective-permute-start(f32[1,64,256]{2,1,0:T(8,128)S(1)} %slice_bitcast_fusion), channel_id=1, source_target_pairs={{0,16},{4,20},{8,24},{12,28},{16,0},{20,4},{24,8},{28,12},{1,17},{... | collective-permute-start | bytes 196616 | tf_op jit(solution)/shard_map/ppermute | solution.py:22
  106.3 5.4 %collective-permute-start.38 = (f32[1,64,256]{2,1,0:T(8,128)S(1)}, f32[1,64,256]{2,1,0:T(8,128)S(1)}, u32[]{:S(2)}, u32[]{:S(2)}) collective-permute-start(f32[1,64,256]{2,1,0:T(8,128)S(1)} %slice_bitcast_fusion), channel_id=1, source_target_pairs={{0,24},{4,28},{8,16},{12,20},{16,8},{20,12},{24,0},{28,4},{1,25},{... | collective-permute-start | bytes 196616 | tf_op jit(solution)/shard_map/ppermute | solution.py:22
  108.0 4.7 %collective-permute-start.25 = (f32[1,96,256]{2,1,0:T(8,128)S(1)}, f32[1,96,256]{2,1,0:T(8,128)S(1)}, u32[]{:S(2)}, u32[]{:S(2)}) collective-permute-start(f32[1,96,256]{2,1,0:T(8,128)S(1)} %get-tuple-element.26), channel_id=1, source_target_pairs={{0,8},{4,12},{8,0},{12,4},{16,24},{20,28},{24,16},{28,20},{1,9},{5... | collective-permute-start | bytes 294920 | tf_op jit(solution)/shard_map/ppermute | solution.py:22
  109.5 4.6 %collective-permute-start.26 = (f32[1,96,256]{2,1,0:T(8,128)S(1)}, f32[1,96,256]{2,1,0:T(8,128)S(1)}, u32[]{:S(2)}, u32[]{:S(2)}) collective-permute-start(f32[1,96,256]{2,1,0:T(8,128)S(1)} %get-tuple-element.26), channel_id=1, source_target_pairs={{0,16},{4,20},{8,24},{12,28},{16,0},{20,4},{24,8},{28,12},{1,17},{... | collective-permute-start | bytes 294920 | tf_op jit(solution)/shard_map/ppermute | solution.py:22
  110.3 5.5 %collective-permute-start.27 = (f32[1,96,256]{2,1,0:T(8,128)S(1)}, f32[1,96,256]{2,1,0:T(8,128)S(1)}, u32[]{:S(2)}, u32[]{:S(2)}) collective-permute-start(f32[1,96,256]{2,1,0:T(8,128)S(1)} %get-tuple-element.26), channel_id=1, source_target_pairs={{0,24},{4,28},{8,16},{12,20},{16,8},{20,12},{24,0},{28,4},{1,25},{... | collective-permute-start | bytes 294920 | tf_op jit(solution)/shard_map/ppermute | solution.py:22
  (21 other events, 81.7 us)

commit v4 on v3

--- a/solution.py
+++ b/solution.py
@@ -15,6 +15,7 @@
 LOG2_E = 1.4426950408889634
 LANES = 128
 CHUNK = 256
+FINAL_TYPE = jnp.float32
 VMEM_LIMIT = 20 * 1024 * 1024
 
 
@@ -35,7 +36,7 @@
 def sum_over(values, axis, first):
     size = lax.axis_size(axis)
     for low, width in stages(size, first):
-        parts = [swap(values, axis, size, k << low) for k in range(1, 1 << width)]
+        parts = [swap(values, axis, size, k << low) for k in reversed(range(1, 1 << width))]
         values = functools.reduce(jnp.add, parts, values)
     return values
 
@@ -51,7 +52,7 @@
         values = values.reshape((rest, ways) + block)
         mine = (me >> low) & (ways - 1)
         own = lax.dynamic_index_in_dim(values, mine, 1, keepdims=False)
-        for k in range(1, ways):
+        for k in reversed(range(1, ways)):
             out = lax.dynamic_index_in_dim(values, mine ^ k, 1, keepdims=False)
             own = own + swap(out, axis, size, k << low)
         values = own[None]
@@ -66,9 +67,9 @@
     for low, width in reversed(stages(size, first)):
         ways = 1 << width
         mine = (me >> low) & (ways - 1)
-        parts = [values] + [swap(values, axis, size, k << low) for k in range(1, ways)]
+        parts = {k: swap(values, axis, size, k << low) if k else values for k in reversed(range(ways))}
         out = jnp.zeros((values.shape[0], ways) + block, values.dtype)
-        for k, part in enumerate(parts):
+        for k, part in parts.items():
             out = lax.dynamic_update_slice_in_dim(out, part[:, None], mine ^ k, 1)
         values = out.reshape((-1,) + block)
     return values
@@ -131,11 +132,14 @@
 
 
 def first_kernel(
-    valid, width, feats_ref, proj_ref, proto_ref, soft_ref, half_ref, col_ref, denom_ref, proto_half_ref,
-    turned_ref, split_ref, raw_ref, acc_ref, unit_ref, in_ref, out_ref, raw_out_ref, in_sems, out_sems, raw_sems,
+    valid, width, feats_ref, proj_ref, proto_ref, codes_ref, col_ref, denom_ref, proto_half_ref,
+    turned_ref, split_ref, raw_ref, acc_ref, unit_ref, in_ref, out_ref, raw_out_ref, proto_in_ref, in_sems,
+    out_sems, raw_sems, proto_sems,
 ):
-    count = half_ref.shape[-1] // width
+    count = denom_ref.shape[-1] // width
     spans = [pl.ds(at * width, width) for at in range(count)]
+    proto_load = pltpu.make_async_copy(proto_ref, proto_in_ref, proto_sems.at[0])
+    proto_load.start()
     loads = copies(lambda at: feats_ref.at[spans[at]], lambda at: in_ref.at[spans[at]], in_sems, count)
     stores = copies(lambda at: out_ref.at[:, spans[at]], lambda at: split_ref.at[:, spans[at]], out_sems, count)
     raw_stores = copies(
@@ -146,7 +150,8 @@
 
     edge = valid // 8 * 8
     unit_ref[edge:] = jnp.zeros_like(unit_ref[edge:])
-    unit_ref[:valid] = proto_ref[...]
+    proto_load.wait()
+    unit_ref[:valid] = proto_in_ref[...]
     unit, _ = unit_rows(unit_ref[...])
     proto_half_ref[...] = unit.astype(jnp.bfloat16)
     turned_ref[...] = jnp.transpose(unit).astype(jnp.bfloat16)
@@ -162,7 +167,6 @@
             raw_out_ref[view, :, lanes] = raw
             unit, _ = unit_columns(raw)
             half = unit.astype(jnp.bfloat16)
-            half_ref[view, :, lanes] = half
             denom = jnp.zeros((8, width), jnp.float32)
             for start in range(0, proto_half_ref.shape[0], CHUNK):
                 logits = product(proto_half_ref[start : start + CHUNK], half, NN)
@@ -170,9 +174,10 @@
                 if start + CHUNK > edge:
                     place = lax.broadcasted_iota(jnp.int32, soft.shape, 0) + start
                     soft = jnp.where(place < valid, soft, 0.0)
-                soft_ref[view, start : start + CHUNK, lanes] = soft
+                code = soft * soft
+                codes_ref[view, start : start + CHUNK, lanes] = code
                 denom = denom + jnp.sum(soft.reshape(-1, 8, width), axis=0)
-                acc_ref[view, start : start + CHUNK] += lane_sums(soft * soft)
+                acc_ref[view, start : start + CHUNK] += lane_sums(code)
             denom_ref[view, :, lanes] = jnp.sum(denom, axis=0, keepdims=True)
         raw_stores[at].start()
 
@@ -182,28 +187,28 @@
         store.wait()
 
 
-def row_kernel(valid, width, soft_ref, sums_ref, row_ref, scale_ref):
+def row_kernel(valid, width, codes_ref, sums_ref, row_ref, scale_ref):
     for view in range(2):
         scale_ref[view] = column_scale(valid, sums_ref[view])
 
     def step(view, lanes):
         total = jnp.zeros((8, width), jnp.float32)
-        for start in range(0, soft_ref.shape[1], 8):
-            soft = soft_ref[view, start : start + 8, lanes]
-            total = total + soft * soft * widen(scale_ref[view, start : start + 8], width)
+        for start in range(0, codes_ref.shape[1], 8):
+            code = codes_ref[view, start : start + 8, lanes]
+            total = total + code * widen(scale_ref[view, start : start + 8], width)
         row_ref[view, :, lanes] = jnp.sum(total, axis=0, keepdims=True)
 
     tiles(row_ref, width, step)
 
 
-def col_kernel(width, soft_ref, sums_ref, col_ref, acc_ref):
+def col_kernel(width, codes_ref, sums_ref, col_ref, acc_ref):
     acc_ref[...] = jnp.zeros_like(acc_ref)
 
     def step(view, lanes):
         scale = jnp.broadcast_to(1.0 / sums_ref[view, :, lanes], (8, width))
-        for start in range(0, soft_ref.shape[1], 8):
-            soft = soft_ref[view, start : start + 8, lanes]
-            acc_ref[view, start : start + 8] += lane_sums(soft * soft * scale)
+        for start in range(0, codes_ref.shape[1], 8):
+            code = codes_ref[view, start : start + 8, lanes]
+            acc_ref[view, start : start + 8] += lane_sums(code * scale)
 
     tiles(sums_ref, width, step)
     for view in range(2):
@@ -211,10 +216,10 @@
 
 
 def grad_kernel(
-    valid, width, factor, feats_ref, raw_ref, proto_ref, turned_ref, half_ref, denom_ref, row_ref, col_ref,
+    valid, width, factor, feats_ref, raw_ref, proto_ref, turned_ref, denom_ref, row_ref, col_ref,
     proto_out, proj_out, loss_ref, scale_ref, grad_ref, turn_ref, in_ref, raw_in_ref, in_sems, raw_sems,
 ):
-    count = half_ref.shape[-1] // width
+    count = row_ref.shape[-1] // width
     spans = [pl.ds(at * width, width) for at in range(count)]
     loads = copies(lambda at: feats_ref.at[:, spans[at]], lambda at: in_ref.at[:, spans[at]], in_sems, count)
     raw_loads = copies(
@@ -225,14 +230,17 @@
         loads[at].start()
     for view in range(2):
         scale_ref[view] = column_scale(valid, col_ref[view])
+    sides = [slice(view * width, (view + 1) * width) for view in range(2)]
     loss = jnp.zeros((8, width), jnp.float32)
     for at in range(count):
         lanes = spans[at]
-        both = lambda ref: jnp.concatenate([ref[view, :, lanes] for view in range(2)], axis=1)
-        halves = [half_ref[view, :, lanes] for view in range(2)]
+        raw_loads[at].wait()
+        raw = jnp.concatenate([raw_in_ref[view, :, lanes] for view in range(2)], axis=1)
+        unit, inverse = unit_columns(raw)
+        halves = unit.astype(jnp.bfloat16)
         for start in range(0, proto_ref.shape[0], CHUNK):
             part = slice(start, start + CHUNK)
-            logits = [product(proto_ref[part], halves[view], NN) for view in range(2)]
+            logits = [product(proto_ref[part], halves[:, side], NN) for side in sides]
             softs = [jnp.exp2(logits[view] * (LOG2_E / SOFTMAX_TEMPER)) for view in range(2)]
             for view in range(2):
                 other = 1 - view
@@ -240,11 +248,10 @@
                 target = target * (factor / row_ref[other, :, lanes])
                 loss = loss + jnp.sum((logits[view] * target).reshape(-1, 8, width), axis=0)
                 grad = softs[view] * (factor / denom_ref[view, :, lanes]) - target
-                grad_ref[part, view * width : (view + 1) * width] = grad.astype(jnp.bfloat16)
-        proto_part = product(grad_ref[...], jnp.concatenate(halves, axis=1), NT)
+                grad_ref[part, sides[view]] = grad.astype(jnp.bfloat16)
+        proto_part = product(grad_ref[...], halves, NT)
         grad_unit = product(turned_ref[...], grad_ref[...], NN)
-        raw_loads[at].wait()
-        unit, inverse = unit_columns(both(raw_in_ref))
+        unit, inverse = unit_columns(raw)
         along = jnp.sum(unit * grad_unit, axis=0, keepdims=True)
         grad_raw = ((grad_unit - unit * along) * inverse).astype(jnp.bfloat16)
         loads[at].wait()
@@ -304,23 +311,24 @@
     turned_proj = projection.T
     sems = pltpu.SemaphoreType.DMA((count,))
     far = lambda array: pltpu.with_memory_space_constraint(array, pltpu.HBM)
-    soft, half, col_part, soft_part, proto_half, turned, feats, raw = call(
+    codes, col_part, soft_part, proto_half, turned, feats, raw = call(
         functools.partial(first_kernel, valid, tile), "first_totals",
         [
-            ((2, block, rows), single), ((2, width, rows), half_type), col_shape, row_shape,
-            ((block, width), half_type), ((width, block), half_type), (split, half_type), ((2, width, rows), single),
+            ((2, block, rows), single), col_shape, row_shape, ((block, width), half_type),
+            ((width, block), half_type), (split, half_type), ((2, width, rows), single),
         ],
         [
             column, pltpu.VMEM((block, width), single), pltpu.VMEM(features.shape, half_type),
-            pltpu.VMEM(split, half_type), pltpu.VMEM((2, width, rows), single), sems, sems, sems,
+            pltpu.VMEM(split, half_type), pltpu.VMEM((2, width, rows), single),
+            pltpu.VMEM(prototypes.shape, single), sems, sems, sems, pltpu.SemaphoreType.DMA((1,)),
         ],
-        work, far(features), turned_proj, prototypes, far_in=(0,), far_out=(6, 7),
+        work, far(features), turned_proj, far(prototypes), far_in=(0, 2), far_out=(5, 6),
     )
     row_call = functools.partial(
-        call, functools.partial(row_kernel, valid, min(512, rows)), "row_totals", [row_shape], [column], work, soft
+        call, functools.partial(row_kernel, valid, min(512, rows)), "row_totals", [row_shape], [column], work, codes
     )
     col_call = functools.partial(
-        call, functools.partial(col_kernel, min(512, rows)), "column_totals", [col_shape], [column], work, soft
+        call, functools.partial(col_kernel, min(512, rows)), "column_totals", [col_shape], [column], work, codes
     )
 
     col_sums = sum_over(col_part, "dp", 1)
@@ -337,20 +345,26 @@
             column, pltpu.VMEM((block, 2 * tile), half_type), pltpu.VMEM(projection.shape[::-1], single),
             pltpu.VMEM(split, half_type), pltpu.VMEM((2, width, rows), single), sems, sems,
         ],
-        3 * work, far(feats), far(raw), proto_half, turned, half, denoms, row_sums, col_sums, far_in=(0, 1),
+        3 * work, far(feats), far(raw), proto_half, turned, denoms, row_sums, col_sums, far_in=(0, 1),
     )
     loss_rows = jnp.broadcast_to(loss[None], (shards,) + loss.shape)
     proj_part = jnp.concatenate([proj_part.reshape(shards, -1, width), loss_rows], axis=1)
     proj_sum = sum_over(scatter_sum(proj_part, "dp", 1), "mp", 2)
     loss_value = -proj_sum[-1, 0] / (2.0 * batch_row_count)
-    proj_grad = gather_blocks(proj_sum[:-8], "dp", 1).reshape(projection.shape)
-
-    proto_sum = scatter_sum(proto_part.reshape(shards, -1, width), "dp", 1)
-    proto_grad = gather_blocks(proto_sum, "dp", 1).reshape(block, width)[:valid]
-    proto_unit, proto_inverse = unit_rows(prototypes)
+
+    share = block // shards
+    proto_grad = scatter_sum(proto_part.reshape(shards, share, width), "dp", 1)
+    mine = lax.dynamic_slice_in_dim(
+        jnp.pad(prototypes, ((0, block - valid), (0, 0))), lax.axis_index("dp") * share, share, 0
+    )
+    proto_unit, proto_inverse = unit_rows(mine)
     along_proto = jnp.sum(proto_unit * proto_grad, axis=-1, keepdims=True)
-    grad_protos = (proto_grad - proto_unit * along_proto) * proto_inverse
-    return (grad_protos, proj_grad, loss_value)
+    grad_share = (proto_grad - proto_unit * along_proto) * proto_inverse
+
+    both = jnp.concatenate([grad_share, proj_sum[:-8]]).astype(FINAL_TYPE)
+    both = gather_blocks(both, "dp", 1).astype(single)
+    grad_protos = both[:, :share].reshape(block, width)[:valid]
+    return (grad_protos, both[:, share:].reshape(projection.shape), loss_value)
 
 
 def solution(mesh):

time: 120 us -> 113 us (0.942)
  starting transfers between devices: 45 us -> 40.7 us
  waiting for transfers between devices: 35.8 us -> 34.4 us
  other arithmetic: 2.04 us -> 0.81 us
    ppermute x40 -> x36, starting transfers between devices: 45 us -> 40.7 us  [swap(): return lax.ppermute(values, axis, [(i, i ^ offset) for i in range(size)])]
    slice x0 -> x4, local copies, waits for them, and re-layouts: none -> 1.81 us  [the longest x2 0.98 us: body(): grad_protos = both[:, :share].reshape(block, width)[:valid]]
    unnamed x11 -> x3, local copies, waits for them, and re-layouts: 3.81 us -> 2.06 us
    ppermute x40 -> x36, waiting for transfers between devices: 35.8 us -> 34.4 us  [swap(): return lax.ppermute(values, axis, [(i, i ^ offset) for i in range(size)])]
  transfers between devices with their start and end apart: 40 -> 36, of which waited for: 24 -> 32; matrix products, arithmetic and copies ran while one was open for 1% -> 1% of each run, Pallas kernels for 0% -> 0%
where the time goes in v4:
time: 113 us
  starting transfers between devices  40.7 us (36%)
  waiting for transfers between devices  34.4 us (30%)
  Pallas kernels  29.2 us (26%)
  local copies, waits for them, and re-layouts  4.82 us (4%)
  between operations  2.76 us (2%)
    ppermute x36, starting transfers between devices, swap(): return lax.ppermute(values, axis, [(i, i ^ offset) for i in range(size)])  40.7 us
    ppermute x36, waiting for transfers between devices, swap(): return lax.ppermute(values, axis, [(i, i ^ offset) for i in range(size)])  34.4 us
    pallas_call x7, Pallas kernels, call(): pl.pallas_call(kernel, in_specs=[IN_HBM if at in far_in else IN_VMEM for...  29.2 us
  transfers between devices with their start and end apart: 36, of which 32 were waited for; matrix products, arithmetic and copies ran while one was open for 1% of the time, Pallas kernels for 0%

profile of v4, /device:TPU:0, one launch (start us, length us, event | category | flops | bytes accessed | tf_op | source)
XLA Modules:
  0.0 112.7 jit_solution(15048133811035521184)
XLA Ops:
  1.7 10.2 %first_totals.1 = (f32[2,768,2048]{2,1,0:T(8,128)S(1)}, f32[2,1,768]{2,1,0:T(1,128)S(1)}, f32[2,1,2048]{2,1,0:T(1,128)S(1)}, bf16[768,256]{1,0:T(8,128)(2,1)S(1)...) custom-call(bf16[2048,2,512]{2,1,0:T(2,128)(2,1)} %feats_ref.1, ...), custom_call_target="tpu_custom_call" | custom-call | flops 1610612736 | bytes 1048576 | tf_op jit(solution)/shard_map/first_totals/pallas_call | solution.py:285
  13.3 3.9 %collective-permute-start.1 = (f32[2,1,768]{2,1,0:T(1,128)S(1)}, f32[2,1,768]{2,1,0:T(1,128)S(1)}, u32[]{:S(2)}, u32[]{:S(2)}) collective-permute-start(f32[2,1,768]{2,1,0:T(1,128)S(1)} %add.146), channel_id=1, source_target_pairs={{0,24},{4,28},{8,16},{12,20},{16,8},{20,12},{24,0},{28,4},{1,25},{... | collective-permute-start | bytes 18440 | tf_op jit(solution)/shard_map/ppermute | solution.py:23
  18.8 2.0 %collective-permute-done.2 = f32[2,1,768]{2,1,0:T(1,128)S(1)} collective-permute-done((f32[2,1,768]{2,1,0:T(1,128)S(1)}, f32[2,1,768]{2,1,0:T(1,128)S(1)}, u32[]{:S(2)}, u32[]{:S(2)}) %collective-permute-start.2) | collective-permute-done | bytes 6176 | tf_op jit(solution)/shard_map/ppermute | solution.py:23
  21.3 1.6 %row_totals.3 = f32[2,1,2048]{2,1,0:T(1,128)S(1)} custom-call(f32[2,768,2048]{2,1,0:T(8,128)S(1)} %get-tuple-element.17.codes_ref, f32[2,1,768]{2,1,0:T(1,128)S(1)} %add_add_fusion.7.sums_ref), custom_call_target="tpu_custom_call" | custom-call | flops 1610612736 | bytes 1048576 | tf_op jit(solution)/shard_map/row_totals/pallas_call | solution.py:285
  22.9 3.7 %collective-permute-start.4 = (f32[4,1,2048]{2,1,0:T(1,128)S(1)}, f32[4,1,2048]{2,1,0:T(1,128)S(1)}, u32[]{:S(2)}, u32[]{:S(2)}) collective-permute-start(f32[4,1,2048]{2,1,0:T(1,128)S(1)} %pad_maximum_fusion.1), channel_id=1, source_target_pairs={{0,3},{1,2},{2,1},{3,0},{4,7},{5,6},{6,5},{7,4},{8,11},{9,10},{10,... | collective-permute-start | bytes 98312 | tf_op jit(solution)/shard_map/ppermute | solution.py:23
  28.8 2.6 %collective-permute-done.5 = f32[4,1,2048]{2,1,0:T(1,128)S(1)} collective-permute-done((f32[4,1,2048]{2,1,0:T(1,128)S(1)}, f32[4,1,2048]{2,1,0:T(1,128)S(1)}, u32[]{:S(2)}, u32[]{:S(2)}) %collective-permute-start.5) | collective-permute-done | bytes 32800 | tf_op jit(solution)/shard_map/ppermute | solution.py:23
  34.8 2.4 %collective-permute-start.8 = (f32[2,1,768]{2,1,0:T(1,128)S(1)}, f32[2,1,768]{2,1,0:T(1,128)S(1)}, u32[]{:S(2)}, u32[]{:S(2)}) collective-permute-start(f32[2,1,768]{2,1,0:T(1,128)S(1)} %add.153), channel_id=1, source_target_pairs={{0,24},{4,28},{8,16},{12,20},{16,8},{20,12},{24,0},{28,4},{1,25},{... | collective-permute-start | bytes 18440 | tf_op jit(solution)/shard_map/ppermute | solution.py:23
  39.3 1.5 %collective-permute-done.9 = f32[2,1,768]{2,1,0:T(1,128)S(1)} collective-permute-done((f32[2,1,768]{2,1,0:T(1,128)S(1)}, f32[2,1,768]{2,1,0:T(1,128)S(1)}, u32[]{:S(2)}, u32[]{:S(2)}) %collective-permute-start.9) | collective-permute-done | bytes 6176 | tf_op jit(solution)/shard_map/ppermute | solution.py:23
  40.9 1.6 %row_totals.4 = f32[2,1,2048]{2,1,0:T(1,128)S(1)} custom-call(f32[2,768,2048]{2,1,0:T(8,128)S(1)} %get-tuple-element.17.codes_ref, f32[2,1,768]{2,1,0:T(1,128)S(1)} %add_add_fusion.6.sums_ref), custom_call_target="tpu_custom_call" | custom-call | flops 1610612736 | bytes 1048576 | tf_op jit(solution)/shard_map/row_totals/pallas_call | solution.py:285
  42.5 1.5 %collective-permute-start.11 = (f32[2,1,2048]{2,1,0:T(1,128)S(1)}, f32[2,1,2048]{2,1,0:T(1,128)S(1)}, u32[]{:S(2)}, u32[]{:S(2)}) collective-permute-start(f32[2,1,2048]{2,1,0:T(1,128)S(1)} %row_totals.4), channel_id=1, source_target_pairs={{0,3},{1,2},{2,1},{3,0},{4,7},{5,6},{6,5},{7,4},{8,11},{9,10},{10,... | collective-permute-start | bytes 49160 | tf_op jit(solution)/shard_map/ppermute | solution.py:23
  44.6 2.3 %collective-permute-start.13 = (f32[2,1,2048]{2,1,0:T(1,128)S(1)}, f32[2,1,2048]{2,1,0:T(1,128)S(1)}, u32[]{:S(2)}, u32[]{:S(2)}) collective-permute-start(f32[2,1,2048]{2,1,0:T(1,128)S(1)} %row_totals.4), channel_id=1, source_target_pairs={{0,1},{1,0},{2,3},{3,2},{4,5},{5,4},{6,7},{7,6},{8,9},{9,8},{10,11... | collective-permute-start | bytes 49160 | tf_op jit(solution)/shard_map/ppermute | solution.py:23
  53.6 1.5 %collective-permute-start.17 = (f32[2,1,768]{2,1,0:T(1,128)S(1)}, f32[2,1,768]{2,1,0:T(1,128)S(1)}, u32[]{:S(2)}, u32[]{:S(2)}) collective-permute-start(f32[2,1,768]{2,1,0:T(1,128)S(1)} %add.160), channel_id=1, source_target_pairs={{0,8},{4,12},{8,0},{12,4},{16,24},{20,28},{24,16},{28,20},{1,9},{5... | collective-permute-start | bytes 18440 | tf_op jit(solution)/shard_map/ppermute | solution.py:23
  57.2 1.8 %row_totals.5 = f32[2,1,2048]{2,1,0:T(1,128)S(1)} custom-call(f32[2,768,2048]{2,1,0:T(8,128)S(1)} %get-tuple-element.17.codes_ref, f32[2,1,768]{2,1,0:T(1,128)S(1)} %add_add_fusion.5.sums_ref.col_ref), custom_call_target="tpu_custom_call" | custom-call | flops 1610612736 | bytes 1048576 | tf_op jit(solution)/shard_map/row_totals/pallas_call | solution.py:285
  59.0 2.5 %collective-permute-start.18 = (f32[2,1,2048]{2,1,0:T(1,128)S(1)}, f32[2,1,2048]{2,1,0:T(1,128)S(1)}, u32[]{:S(2)}, u32[]{:S(2)}) collective-permute-start(f32[2,1,2048]{2,1,0:T(1,128)S(1)} %row_totals.5), channel_id=1, source_target_pairs={{0,3},{1,2},{2,1},{3,0},{4,7},{5,6},{6,5},{7,4},{8,11},{9,10},{10,... | collective-permute-start | bytes 49160 | tf_op jit(solution)/shard_map/ppermute | solution.py:23
  64.6 1.5 %collective-permute-done.19 = f32[2,1,2048]{2,1,0:T(1,128)S(1)} collective-permute-done((f32[2,1,2048]{2,1,0:T(1,128)S(1)}, f32[2,1,2048]{2,1,0:T(1,128)S(1)}, u32[]{:S(2)}, u32[]{:S(2)}) %collective-permute-start.19) | collective-permute-done | bytes 16416 | tf_op jit(solution)/shard_map/ppermute | solution.py:23
  66.3 11.2 %gradients.1 = (f32[768,256]{1,0:T(8,128)S(1)}, f32[512,256]{1,0:T(8,128)S(1)}, f32[8,256]{1,0:T(8,128)S(1)}) custom-call(bf16[2,2048,512]{2,1,0:T(8,128)(2,1)} %get-tuple-element.13.feats_ref, f32[2,256,2048]{2,1,0:T(8,128)} %get-tuple-element.14.raw_ref, bf16[768,256]{1,0:T(8,128)(2,1)S(1)} %get-tuple-element.15.proto_ref, ...), custom_call_target="tpu_custom_call" | custom-call | flops 4831838208 | bytes 1048576 | tf_op jit(solution)/shard_map/gradients/pallas_call | solution.py:285
  79.3 1.5 %collective-permute-start.26 = (f32[1,72,256]{2,1,0:T(8,128)S(1)}, f32[1,72,256]{2,1,0:T(8,128)S(1)}, u32[]{:S(2)}, u32[]{:S(2)}) collective-permute-start(f32[1,72,256]{2,1,0:T(8,128)S(1)} %get-tuple-element.28), channel_id=1, source_target_pairs={{0,24},{4,28},{8,16},{12,20},{16,8},{20,12},{24,0},{28,4},{1,25},{... | collective-permute-start | bytes 221192 | tf_op jit(solution)/shard_map/ppermute | solution.py:23
  80.8 1.5 %collective-permute-start.27 = (f32[1,72,256]{2,1,0:T(8,128)S(1)}, f32[1,72,256]{2,1,0:T(8,128)S(1)}, u32[]{:S(2)}, u32[]{:S(2)}) collective-permute-start(f32[1,72,256]{2,1,0:T(8,128)S(1)} %get-tuple-element.30), channel_id=1, source_target_pairs={{0,16},{4,20},{8,24},{12,28},{16,0},{20,4},{24,8},{28,12},{1,17},{... | collective-permute-start | bytes 221192 | tf_op jit(solution)/shard_map/ppermute | solution.py:23
  82.9 2.0 %collective-permute-done.26 = f32[1,72,256]{2,1,0:T(8,128)S(1)} collective-permute-done((f32[1,72,256]{2,1,0:T(8,128)S(1)}, f32[1,72,256]{2,1,0:T(8,128)S(1)}, u32[]{:S(2)}, u32[]{:S(2)}) %collective-permute-start.26) | collective-permute-done | bytes 73760 | tf_op jit(solution)/shard_map/ppermute | solution.py:23
  86.7 1.5 %collective-permute-start.29 = (f32[72,256]{1,0:T(8,128)S(1)}, f32[72,256]{1,0:T(8,128)S(1)}, u32[]{:S(2)}, u32[]{:S(2)}) collective-permute-start(f32[72,256]{1,0:T(8,128)S(1)} %add_bitcast_fusion), channel_id=1, source_target_pairs={{0,3},{1,2},{2,1},{3,0},{4,7},{5,6},{6,5},{7,4},{8,11},{9,10},{10,... | collective-permute-start | bytes 221192 | tf_op jit(solution)/shard_map/ppermute | solution.py:23
  89.2 2.0 %collective-permute-start.31 = (f32[72,256]{1,0:T(8,128)S(1)}, f32[72,256]{1,0:T(8,128)S(1)}, u32[]{:S(2)}, u32[]{:S(2)}) collective-permute-start(f32[72,256]{1,0:T(8,128)S(1)} %add_bitcast_fusion), channel_id=1, source_target_pairs={{0,1},{1,0},{2,3},{3,2},{4,5},{5,4},{6,7},{7,6},{8,9},{9,8},{10,11... | collective-permute-start | bytes 221192 | tf_op jit(solution)/shard_map/ppermute | solution.py:23
  99.8 1.5 %collective-permute-start.33 = (f32[1,160,256]{2,1,0:T(8,128)S(1)}, f32[1,160,256]{2,1,0:T(8,128)S(1)}, u32[]{:S(2)}, u32[]{:S(2)}) collective-permute-start(f32[1,160,256]{2,1,0:T(8,128)S(1)} %fusion.5), channel_id=1, source_target_pairs={{0,16},{4,20},{8,24},{12,28},{16,0},{20,4},{24,8},{28,12},{1,17},{... | collective-permute-start | bytes 491528 | tf_op jit(solution)/shard_map/ppermute | solution.py:23
  102.3 3.4 %collective-permute-done.32 = f32[1,160,256]{2,1,0:T(8,128)S(1)} collective-permute-done((f32[1,160,256]{2,1,0:T(8,128)S(1)}, f32[1,160,256]{2,1,0:T(8,128)S(1)}, u32[]{:S(2)}, u32[]{:S(2)}) %collective-permute-start.32) | collective-permute-done | bytes 163872 | tf_op jit(solution)/shard_map/ppermute | solution.py:23
  105.7 1.5 %collective-permute-done.33 = f32[1,160,256]{2,1,0:T(8,128)S(1)} collective-permute-done((f32[1,160,256]{2,1,0:T(8,128)S(1)}, f32[1,160,256]{2,1,0:T(8,128)S(1)}, u32[]{:S(2)}, u32[]{:S(2)}) %collective-permute-start.33) | collective-permute-done | bytes 163872 | tf_op jit(solution)/shard_map/ppermute | solution.py:23
  (96 shorter events, 43.2 us)
Async XLA Ops:
  13.3 5.5 %collective-permute-start.1 = (f32[2,1,768]{2,1,0:T(1,128)S(1)}, f32[2,1,768]{2,1,0:T(1,128)S(1)}, u32[]{:S(2)}, u32[]{:S(2)}) collective-permute-start(f32[2,1,768]{2,1,0:T(1,128)S(1)} %add.146), channel_id=1, source_target_pairs={{0,24},{4,28},{8,16},{12,20},{16,8},{20,12},{24,0},{28,4},{1,25},{... | collective-permute-start | bytes 18440 | tf_op jit(solution)/shard_map/ppermute | solution.py:23
  22.9 5.9 %collective-permute-start.4 = (f32[4,1,2048]{2,1,0:T(1,128)S(1)}, f32[4,1,2048]{2,1,0:T(1,128)S(1)}, u32[]{:S(2)}, u32[]{:S(2)}) collective-permute-start(f32[4,1,2048]{2,1,0:T(1,128)S(1)} %pad_maximum_fusion.1), channel_id=1, source_target_pairs={{0,3},{1,2},{2,1},{3,0},{4,7},{5,6},{6,5},{7,4},{8,11},{9,10},{10,... | collective-permute-start | bytes 98312 | tf_op jit(solution)/shard_map/ppermute | solution.py:23
  26.6 4.8 %collective-permute-start.5 = (f32[4,1,2048]{2,1,0:T(1,128)S(1)}, f32[4,1,2048]{2,1,0:T(1,128)S(1)}, u32[]{:S(2)}, u32[]{:S(2)}) collective-permute-start(f32[4,1,2048]{2,1,0:T(1,128)S(1)} %pad_maximum_fusion.1), channel_id=1, source_target_pairs={{0,2},{1,3},{2,0},{3,1},{4,6},{5,7},{6,4},{7,5},{8,10},{9,11},{10,... | collective-permute-start | bytes 98312 | tf_op jit(solution)/shard_map/ppermute | solution.py:23
  26.6 4.8 %collective-permute-start.6 = (f32[4,1,2048]{2,1,0:T(1,128)S(1)}, f32[4,1,2048]{2,1,0:T(1,128)S(1)}, u32[]{:S(2)}, u32[]{:S(2)}) collective-permute-start(f32[4,1,2048]{2,1,0:T(1,128)S(1)} %pad_maximum_fusion.1), channel_id=1, source_target_pairs={{0,1},{1,0},{2,3},{3,2},{4,5},{5,4},{6,7},{7,6},{8,9},{9,8},{10,11... | collective-permute-start | bytes 98312 | tf_op jit(solution)/shard_map/ppermute | solution.py:23
  34.8 4.5 %collective-permute-start.8 = (f32[2,1,768]{2,1,0:T(1,128)S(1)}, f32[2,1,768]{2,1,0:T(1,128)S(1)}, u32[]{:S(2)}, u32[]{:S(2)}) collective-permute-start(f32[2,1,768]{2,1,0:T(1,128)S(1)} %add.153), channel_id=1, source_target_pairs={{0,24},{4,28},{8,16},{12,20},{16,8},{20,12},{24,0},{28,4},{1,25},{... | collective-permute-start | bytes 18440 | tf_op jit(solution)/shard_map/ppermute | solution.py:23
  42.5 5.6 %collective-permute-start.11 = (f32[2,1,2048]{2,1,0:T(1,128)S(1)}, f32[2,1,2048]{2,1,0:T(1,128)S(1)}, u32[]{:S(2)}, u32[]{:S(2)}) collective-permute-start(f32[2,1,2048]{2,1,0:T(1,128)S(1)} %row_totals.4), channel_id=1, source_target_pairs={{0,3},{1,2},{2,1},{3,0},{4,7},{5,6},{6,5},{7,4},{8,11},{9,10},{10,... | collective-permute-start | bytes 49160 | tf_op jit(solution)/shard_map/ppermute | solution.py:23
  44.0 4.7 %collective-permute-start.12 = (f32[2,1,2048]{2,1,0:T(1,128)S(1)}, f32[2,1,2048]{2,1,0:T(1,128)S(1)}, u32[]{:S(2)}, u32[]{:S(2)}) collective-permute-start(f32[2,1,2048]{2,1,0:T(1,128)S(1)} %row_totals.4), channel_id=1, source_target_pairs={{0,2},{1,3},{2,0},{3,1},{4,6},{5,7},{6,4},{7,5},{8,10},{9,11},{10,... | collective-permute-start | bytes 49160 | tf_op jit(solution)/shard_map/ppermute | solution.py:23
  44.6 4.2 %collective-permute-start.13 = (f32[2,1,2048]{2,1,0:T(1,128)S(1)}, f32[2,1,2048]{2,1,0:T(1,128)S(1)}, u32[]{:S(2)}, u32[]{:S(2)}) collective-permute-start(f32[2,1,2048]{2,1,0:T(1,128)S(1)} %row_totals.4), channel_id=1, source_target_pairs={{0,1},{1,0},{2,3},{3,2},{4,5},{5,4},{6,7},{7,6},{8,9},{9,8},{10,11... | collective-permute-start | bytes 49160 | tf_op jit(solution)/shard_map/ppermute | solution.py:23
  51.5 4.6 %collective-permute-start.15 = (f32[2,1,768]{2,1,0:T(1,128)S(1)}, f32[2,1,768]{2,1,0:T(1,128)S(1)}, u32[]{:S(2)}, u32[]{:S(2)}) collective-permute-start(f32[2,1,768]{2,1,0:T(1,128)S(1)} %add.160), channel_id=1, source_target_pairs={{0,24},{4,28},{8,16},{12,20},{16,8},{20,12},{24,0},{28,4},{1,25},{... | collective-permute-start | bytes 18440 | tf_op jit(solution)/shard_map/ppermute | solution.py:23
  59.0 5.6 %collective-permute-start.18 = (f32[2,1,2048]{2,1,0:T(1,128)S(1)}, f32[2,1,2048]{2,1,0:T(1,128)S(1)}, u32[]{:S(2)}, u32[]{:S(2)}) collective-permute-start(f32[2,1,2048]{2,1,0:T(1,128)S(1)} %row_totals.5), channel_id=1, source_target_pairs={{0,3},{1,2},{2,1},{3,0},{4,7},{5,6},{6,5},{7,4},{8,11},{9,10},{10,... | collective-permute-start | bytes 49160 | tf_op jit(solution)/shard_map/ppermute | solution.py:23
  61.5 4.7 %collective-permute-start.19 = (f32[2,1,2048]{2,1,0:T(1,128)S(1)}, f32[2,1,2048]{2,1,0:T(1,128)S(1)}, u32[]{:S(2)}, u32[]{:S(2)}) collective-permute-start(f32[2,1,2048]{2,1,0:T(1,128)S(1)} %row_totals.5), channel_id=1, source_target_pairs={{0,2},{1,3},{2,0},{3,1},{4,6},{5,7},{6,4},{7,5},{8,10},{9,11},{10,... | collective-permute-start | bytes 49160 | tf_op jit(solution)/shard_map/ppermute | solution.py:23
  78.8 12.4 %collective-permute-start.21 = (f32[4,96,256]{2,1,0:T(8,128)S(1)}, f32[4,96,256]{2,1,0:T(8,128)S(1)}, u32[]{:S(2)}, u32[]{:S(2)}) collective-permute-start(f32[4,96,256]{2,1,0:T(8,128)S(1)} %dynamic-slice_bitcast_fusion), channel_id=1, source_target_pairs={{0,4},{4,0},{8,12},{12,8},{16,20},{20,16},{24,28},{28,24},{1,5},{5... | collective-permute-start | bytes 1179656 | tf_op jit(solution)/shard_map/ppermute | solution.py:23
  79.3 5.5 %collective-permute-start.26 = (f32[1,72,256]{2,1,0:T(8,128)S(1)}, f32[1,72,256]{2,1,0:T(8,128)S(1)}, u32[]{:S(2)}, u32[]{:S(2)}) collective-permute-start(f32[1,72,256]{2,1,0:T(8,128)S(1)} %get-tuple-element.28), channel_id=1, source_target_pairs={{0,24},{4,28},{8,16},{12,20},{16,8},{20,12},{24,0},{28,4},{1,25},{... | collective-permute-start | bytes 221192 | tf_op jit(solution)/shard_map/ppermute | solution.py:23
  80.8 5.4 %collective-permute-start.27 = (f32[1,72,256]{2,1,0:T(8,128)S(1)}, f32[1,72,256]{2,1,0:T(8,128)S(1)}, u32[]{:S(2)}, u32[]{:S(2)}) collective-permute-start(f32[1,72,256]{2,1,0:T(8,128)S(1)} %get-tuple-element.30), channel_id=1, source_target_pairs={{0,16},{4,20},{8,24},{12,28},{16,0},{20,4},{24,8},{28,12},{1,17},{... | collective-permute-start | bytes 221192 | tf_op jit(solution)/shard_map/ppermute | solution.py:23
  82.4 4.4 %collective-permute-start.28 = (f32[1,72,256]{2,1,0:T(8,128)S(1)}, f32[1,72,256]{2,1,0:T(8,128)S(1)}, u32[]{:S(2)}, u32[]{:S(2)}) collective-permute-start(f32[1,72,256]{2,1,0:T(8,128)S(1)} %get-tuple-element.29), channel_id=1, source_target_pairs={{0,8},{4,12},{8,0},{12,4},{16,24},{20,28},{24,16},{28,20},{1,9},{5... | collective-permute-start | bytes 221192 | tf_op jit(solution)/shard_map/ppermute | solution.py:23
  86.7 7.1 %collective-permute-start.29 = (f32[72,256]{1,0:T(8,128)S(1)}, f32[72,256]{1,0:T(8,128)S(1)}, u32[]{:S(2)}, u32[]{:S(2)}) collective-permute-start(f32[72,256]{1,0:T(8,128)S(1)} %add_bitcast_fusion), channel_id=1, source_target_pairs={{0,3},{1,2},{2,1},{3,0},{4,7},{5,6},{6,5},{7,4},{8,11},{9,10},{10,... | collective-permute-start | bytes 221192 | tf_op jit(solution)/shard_map/ppermute | solution.py:23
  88.2 8.0 %collective-permute-start.30 = (f32[72,256]{1,0:T(8,128)S(1)}, f32[72,256]{1,0:T(8,128)S(1)}, u32[]{:S(2)}, u32[]{:S(2)}) collective-permute-start(f32[72,256]{1,0:T(8,128)S(1)} %add_bitcast_fusion), channel_id=1, source_target_pairs={{0,2},{1,3},{2,0},{3,1},{4,6},{5,7},{6,4},{7,5},{8,10},{9,11},{10,... | collective-permute-start | bytes 221192 | tf_op jit(solution)/shard_map/ppermute | solution.py:23
  89.2 7.1 %collective-permute-start.31 = (f32[72,256]{1,0:T(8,128)S(1)}, f32[72,256]{1,0:T(8,128)S(1)}, u32[]{:S(2)}, u32[]{:S(2)}) collective-permute-start(f32[72,256]{1,0:T(8,128)S(1)} %add_bitcast_fusion), channel_id=1, source_target_pairs={{0,1},{1,0},{2,3},{3,2},{4,5},{5,4},{6,7},{7,6},{8,9},{9,8},{10,11... | collective-permute-start | bytes 221192 | tf_op jit(solution)/shard_map/ppermute | solution.py:23
  91.3 5.9 %collective-permute-start.22 = (f32[1,96,256]{2,1,0:T(8,128)S(1)}, f32[1,96,256]{2,1,0:T(8,128)S(1)}, u32[]{:S(2)}, u32[]{:S(2)}) collective-permute-start(f32[1,96,256]{2,1,0:T(8,128)S(1)} %get-tuple-element.25), channel_id=1, source_target_pairs={{0,24},{4,28},{8,16},{12,20},{16,8},{20,12},{24,0},{28,4},{1,25},{... | collective-permute-start | bytes 294920 | tf_op jit(solution)/shard_map/ppermute | solution.py:23
  92.4 5.6 %collective-permute-start.23 = (f32[1,96,256]{2,1,0:T(8,128)S(1)}, f32[1,96,256]{2,1,0:T(8,128)S(1)}, u32[]{:S(2)}, u32[]{:S(2)}) collective-permute-start(f32[1,96,256]{2,1,0:T(8,128)S(1)} %get-tuple-element.27), channel_id=1, source_target_pairs={{0,16},{4,20},{8,24},{12,28},{16,0},{20,4},{24,8},{28,12},{1,17},{... | collective-permute-start | bytes 294920 | tf_op jit(solution)/shard_map/ppermute | solution.py:23
  93.8 4.6 %collective-permute-start.24 = (f32[1,96,256]{2,1,0:T(8,128)S(1)}, f32[1,96,256]{2,1,0:T(8,128)S(1)}, u32[]{:S(2)}, u32[]{:S(2)}) collective-permute-start(f32[1,96,256]{2,1,0:T(8,128)S(1)} %get-tuple-element.26), channel_id=1, source_target_pairs={{0,8},{4,12},{8,0},{12,4},{16,24},{20,28},{24,16},{28,20},{1,9},{5... | collective-permute-start | bytes 294920 | tf_op jit(solution)/shard_map/ppermute | solution.py:23
  98.7 6.9 %collective-permute-start.32 = (f32[1,160,256]{2,1,0:T(8,128)S(1)}, f32[1,160,256]{2,1,0:T(8,128)S(1)}, u32[]{:S(2)}, u32[]{:S(2)}) collective-permute-start(f32[1,160,256]{2,1,0:T(8,128)S(1)} %fusion.5), channel_id=1, source_target_pairs={{0,24},{4,28},{8,16},{12,20},{16,8},{20,12},{24,0},{28,4},{1,25},{... | collective-permute-start | bytes 491528 | tf_op jit(solution)/shard_map/ppermute | solution.py:23
  99.8 7.4 %collective-permute-start.33 = (f32[1,160,256]{2,1,0:T(8,128)S(1)}, f32[1,160,256]{2,1,0:T(8,128)S(1)}, u32[]{:S(2)}, u32[]{:S(2)}) collective-permute-start(f32[1,160,256]{2,1,0:T(8,128)S(1)} %fusion.5), channel_id=1, source_target_pairs={{0,16},{4,20},{8,24},{12,28},{16,0},{20,4},{24,8},{28,12},{1,17},{... | collective-permute-start | bytes 491528 | tf_op jit(solution)/shard_map/ppermute | solution.py:23
  101.3 5.9 %collective-permute-start.34 = (f32[1,160,256]{2,1,0:T(8,128)S(1)}, f32[1,160,256]{2,1,0:T(8,128)S(1)}, u32[]{:S(2)}, u32[]{:S(2)}) collective-permute-start(f32[1,160,256]{2,1,0:T(8,128)S(1)} %fusion.5), channel_id=1, source_target_pairs={{0,8},{4,12},{8,0},{12,4},{16,24},{20,28},{24,16},{28,20},{1,9},{5... | collective-permute-start | bytes 491528 | tf_op jit(solution)/shard_map/ppermute | solution.py:23
  (13 other events, 34.6 us)

commit v5 on v4

--- a/solution.py
+++ b/solution.py
@@ -15,8 +15,9 @@
 LOG2_E = 1.4426950408889634
 LANES = 128
 CHUNK = 256
-FINAL_TYPE = jnp.float32
-VMEM_LIMIT = 20 * 1024 * 1024
+WIDE = 1024
+FINAL_TYPE = jnp.bfloat16
+VMEM_LIMIT = 22 * 1024 * 1024
 
 
 def swap(values, axis, size, offset):
@@ -41,22 +42,23 @@
     return values
 
 
-def scatter_sum(values, axis, first):
+def scatter_sums(arrays, axis, groups):
     size = lax.axis_size(axis)
     me = lax.axis_index(axis)
-    block = values.shape[1:]
-    values = values[None]
-    for low, width in stages(size, first):
+    for low, width in groups:
         ways = 1 << width
-        rest = values.shape[1] // ways
-        values = values.reshape((rest, ways) + block)
         mine = (me >> low) & (ways - 1)
-        own = lax.dynamic_index_in_dim(values, mine, 1, keepdims=False)
-        for k in reversed(range(1, ways)):
-            out = lax.dynamic_index_in_dim(values, mine ^ k, 1, keepdims=False)
-            own = own + swap(out, axis, size, k << low)
-        values = own[None]
-    return values.reshape(block)
+        split = [values.reshape((values.shape[0] // ways, ways) + values.shape[1:]) for values in arrays]
+        pick = lambda values, at: lax.dynamic_index_in_dim(values, at, 1, keepdims=False)
+        outs = [[pick(values, mine ^ k) for k in reversed(range(1, ways))] for values in split]
+        outs = lax.optimization_barrier(outs)
+        arrays = []
+        for values, sent in zip(split, outs):
+            own = pick(values, mine)
+            for k, out in zip(reversed(range(1, ways)), sent):
+                own = own + swap(out, axis, size, k << low)
+            arrays.append(own)
+    return arrays
 
 
 def gather_blocks(values, axis, first):
@@ -64,7 +66,7 @@
     me = lax.axis_index(axis)
     block = values.shape
     values = values[None]
-    for low, width in reversed(stages(size, first)):
+    for low, width in reversed(stages(size, first)[1:]):
         ways = 1 << width
         mine = (me >> low) & (ways - 1)
         parts = {k: swap(values, axis, size, k << low) if k else values for k in reversed(range(ways))}
@@ -132,20 +134,20 @@
 
 
 def first_kernel(
-    valid, width, feats_ref, proj_ref, proto_ref, codes_ref, col_ref, denom_ref, proto_half_ref,
-    turned_ref, split_ref, raw_ref, acc_ref, unit_ref, in_ref, out_ref, raw_out_ref, proto_in_ref, in_sems,
+    valid, width, wide, feats_ref, proj_ref, proto_ref, codes_ref, col_ref, denom_ref, proto_half_ref,
+    turned_ref, split_ref, raw_ref, acc_ref, unit_ref, in_ref, out_ref, raw_out_ref, proto_in_ref, proj_in_ref, proj_turned_ref, half_ref, in_sems,
     out_sems, raw_sems, proto_sems,
 ):
     count = denom_ref.shape[-1] // width
     spans = [pl.ds(at * width, width) for at in range(count)]
-    proto_load = pltpu.make_async_copy(proto_ref, proto_in_ref, proto_sems.at[0])
-    proto_load.start()
+    proj_load = pltpu.make_async_copy(proj_ref, proj_in_ref, proto_sems.at[0])
+    proto_load = pltpu.make_async_copy(proto_ref, proto_in_ref, proto_sems.at[1])
     loads = copies(lambda at: feats_ref.at[spans[at]], lambda at: in_ref.at[spans[at]], in_sems, count)
     stores = copies(lambda at: out_ref.at[:, spans[at]], lambda at: split_ref.at[:, spans[at]], out_sems, count)
     raw_stores = copies(
         lambda at: raw_out_ref.at[:, :, spans[at]], lambda at: raw_ref.at[:, :, spans[at]], raw_sems, count
     )
-    for load in loads:
+    for load in [proto_load, proj_load] + loads:
         load.start()
 
     edge = valid // 8 * 8
@@ -155,7 +157,8 @@
     unit, _ = unit_rows(unit_ref[...])
     proto_half_ref[...] = unit.astype(jnp.bfloat16)
     turned_ref[...] = jnp.transpose(unit).astype(jnp.bfloat16)
-    acc_ref[...] = jnp.zeros_like(acc_ref)
+    proj_load.wait()
+    proj_turned_ref[...] = jnp.transpose(proj_in_ref[...].astype(jnp.float32)).astype(jnp.bfloat16)
 
     for at in range(count):
         lanes = spans[at]
@@ -163,23 +166,30 @@
         out_ref[:, lanes] = jnp.transpose(in_ref[lanes], (1, 0, 2))
         stores[at].start()
         for view in range(2):
-            raw = product(proj_ref[...], out_ref[view, lanes], NT)
+            raw = product(proj_turned_ref[...], out_ref[view, lanes], NT)
             raw_out_ref[view, :, lanes] = raw
             unit, _ = unit_columns(raw)
-            half = unit.astype(jnp.bfloat16)
-            denom = jnp.zeros((8, width), jnp.float32)
+            half_ref[view, :, lanes] = unit.astype(jnp.bfloat16)
+        raw_stores[at].start()
+
+    for view in range(2):
+        for low in range(0, half_ref.shape[-1], wide):
+            lanes = slice(low, low + wide)
+            half = half_ref[view, :, lanes]
+            denom = jnp.zeros((8, wide), jnp.float32)
             for start in range(0, proto_half_ref.shape[0], CHUNK):
-                logits = product(proto_half_ref[start : start + CHUNK], half, NN)
+                part = slice(start, start + CHUNK)
+                logits = product(proto_half_ref[part], half, NN)
                 soft = jnp.exp2(logits * (LOG2_E / SOFTMAX_TEMPER))
                 if start + CHUNK > edge:
                     place = lax.broadcasted_iota(jnp.int32, soft.shape, 0) + start
                     soft = jnp.where(place < valid, soft, 0.0)
                 code = soft * soft
-                codes_ref[view, start : start + CHUNK, lanes] = code
-                denom = denom + jnp.sum(soft.reshape(-1, 8, width), axis=0)
-                acc_ref[view, start : start + CHUNK] += lane_sums(code)
+                codes_ref[view, part, lanes] = code
+                denom = denom + jnp.sum(soft.reshape(-1, 8, wide), axis=0)
+                total = lane_sums(code)
+                acc_ref[view, part] = total if low == 0 else acc_ref[view, part] + total
             denom_ref[view, :, lanes] = jnp.sum(denom, axis=0, keepdims=True)
-        raw_stores[at].start()
 
     for view in range(2):
         col_ref[view] = as_row(acc_ref[view])
@@ -217,7 +227,7 @@
 
 def grad_kernel(
     valid, width, factor, feats_ref, raw_ref, proto_ref, turned_ref, denom_ref, row_ref, col_ref,
-    proto_out, proj_out, loss_ref, scale_ref, grad_ref, turn_ref, in_ref, raw_in_ref, in_sems, raw_sems,
+    out_ref, scale_ref, grad_ref, turn_ref, proto_sum_ref, in_ref, raw_in_ref, in_sems, raw_sems,
 ):
     count = row_ref.shape[-1] // width
     spans = [pl.ds(at * width, width) for at in range(count)]
@@ -258,19 +268,35 @@
         feats = jnp.concatenate([in_ref[view, lanes] for view in range(2)], axis=0)
         proj_part = product(grad_raw, feats, NN)
         if at == 0:
-            proto_out[...] = proto_part
+            proto_sum_ref[...] = proto_part
             turn_ref[...] = proj_part
         else:
-            proto_out[...] += proto_part
+            proto_sum_ref[...] += proto_part
             turn_ref[...] += proj_part
 
-    proj_out[...] = jnp.transpose(turn_ref[...])
     logs = jnp.log(denom_ref[0]) + jnp.log(denom_ref[1])
     loss = jnp.sum(loss, axis=0, keepdims=True) * (1.0 / (SOFTMAX_TEMPER * factor))
-    loss_ref[...] = jnp.broadcast_to(
-        jnp.sum(loss, axis=1, keepdims=True) - jnp.sum(logs, axis=1, keepdims=True) * (1.0 / lax.axis_size("mp")),
-        loss_ref.shape,
-    )
+    loss = jnp.sum(loss, axis=1, keepdims=True) - jnp.sum(logs, axis=1, keepdims=True) * (1.0 / lax.axis_size("mp"))
+    proj = jnp.transpose(turn_ref[...])
+    shards = out_ref.shape[0]
+    share, proj_share = proto_sum_ref.shape[0] // shards, proj.shape[0] // shards
+    for at in range(shards):
+        out_ref[at, :share] = proto_sum_ref[at * share : (at + 1) * share]
+        out_ref[at, share : share + proj_share] = proj[at * proj_share : (at + 1) * proj_share]
+        out_ref[at, share + proj_share :] = jnp.broadcast_to(loss, (8, out_ref.shape[-1]))
+
+
+def assemble_kernel(share, side_ref, own_ref, other_ref, proto_out, proj_out):
+    first = side_ref[0] == 0
+    pairs, size, _ = own_ref.shape
+    for pair in range(pairs):
+        own, other = own_ref[pair].astype(jnp.float32), other_ref[pair].astype(jnp.float32)
+        for core, block in enumerate([jnp.where(first, own, other), jnp.where(first, other, own)]):
+            for out, part in ((proto_out, block[:share]), (proj_out, block[share:])):
+                at = (2 * pair + core) * part.shape[0]
+                rows = min(part.shape[0], out.shape[0] - at)
+                if rows > 0:
+                    out[at : at + rows] = part[:rows]
 
 
 IN_VMEM = pl.BlockSpec(memory_space=pltpu.VMEM)
@@ -279,7 +305,7 @@
 
 def call(kernel, name, out_shapes, scratch, work, *args, far_in=(), far_out=()):
     outs = [
-        pltpu.HBM(shape, dtype) if at in far_out else jax.ShapeDtypeStruct(shape, dtype)
+        (pltpu.HBM if at in far_out else pltpu.VMEM)(shape, dtype)
         for at, (shape, dtype) in enumerate(out_shapes)
     ]
     return pl.pallas_call(
@@ -302,17 +328,17 @@
     block = -(-valid // LANES) * LANES
     single, half_type = jnp.float32, jnp.bfloat16
 
-    tile = min(512, rows)
+    tile = min(1024, rows)
+    share = block // shards
     count = rows // tile
     row_shape, col_shape = ((2, 1, rows), single), ((2, 1, block), single)
     column = pltpu.VMEM((2, block, LANES), single)
     split = (2, rows, features.shape[-1])
     work = 4 * rows * block * width
-    turned_proj = projection.T
     sems = pltpu.SemaphoreType.DMA((count,))
     far = lambda array: pltpu.with_memory_space_constraint(array, pltpu.HBM)
     codes, col_part, soft_part, proto_half, turned, feats, raw = call(
-        functools.partial(first_kernel, valid, tile), "first_totals",
+        functools.partial(first_kernel, valid, tile, min(WIDE, rows)), "first_totals",
         [
             ((2, block, rows), single), col_shape, row_shape, ((block, width), half_type),
             ((width, block), half_type), (split, half_type), ((2, width, rows), single),
@@ -320,9 +346,11 @@
         [
             column, pltpu.VMEM((block, width), single), pltpu.VMEM(features.shape, half_type),
             pltpu.VMEM(split, half_type), pltpu.VMEM((2, width, rows), single),
-            pltpu.VMEM(prototypes.shape, single), sems, sems, sems, pltpu.SemaphoreType.DMA((1,)),
+            pltpu.VMEM(prototypes.shape, single), pltpu.VMEM(projection.shape, half_type),
+            pltpu.VMEM(projection.shape[::-1], half_type), pltpu.VMEM((2, width, rows), half_type),
+            sems, sems, sems, pltpu.SemaphoreType.DMA((2,)),
         ],
-        work, far(features), turned_proj, far(prototypes), far_in=(0, 2), far_out=(5, 6),
+        work, far(features), far(projection), far(prototypes), far_in=(0, 1, 2), far_out=(5, 6),
     )
     row_call = functools.partial(
         call, functools.partial(row_kernel, valid, min(512, rows)), "row_totals", [row_shape], [column], work, codes
@@ -338,22 +366,20 @@
         col_sums = sum_over(col_call(row_sums)[0], "dp", 1)
         row_sums = sum_over(row_call(col_sums)[0], "mp", 2)
 
-    proto_part, proj_part, loss = call(
-        functools.partial(grad_kernel, valid, tile, factor), "gradients",
-        [((block, width), single), (projection.shape, single), ((8, width), single)],
+    parts = call(
+        functools.partial(grad_kernel, valid, 1024, factor), "gradients",
+        [((shards, share + projection.shape[0] // shards + 8, width), single)],
         [
             column, pltpu.VMEM((block, 2 * tile), half_type), pltpu.VMEM(projection.shape[::-1], single),
-            pltpu.VMEM(split, half_type), pltpu.VMEM((2, width, rows), single), sems, sems,
+            pltpu.VMEM((block, width), single), pltpu.VMEM(split, half_type), pltpu.VMEM((2, width, rows), single), sems, sems,
         ],
         3 * work, far(feats), far(raw), proto_half, turned, denoms, row_sums, col_sums, far_in=(0, 1),
-    )
-    loss_rows = jnp.broadcast_to(loss[None], (shards,) + loss.shape)
-    proj_part = jnp.concatenate([proj_part.reshape(shards, -1, width), loss_rows], axis=1)
-    proj_sum = sum_over(scatter_sum(proj_part, "dp", 1), "mp", 2)
+    )[0]
+    pair, *others = stages(shards, 1)
+    parts = scatter_sums([parts[:, share:], parts[:, :share]], "dp", [pair] + others)
+    proj_part, proto_grad = [values[0] for values in parts]
+    proj_sum = sum_over(proj_part, "mp", 2)
     loss_value = -proj_sum[-1, 0] / (2.0 * batch_row_count)
-
-    share = block // shards
-    proto_grad = scatter_sum(proto_part.reshape(shards, share, width), "dp", 1)
     mine = lax.dynamic_slice_in_dim(
         jnp.pad(prototypes, ((0, block - valid), (0, 0))), lax.axis_index("dp") * share, share, 0
     )
@@ -361,10 +387,17 @@
     along_proto = jnp.sum(proto_unit * proto_grad, axis=-1, keepdims=True)
     grad_share = (proto_grad - proto_unit * along_proto) * proto_inverse
 
-    both = jnp.concatenate([grad_share, proj_sum[:-8]]).astype(FINAL_TYPE)
-    both = gather_blocks(both, "dp", 1).astype(single)
-    grad_protos = both[:, :share].reshape(block, width)[:valid]
-    return (grad_protos, both[:, share:].reshape(projection.shape), loss_value)
+    blocks = jnp.concatenate([grad_share, proj_sum[:-8]]).astype(FINAL_TYPE)
+    blocks = gather_blocks(blocks, "dp", 1)
+    other = swap(blocks, "dp", shards, 1)
+    side = (lax.axis_index("dp") & 1).astype(jnp.int32).reshape(1)
+    grad_protos, proj_grad = pl.pallas_call(
+        functools.partial(assemble_kernel, share), in_specs=[pl.BlockSpec(memory_space=pltpu.SMEM), IN_VMEM, IN_VMEM],
+        out_specs=[IN_VMEM, IN_VMEM],
+        out_shape=[pltpu.HBM(prototypes.shape, single), pltpu.HBM(projection.shape, single)],
+        compiler_params=pltpu.CompilerParams(vmem_limit_bytes=VMEM_LIMIT), name="assemble",
+    )(side, blocks, other)
+    return (grad_protos, proj_grad, loss_value)
 
 
 def solution(mesh):

time: 113 us -> 104 us (0.920)
  waiting for transfers between devices: 34.4 us -> 30.3 us
  local copies, waits for them, and re-layouts: 4.82 us -> 1.16 us
  Pallas kernels: 29.2 us -> 27.5 us
    ppermute x36, waiting for transfers between devices: 34.4 us -> 30.3 us  [swap(): return lax.ppermute(values, axis, [(i, i ^ offset) for i in range(size)])]
    pallas_call x7, Pallas kernels: 29.2 us -> 26.3 us  [call(): pl.pallas_call(kernel, in_specs=[IN_HBM if at in far_in else IN_VMEM for...]
    unnamed x3 -> x2, local copies, waits for them, and re-layouts: 2.06 us -> 0.34 us
    slice x4 -> x2, local copies, waits for them, and re-layouts: 1.81 us -> 0.11 us  [the longest x1 0.07 us: body(): parts[:, :share]]
    pallas_call x0 -> x1, Pallas kernels: none -> 1.16 us  [body(): pl.pallas_call(functools.partial(assemble_kernel, share), in_specs=[pl.Bl...]
  transfers between devices with their start and end apart: 36 -> 36, of which waited for: 32 -> 29; matrix products, arithmetic and copies ran while one was open for 1% -> 1% of each run, Pallas kernels for 0% -> 0%
where the time goes in v5:
time: 104 us
  starting transfers between devices  41.8 us (40%)
  waiting for transfers between devices  30.3 us (29%)
  Pallas kernels  27.5 us (26%)
  between operations  2.69 us (3%)
  local copies, waits for them, and re-layouts  1.16 us (1%)
    ppermute x36, starting transfers between devices, swap(): return lax.ppermute(values, axis, [(i, i ^ offset) for i in range(size)])  41.8 us
    ppermute x36, waiting for transfers between devices, swap(): return lax.ppermute(values, axis, [(i, i ^ offset) for i in range(size)])  30.3 us
    pallas_call x7, Pallas kernels, call(): pl.pallas_call(kernel, in_specs=[IN_HBM if at in far_in else IN_VMEM for...  26.3 us
  transfers between devices with their start and end apart: 36, of which 29 were waited for; matrix products, arithmetic and copies ran while one was open for 1% of the time, Pallas kernels for 0%

profile of v5, /device:TPU:0, one launch (start us, length us, event | category | flops | bytes accessed | tf_op | source)
XLA Modules:
  0.0 104.2 jit_solution(12840096752183672406)
XLA Ops:
  0.6 7.6 %first_totals.1 = (f32[2,768,2048]{2,1,0:T(8,128)S(1)}, f32[2,1,768]{2,1,0:T(1,128)S(1)}, f32[2,1,2048]{2,1,0:T(1,128)S(1)}, bf16[768,256]{1,0:T(8,128)(2,1)S(1)...) custom-call(bf16[2048,2,512]{2,1,0:T(2,128)(2,1)} %feats_ref.1, ...), custom_call_target="tpu_custom_call" | custom-call | flops 1610612736 | bytes 1048576 | tf_op jit(solution)/shard_map/first_totals/pallas_call | solution.py:311
  9.5 3.9 %collective-permute-start.1 = (f32[2,1,768]{2,1,0:T(1,128)S(1)}, f32[2,1,768]{2,1,0:T(1,128)S(1)}, u32[]{:S(2)}, u32[]{:S(2)}) collective-permute-start(f32[2,1,768]{2,1,0:T(1,128)S(1)} %add.144), channel_id=1, source_target_pairs={{0,24},{4,28},{8,16},{12,20},{16,8},{20,12},{24,0},{28,4},{1,25},{... | collective-permute-start | bytes 18440 | tf_op jit(solution)/shard_map/ppermute | solution.py:24
  15.0 2.0 %collective-permute-done.2 = f32[2,1,768]{2,1,0:T(1,128)S(1)} collective-permute-done((f32[2,1,768]{2,1,0:T(1,128)S(1)}, f32[2,1,768]{2,1,0:T(1,128)S(1)}, u32[]{:S(2)}, u32[]{:S(2)}) %collective-permute-start.2) | collective-permute-done | bytes 6176 | tf_op jit(solution)/shard_map/ppermute | solution.py:24
  17.6 1.6 %row_totals.3 = f32[2,1,2048]{2,1,0:T(1,128)S(1)} custom-call(f32[2,768,2048]{2,1,0:T(8,128)S(1)} %get-tuple-element.24.codes_ref, f32[2,1,768]{2,1,0:T(1,128)S(1)} %add_add_fusion.7.sums_ref), custom_call_target="tpu_custom_call" | custom-call | flops 1610612736 | bytes 1048576 | tf_op jit(solution)/shard_map/row_totals/pallas_call | solution.py:311
  19.2 3.7 %collective-permute-start.4 = (f32[4,1,2048]{2,1,0:T(1,128)S(1)}, f32[4,1,2048]{2,1,0:T(1,128)S(1)}, u32[]{:S(2)}, u32[]{:S(2)}) collective-permute-start(f32[4,1,2048]{2,1,0:T(1,128)S(1)} %pad_maximum_fusion.1), channel_id=1, source_target_pairs={{0,3},{1,2},{2,1},{3,0},{4,7},{5,6},{6,5},{7,4},{8,11},{9,10},{10,... | collective-permute-start | bytes 98312 | tf_op jit(solution)/shard_map/ppermute | solution.py:24
  25.1 2.6 %collective-permute-done.5 = f32[4,1,2048]{2,1,0:T(1,128)S(1)} collective-permute-done((f32[4,1,2048]{2,1,0:T(1,128)S(1)}, f32[4,1,2048]{2,1,0:T(1,128)S(1)}, u32[]{:S(2)}, u32[]{:S(2)}) %collective-permute-start.5) | collective-permute-done | bytes 32800 | tf_op jit(solution)/shard_map/ppermute | solution.py:24
  31.0 2.5 %collective-permute-start.8 = (f32[2,1,768]{2,1,0:T(1,128)S(1)}, f32[2,1,768]{2,1,0:T(1,128)S(1)}, u32[]{:S(2)}, u32[]{:S(2)}) collective-permute-start(f32[2,1,768]{2,1,0:T(1,128)S(1)} %add.151), channel_id=1, source_target_pairs={{0,24},{4,28},{8,16},{12,20},{16,8},{20,12},{24,0},{28,4},{1,25},{... | collective-permute-start | bytes 18440 | tf_op jit(solution)/shard_map/ppermute | solution.py:24
  35.6 1.6 %collective-permute-done.9 = f32[2,1,768]{2,1,0:T(1,128)S(1)} collective-permute-done((f32[2,1,768]{2,1,0:T(1,128)S(1)}, f32[2,1,768]{2,1,0:T(1,128)S(1)}, u32[]{:S(2)}, u32[]{:S(2)}) %collective-permute-start.9) | collective-permute-done | bytes 6176 | tf_op jit(solution)/shard_map/ppermute | solution.py:24
  37.1 1.6 %row_totals.4 = f32[2,1,2048]{2,1,0:T(1,128)S(1)} custom-call(f32[2,768,2048]{2,1,0:T(8,128)S(1)} %get-tuple-element.24.codes_ref, f32[2,1,768]{2,1,0:T(1,128)S(1)} %add_add_fusion.6.sums_ref), custom_call_target="tpu_custom_call" | custom-call | flops 1610612736 | bytes 1048576 | tf_op jit(solution)/shard_map/row_totals/pallas_call | solution.py:311
  38.7 1.5 %collective-permute-start.11 = (f32[2,1,2048]{2,1,0:T(1,128)S(1)}, f32[2,1,2048]{2,1,0:T(1,128)S(1)}, u32[]{:S(2)}, u32[]{:S(2)}) collective-permute-start(f32[2,1,2048]{2,1,0:T(1,128)S(1)} %row_totals.4), channel_id=1, source_target_pairs={{0,3},{1,2},{2,1},{3,0},{4,7},{5,6},{6,5},{7,4},{8,11},{9,10},{10,... | collective-permute-start | bytes 49160 | tf_op jit(solution)/shard_map/ppermute | solution.py:24
  40.9 2.3 %collective-permute-start.13 = (f32[2,1,2048]{2,1,0:T(1,128)S(1)}, f32[2,1,2048]{2,1,0:T(1,128)S(1)}, u32[]{:S(2)}, u32[]{:S(2)}) collective-permute-start(f32[2,1,2048]{2,1,0:T(1,128)S(1)} %row_totals.4), channel_id=1, source_target_pairs={{0,1},{1,0},{2,3},{3,2},{4,5},{5,4},{6,7},{7,6},{8,9},{9,8},{10,11... | collective-permute-start | bytes 49160 | tf_op jit(solution)/shard_map/ppermute | solution.py:24
  49.8 1.5 %collective-permute-start.17 = (f32[2,1,768]{2,1,0:T(1,128)S(1)}, f32[2,1,768]{2,1,0:T(1,128)S(1)}, u32[]{:S(2)}, u32[]{:S(2)}) collective-permute-start(f32[2,1,768]{2,1,0:T(1,128)S(1)} %add.158), channel_id=1, source_target_pairs={{0,8},{4,12},{8,0},{12,4},{16,24},{20,28},{24,16},{28,20},{1,9},{5... | collective-permute-start | bytes 18440 | tf_op jit(solution)/shard_map/ppermute | solution.py:24
  53.5 1.8 %row_totals.5 = f32[2,1,2048]{2,1,0:T(1,128)S(1)} custom-call(f32[2,768,2048]{2,1,0:T(8,128)S(1)} %get-tuple-element.24.codes_ref, f32[2,1,768]{2,1,0:T(1,128)S(1)} %add_add_fusion.5.sums_ref.col_ref), custom_call_target="tpu_custom_call" | custom-call | flops 1610612736 | bytes 1048576 | tf_op jit(solution)/shard_map/row_totals/pallas_call | solution.py:311
  55.2 2.5 %collective-permute-start.18 = (f32[2,1,2048]{2,1,0:T(1,128)S(1)}, f32[2,1,2048]{2,1,0:T(1,128)S(1)}, u32[]{:S(2)}, u32[]{:S(2)}) collective-permute-start(f32[2,1,2048]{2,1,0:T(1,128)S(1)} %row_totals.5), channel_id=1, source_target_pairs={{0,3},{1,2},{2,1},{3,0},{4,7},{5,6},{6,5},{7,4},{8,11},{9,10},{10,... | collective-permute-start | bytes 49160 | tf_op jit(solution)/shard_map/ppermute | solution.py:24
  60.8 1.5 %collective-permute-done.19 = f32[2,1,2048]{2,1,0:T(1,128)S(1)} collective-permute-done((f32[2,1,2048]{2,1,0:T(1,128)S(1)}, f32[2,1,2048]{2,1,0:T(1,128)S(1)}, u32[]{:S(2)}, u32[]{:S(2)}) %collective-permute-start.19) | collective-permute-done | bytes 16416 | tf_op jit(solution)/shard_map/ppermute | solution.py:24
  62.6 11.0 %gradients.1 = f32[8,168,256]{2,1,0:T(8,128)S(1)} custom-call(bf16[2,2048,512]{2,1,0:T(8,128)(2,1)} %get-tuple-element.20.feats_ref, f32[2,256,2048]{2,1,0:T(8,128)} %get-tuple-element.21.raw_ref, bf16[768,256]{1,0:T(8,128)(2,1)S(1)} %get-tuple-element.22.proto_ref, bf16[256,768]{1,0:T(8,128)(2,1)S(1)} %get-tuple-element.23.turned_ref, ...), custom_call_target="tpu_custom_call" | custom-call | flops 4831838208 | bytes 1048576 | tf_op jit(solution)/shard_map/gradients/pallas_call | solution.py:311
  76.1 1.5 %collective-permute-start.26 = (f32[1,72,256]{2,1,0:T(8,128)S(1)}, f32[1,72,256]{2,1,0:T(8,128)S(1)}, u32[]{:S(2)}, u32[]{:S(2)}) collective-permute-start(f32[1,72,256]{2,1,0:T(8,128)S(1)} %get-tuple-element.32), channel_id=1, source_target_pairs={{0,24},{4,28},{8,16},{12,20},{16,8},{20,12},{24,0},{28,4},{1,25},{... | collective-permute-start | bytes 221192 | tf_op jit(solution)/shard_map/ppermute | solution.py:24
  77.6 1.5 %collective-permute-start.27 = (f32[1,72,256]{2,1,0:T(8,128)S(1)}, f32[1,72,256]{2,1,0:T(8,128)S(1)}, u32[]{:S(2)}, u32[]{:S(2)}) collective-permute-start(f32[1,72,256]{2,1,0:T(8,128)S(1)} %get-tuple-element.33), channel_id=1, source_target_pairs={{0,16},{4,20},{8,24},{12,28},{16,0},{20,4},{24,8},{28,12},{1,17},{... | collective-permute-start | bytes 221192 | tf_op jit(solution)/shard_map/ppermute | solution.py:24
  81.1 1.5 %collective-permute-start.24 = (f32[1,96,256]{2,1,0:T(8,128)S(1)}, f32[1,96,256]{2,1,0:T(8,128)S(1)}, u32[]{:S(2)}, u32[]{:S(2)}) collective-permute-start(f32[1,96,256]{2,1,0:T(8,128)S(1)} %get-tuple-element.30), channel_id=1, source_target_pairs={{0,16},{4,20},{8,24},{12,28},{16,0},{20,4},{24,8},{28,12},{1,17},{... | collective-permute-start | bytes 294920 | tf_op jit(solution)/shard_map/ppermute | solution.py:24
  86.4 2.0 %collective-permute-start.31 = (f32[72,256]{1,0:T(8,128)S(1)}, f32[72,256]{1,0:T(8,128)S(1)}, u32[]{:S(2)}, u32[]{:S(2)}) collective-permute-start(f32[72,256]{1,0:T(8,128)S(1)} %add_bitcast_fusion), channel_id=1, source_target_pairs={{0,1},{1,0},{2,3},{3,2},{4,5},{5,4},{6,7},{7,6},{8,9},{9,8},{10,11... | collective-permute-start | bytes 221192 | tf_op jit(solution)/shard_map/ppermute | solution.py:24
  88.7 2.3 %collective-permute-done.29 = f32[72,256]{1,0:T(8,128)S(1)} collective-permute-done((f32[72,256]{1,0:T(8,128)S(1)}, f32[72,256]{1,0:T(8,128)S(1)}, u32[]{:S(2)}, u32[]{:S(2)}) %collective-permute-start.29) | collective-permute-done | bytes 73760 | tf_op jit(solution)/shard_map/ppermute | solution.py:24
  91.0 2.5 %collective-permute-done.30 = f32[72,256]{1,0:T(8,128)S(1)} collective-permute-done((f32[72,256]{1,0:T(8,128)S(1)}, f32[72,256]{1,0:T(8,128)S(1)}, u32[]{:S(2)}, u32[]{:S(2)}) %collective-permute-start.30) | collective-permute-done | bytes 73760 | tf_op jit(solution)/shard_map/ppermute | solution.py:24
  95.5 1.6 %collective-permute-start.34 = (bf16[1,160,256]{2,1,0:T(8,128)(2,1)S(1)}, bf16[1,160,256]{2,1,0:T(8,128)(2,1)S(1)}, u32[]{:S(2)}, u32[]{:S(2)}) collective-permute-start(bf16[1,160,256]{2,1,0:T(8,128)(2,1)S(1)} %pad_maximum_fusion), channel_id=1, source_target_pairs={{0,8},{4,12},{8,0},{12,4},{16,24},{20,28},{24,16},{28,20},{1,9},{5... | collective-permute-start | bytes 245768 | tf_op jit(solution)/shard_map/ppermute | solution.py:24
  97.1 2.7 %collective-permute-done.32 = bf16[1,160,256]{2,1,0:T(8,128)(2,1)S(1)} collective-permute-done((bf16[1,160,256]{2,1,0:T(8,128)(2,1)S(1)}, bf16[1,160,256]{2,1,0:T(8,128)(2,1)S(1)}, u32[]{:S(2)}, u32[]{:S(2)}) %collective-permute-start.32) | collective-permute-done | bytes 81952 | tf_op jit(solution)/shard_map/ppermute | solution.py:24
  (91 shorter events, 37.0 us)
Async XLA Ops:
  9.5 5.5 %collective-permute-start.1 = (f32[2,1,768]{2,1,0:T(1,128)S(1)}, f32[2,1,768]{2,1,0:T(1,128)S(1)}, u32[]{:S(2)}, u32[]{:S(2)}) collective-permute-start(f32[2,1,768]{2,1,0:T(1,128)S(1)} %add.144), channel_id=1, source_target_pairs={{0,24},{4,28},{8,16},{12,20},{16,8},{20,12},{24,0},{28,4},{1,25},{... | collective-permute-start | bytes 18440 | tf_op jit(solution)/shard_map/ppermute | solution.py:24
  19.2 5.9 %collective-permute-start.4 = (f32[4,1,2048]{2,1,0:T(1,128)S(1)}, f32[4,1,2048]{2,1,0:T(1,128)S(1)}, u32[]{:S(2)}, u32[]{:S(2)}) collective-permute-start(f32[4,1,2048]{2,1,0:T(1,128)S(1)} %pad_maximum_fusion.1), channel_id=1, source_target_pairs={{0,3},{1,2},{2,1},{3,0},{4,7},{5,6},{6,5},{7,4},{8,11},{9,10},{10,... | collective-permute-start | bytes 98312 | tf_op jit(solution)/shard_map/ppermute | solution.py:24
  22.9 4.8 %collective-permute-start.5 = (f32[4,1,2048]{2,1,0:T(1,128)S(1)}, f32[4,1,2048]{2,1,0:T(1,128)S(1)}, u32[]{:S(2)}, u32[]{:S(2)}) collective-permute-start(f32[4,1,2048]{2,1,0:T(1,128)S(1)} %pad_maximum_fusion.1), channel_id=1, source_target_pairs={{0,2},{1,3},{2,0},{3,1},{4,6},{5,7},{6,4},{7,5},{8,10},{9,11},{10,... | collective-permute-start | bytes 98312 | tf_op jit(solution)/shard_map/ppermute | solution.py:24
  22.9 4.8 %collective-permute-start.6 = (f32[4,1,2048]{2,1,0:T(1,128)S(1)}, f32[4,1,2048]{2,1,0:T(1,128)S(1)}, u32[]{:S(2)}, u32[]{:S(2)}) collective-permute-start(f32[4,1,2048]{2,1,0:T(1,128)S(1)} %pad_maximum_fusion.1), channel_id=1, source_target_pairs={{0,1},{1,0},{2,3},{3,2},{4,5},{5,4},{6,7},{7,6},{8,9},{9,8},{10,11... | collective-permute-start | bytes 98312 | tf_op jit(solution)/shard_map/ppermute | solution.py:24
  31.0 4.5 %collective-permute-start.8 = (f32[2,1,768]{2,1,0:T(1,128)S(1)}, f32[2,1,768]{2,1,0:T(1,128)S(1)}, u32[]{:S(2)}, u32[]{:S(2)}) collective-permute-start(f32[2,1,768]{2,1,0:T(1,128)S(1)} %add.151), channel_id=1, source_target_pairs={{0,24},{4,28},{8,16},{12,20},{16,8},{20,12},{24,0},{28,4},{1,25},{... | collective-permute-start | bytes 18440 | tf_op jit(solution)/shard_map/ppermute | solution.py:24
  38.7 5.6 %collective-permute-start.11 = (f32[2,1,2048]{2,1,0:T(1,128)S(1)}, f32[2,1,2048]{2,1,0:T(1,128)S(1)}, u32[]{:S(2)}, u32[]{:S(2)}) collective-permute-start(f32[2,1,2048]{2,1,0:T(1,128)S(1)} %row_totals.4), channel_id=1, source_target_pairs={{0,3},{1,2},{2,1},{3,0},{4,7},{5,6},{6,5},{7,4},{8,11},{9,10},{10,... | collective-permute-start | bytes 49160 | tf_op jit(solution)/shard_map/ppermute | solution.py:24
  40.2 4.7 %collective-permute-start.12 = (f32[2,1,2048]{2,1,0:T(1,128)S(1)}, f32[2,1,2048]{2,1,0:T(1,128)S(1)}, u32[]{:S(2)}, u32[]{:S(2)}) collective-permute-start(f32[2,1,2048]{2,1,0:T(1,128)S(1)} %row_totals.4), channel_id=1, source_target_pairs={{0,2},{1,3},{2,0},{3,1},{4,6},{5,7},{6,4},{7,5},{8,10},{9,11},{10,... | collective-permute-start | bytes 49160 | tf_op jit(solution)/shard_map/ppermute | solution.py:24
  40.9 4.2 %collective-permute-start.13 = (f32[2,1,2048]{2,1,0:T(1,128)S(1)}, f32[2,1,2048]{2,1,0:T(1,128)S(1)}, u32[]{:S(2)}, u32[]{:S(2)}) collective-permute-start(f32[2,1,2048]{2,1,0:T(1,128)S(1)} %row_totals.4), channel_id=1, source_target_pairs={{0,1},{1,0},{2,3},{3,2},{4,5},{5,4},{6,7},{7,6},{8,9},{9,8},{10,11... | collective-permute-start | bytes 49160 | tf_op jit(solution)/shard_map/ppermute | solution.py:24
  47.8 4.6 %collective-permute-start.15 = (f32[2,1,768]{2,1,0:T(1,128)S(1)}, f32[2,1,768]{2,1,0:T(1,128)S(1)}, u32[]{:S(2)}, u32[]{:S(2)}) collective-permute-start(f32[2,1,768]{2,1,0:T(1,128)S(1)} %add.158), channel_id=1, source_target_pairs={{0,24},{4,28},{8,16},{12,20},{16,8},{20,12},{24,0},{28,4},{1,25},{... | collective-permute-start | bytes 18440 | tf_op jit(solution)/shard_map/ppermute | solution.py:24
  55.2 5.6 %collective-permute-start.18 = (f32[2,1,2048]{2,1,0:T(1,128)S(1)}, f32[2,1,2048]{2,1,0:T(1,128)S(1)}, u32[]{:S(2)}, u32[]{:S(2)}) collective-permute-start(f32[2,1,2048]{2,1,0:T(1,128)S(1)} %row_totals.5), channel_id=1, source_target_pairs={{0,3},{1,2},{2,1},{3,0},{4,7},{5,6},{6,5},{7,4},{8,11},{9,10},{10,... | collective-permute-start | bytes 49160 | tf_op jit(solution)/shard_map/ppermute | solution.py:24
  57.7 4.7 %collective-permute-start.19 = (f32[2,1,2048]{2,1,0:T(1,128)S(1)}, f32[2,1,2048]{2,1,0:T(1,128)S(1)}, u32[]{:S(2)}, u32[]{:S(2)}) collective-permute-start(f32[2,1,2048]{2,1,0:T(1,128)S(1)} %row_totals.5), channel_id=1, source_target_pairs={{0,2},{1,3},{2,0},{3,1},{4,6},{5,7},{6,4},{7,5},{8,10},{9,11},{10,... | collective-permute-start | bytes 49160 | tf_op jit(solution)/shard_map/ppermute | solution.py:24
  58.6 3.9 %collective-permute-start.20 = (f32[2,1,2048]{2,1,0:T(1,128)S(1)}, f32[2,1,2048]{2,1,0:T(1,128)S(1)}, u32[]{:S(2)}, u32[]{:S(2)}) collective-permute-start(f32[2,1,2048]{2,1,0:T(1,128)S(1)} %row_totals.5), channel_id=1, source_target_pairs={{0,1},{1,0},{2,3},{3,2},{4,5},{5,4},{6,7},{7,6},{8,9},{9,8},{10,11... | collective-permute-start | bytes 49160 | tf_op jit(solution)/shard_map/ppermute | solution.py:24
  76.1 6.5 %collective-permute-start.26 = (f32[1,72,256]{2,1,0:T(8,128)S(1)}, f32[1,72,256]{2,1,0:T(8,128)S(1)}, u32[]{:S(2)}, u32[]{:S(2)}) collective-permute-start(f32[1,72,256]{2,1,0:T(8,128)S(1)} %get-tuple-element.32), channel_id=1, source_target_pairs={{0,24},{4,28},{8,16},{12,20},{16,8},{20,12},{24,0},{28,4},{1,25},{... | collective-permute-start | bytes 221192 | tf_op jit(solution)/shard_map/ppermute | solution.py:24
  77.6 6.2 %collective-permute-start.27 = (f32[1,72,256]{2,1,0:T(8,128)S(1)}, f32[1,72,256]{2,1,0:T(8,128)S(1)}, u32[]{:S(2)}, u32[]{:S(2)}) collective-permute-start(f32[1,72,256]{2,1,0:T(8,128)S(1)} %get-tuple-element.33), channel_id=1, source_target_pairs={{0,16},{4,20},{8,24},{12,28},{16,0},{20,4},{24,8},{28,12},{1,17},{... | collective-permute-start | bytes 221192 | tf_op jit(solution)/shard_map/ppermute | solution.py:24
  79.1 4.8 %collective-permute-start.28 = (f32[1,72,256]{2,1,0:T(8,128)S(1)}, f32[1,72,256]{2,1,0:T(8,128)S(1)}, u32[]{:S(2)}, u32[]{:S(2)}) collective-permute-start(f32[1,72,256]{2,1,0:T(8,128)S(1)} %get-tuple-element.34), channel_id=1, source_target_pairs={{0,8},{4,12},{8,0},{12,4},{16,24},{20,28},{24,16},{28,20},{1,9},{5... | collective-permute-start | bytes 221192 | tf_op jit(solution)/shard_map/ppermute | solution.py:24
  79.7 6.7 %collective-permute-start.23 = (f32[1,96,256]{2,1,0:T(8,128)S(1)}, f32[1,96,256]{2,1,0:T(8,128)S(1)}, u32[]{:S(2)}, u32[]{:S(2)}) collective-permute-start(f32[1,96,256]{2,1,0:T(8,128)S(1)} %get-tuple-element.29), channel_id=1, source_target_pairs={{0,24},{4,28},{8,16},{12,20},{16,8},{20,12},{24,0},{28,4},{1,25},{... | collective-permute-start | bytes 294920 | tf_op jit(solution)/shard_map/ppermute | solution.py:24
  81.1 7.3 %collective-permute-start.24 = (f32[1,96,256]{2,1,0:T(8,128)S(1)}, f32[1,96,256]{2,1,0:T(8,128)S(1)}, u32[]{:S(2)}, u32[]{:S(2)}) collective-permute-start(f32[1,96,256]{2,1,0:T(8,128)S(1)} %get-tuple-element.30), channel_id=1, source_target_pairs={{0,16},{4,20},{8,24},{12,28},{16,0},{20,4},{24,8},{28,12},{1,17},{... | collective-permute-start | bytes 294920 | tf_op jit(solution)/shard_map/ppermute | solution.py:24
  82.6 5.8 %collective-permute-start.25 = (f32[1,96,256]{2,1,0:T(8,128)S(1)}, f32[1,96,256]{2,1,0:T(8,128)S(1)}, u32[]{:S(2)}, u32[]{:S(2)}) collective-permute-start(f32[1,96,256]{2,1,0:T(8,128)S(1)} %get-tuple-element.31), channel_id=1, source_target_pairs={{0,8},{4,12},{8,0},{12,4},{16,24},{20,28},{24,16},{28,20},{1,9},{5... | collective-permute-start | bytes 294920 | tf_op jit(solution)/shard_map/ppermute | solution.py:24
  84.0 7.0 %collective-permute-start.29 = (f32[72,256]{1,0:T(8,128)S(1)}, f32[72,256]{1,0:T(8,128)S(1)}, u32[]{:S(2)}, u32[]{:S(2)}) collective-permute-start(f32[72,256]{1,0:T(8,128)S(1)} %add_bitcast_fusion), channel_id=1, source_target_pairs={{0,3},{1,2},{2,1},{3,0},{4,7},{5,6},{6,5},{7,4},{8,11},{9,10},{10,... | collective-permute-start | bytes 221192 | tf_op jit(solution)/shard_map/ppermute | solution.py:24
  85.5 8.0 %collective-permute-start.30 = (f32[72,256]{1,0:T(8,128)S(1)}, f32[72,256]{1,0:T(8,128)S(1)}, u32[]{:S(2)}, u32[]{:S(2)}) collective-permute-start(f32[72,256]{1,0:T(8,128)S(1)} %add_bitcast_fusion), channel_id=1, source_target_pairs={{0,2},{1,3},{2,0},{3,1},{4,6},{5,7},{6,4},{7,5},{8,10},{9,11},{10,... | collective-permute-start | bytes 221192 | tf_op jit(solution)/shard_map/ppermute | solution.py:24
  86.4 7.1 %collective-permute-start.31 = (f32[72,256]{1,0:T(8,128)S(1)}, f32[72,256]{1,0:T(8,128)S(1)}, u32[]{:S(2)}, u32[]{:S(2)}) collective-permute-start(f32[72,256]{1,0:T(8,128)S(1)} %add_bitcast_fusion), channel_id=1, source_target_pairs={{0,1},{1,0},{2,3},{3,2},{4,5},{5,4},{6,7},{7,6},{8,9},{9,8},{10,11... | collective-permute-start | bytes 221192 | tf_op jit(solution)/shard_map/ppermute | solution.py:24
  93.5 6.2 %collective-permute-start.32 = (bf16[1,160,256]{2,1,0:T(8,128)(2,1)S(1)}, bf16[1,160,256]{2,1,0:T(8,128)(2,1)S(1)}, u32[]{:S(2)}, u32[]{:S(2)}) collective-permute-start(bf16[1,160,256]{2,1,0:T(8,128)(2,1)S(1)} %pad_maximum_fusion), channel_id=1, source_target_pairs={{0,24},{4,28},{8,16},{12,20},{16,8},{20,12},{24,0},{28,4},{1,25},{... | collective-permute-start | bytes 245768 | tf_op jit(solution)/shard_map/ppermute | solution.py:24
  95.0 5.1 %collective-permute-start.33 = (bf16[1,160,256]{2,1,0:T(8,128)(2,1)S(1)}, bf16[1,160,256]{2,1,0:T(8,128)(2,1)S(1)}, u32[]{:S(2)}, u32[]{:S(2)}) collective-permute-start(bf16[1,160,256]{2,1,0:T(8,128)(2,1)S(1)} %pad_maximum_fusion), channel_id=1, source_target_pairs={{0,16},{4,20},{8,24},{12,28},{16,0},{20,4},{24,8},{28,12},{1,17},{... | collective-permute-start | bytes 245768 | tf_op jit(solution)/shard_map/ppermute | solution.py:24
  95.5 4.6 %collective-permute-start.34 = (bf16[1,160,256]{2,1,0:T(8,128)(2,1)S(1)}, bf16[1,160,256]{2,1,0:T(8,128)(2,1)S(1)}, u32[]{:S(2)}, u32[]{:S(2)}) collective-permute-start(bf16[1,160,256]{2,1,0:T(8,128)(2,1)S(1)} %pad_maximum_fusion), channel_id=1, source_target_pairs={{0,8},{4,12},{8,0},{12,4},{16,24},{20,28},{24,16},{28,20},{1,9},{5... | collective-permute-start | bytes 245768 | tf_op jit(solution)/shard_map/ppermute | solution.py:24
  (13 other events, 32.3 us)

commit v6 on v5

--- a/solution.py
+++ b/solution.py
@@ -96,10 +96,10 @@
 
 
 def lane_sums(values):
-    total = values[:, :LANES]
-    for start in range(LANES, values.shape[1], LANES):
-        total = total + values[:, start : start + LANES]
-    return total
+    parts = [values[:, start : start + LANES] for start in range(0, values.shape[1], LANES)]
+    while len(parts) > 1:
+        parts = [a + b for a, b in zip(parts[::2], parts[1::2])] + parts[len(parts) - len(parts) % 2 :]
+    return parts[0]
 
 
 def as_row(column):
@@ -208,20 +208,16 @@
             total = total + code * widen(scale_ref[view, start : start + 8], width)
         row_ref[view, :, lanes] = jnp.sum(total, axis=0, keepdims=True)
 
-    tiles(row_ref, width, step)
-
-
-def col_kernel(width, codes_ref, sums_ref, col_ref, acc_ref):
-    acc_ref[...] = jnp.zeros_like(acc_ref)
-
-    def step(view, lanes):
-        scale = jnp.broadcast_to(1.0 / sums_ref[view, :, lanes], (8, width))
+    for view in range(2):
+        for low in range(0, row_ref.shape[-1], width):
+            step(view, slice(low, low + width))
+
+
+def col_kernel(codes_ref, sums_ref, col_ref, acc_ref):
+    for view in range(2):
+        scale = jnp.broadcast_to(1.0 / sums_ref[view], (8, sums_ref.shape[-1]))
         for start in range(0, codes_ref.shape[1], 8):
-            code = codes_ref[view, start : start + 8, lanes]
-            acc_ref[view, start : start + 8] += lane_sums(code * scale)
-
-    tiles(sums_ref, width, step)
-    for view in range(2):
+            acc_ref[view, start : start + 8] = lane_sums(codes_ref[view, start : start + 8] * scale)
         col_ref[view] = as_row(acc_ref[view])
 
 
@@ -353,10 +349,10 @@
         work, far(features), far(projection), far(prototypes), far_in=(0, 1, 2), far_out=(5, 6),
     )
     row_call = functools.partial(
-        call, functools.partial(row_kernel, valid, min(512, rows)), "row_totals", [row_shape], [column], work, codes
+        call, functools.partial(row_kernel, valid, min(1024, rows)), "row_totals", [row_shape], [column], work, codes
     )
     col_call = functools.partial(
-        call, functools.partial(col_kernel, min(512, rows)), "column_totals", [col_shape], [column], work, codes
+        call, col_kernel, "column_totals", [col_shape], [column], work, codes
     )
 
     col_sums = sum_over(col_part, "dp", 1)
@@ -375,8 +371,7 @@
         ],
         3 * work, far(feats), far(raw), proto_half, turned, denoms, row_sums, col_sums, far_in=(0, 1),
     )[0]
-    pair, *others = stages(shards, 1)
-    parts = scatter_sums([parts[:, share:], parts[:, :share]], "dp", [pair] + others)
+    parts = scatter_sums([parts[:, share:], parts[:, :share]], "dp", stages(shards, 1))
     proj_part, proto_grad = [values[0] for values in parts]
     proj_sum = sum_over(proj_part, "mp", 2)
     loss_value = -proj_sum[-1, 0] / (2.0 * batch_row_count)

time: 104 us -> 102 us (0.981)
  Pallas kernels: 27.5 us -> 25 us
    pallas_call x7, Pallas kernels: 26.3 us -> 23.8 us  [call(): pl.pallas_call(kernel, in_specs=[IN_HBM if at in far_in else IN_VMEM for...]
where the time goes in v6:
time: 102 us
  starting transfers between devices  41.8 us (41%)
  waiting for transfers between devices  30.3 us (30%)
  Pallas kernels  25 us (25%)
  between operations  2.68 us (3%)
  local copies, waits for them, and re-layouts  1.16 us (1%)
    ppermute x36, starting transfers between devices, swap(): return lax.ppermute(values, axis, [(i, i ^ offset) for i in range(size)])  41.8 us
    ppermute x36, waiting for transfers between devices, swap(): return lax.ppermute(values, axis, [(i, i ^ offset) for i in range(size)])  30.3 us
    pallas_call x7, Pallas kernels, call(): pl.pallas_call(kernel, in_specs=[IN_HBM if at in far_in else IN_VMEM for...  23.8 us
  transfers between devices with their start and end apart: 36, of which 29 were waited for; matrix products, arithmetic and copies ran while one was open for 1% of the time, Pallas kernels for 0%

profile of v6, /device:TPU:0, one launch (start us, length us, event | category | flops | bytes accessed | tf_op | source)
XLA Modules:
  0.0 101.7 jit_solution(11054111368703241202)
XLA Ops:
  0.6 7.7 %first_totals.1 = (f32[2,768,2048]{2,1,0:T(8,128)S(1)}, f32[2,1,768]{2,1,0:T(1,128)S(1)}, f32[2,1,2048]{2,1,0:T(1,128)S(1)}, bf16[768,256]{1,0:T(8,128)(2,1)S(1)...) custom-call(bf16[2048,2,512]{2,1,0:T(2,128)(2,1)} %feats_ref.1, ...), custom_call_target="tpu_custom_call" | custom-call | flops 1610612736 | bytes 1048576 | tf_op jit(solution)/shard_map/first_totals/pallas_call | solution.py:307
  9.6 3.9 %collective-permute-start.1 = (f32[2,1,768]{2,1,0:T(1,128)S(1)}, f32[2,1,768]{2,1,0:T(1,128)S(1)}, u32[]{:S(2)}, u32[]{:S(2)}) collective-permute-start(f32[2,1,768]{2,1,0:T(1,128)S(1)} %add.144), channel_id=1, source_target_pairs={{0,24},{4,28},{8,16},{12,20},{16,8},{20,12},{24,0},{28,4},{1,25},{... | collective-permute-start | bytes 18440 | tf_op jit(solution)/shard_map/ppermute | solution.py:24
  15.1 2.0 %collective-permute-done.2 = f32[2,1,768]{2,1,0:T(1,128)S(1)} collective-permute-done((f32[2,1,768]{2,1,0:T(1,128)S(1)}, f32[2,1,768]{2,1,0:T(1,128)S(1)}, u32[]{:S(2)}, u32[]{:S(2)}) %collective-permute-start.2) | collective-permute-done | bytes 6176 | tf_op jit(solution)/shard_map/ppermute | solution.py:24
  18.8 3.7 %collective-permute-start.4 = (f32[4,1,2048]{2,1,0:T(1,128)S(1)}, f32[4,1,2048]{2,1,0:T(1,128)S(1)}, u32[]{:S(2)}, u32[]{:S(2)}) collective-permute-start(f32[4,1,2048]{2,1,0:T(1,128)S(1)} %pad_maximum_fusion.1), channel_id=1, source_target_pairs={{0,3},{1,2},{2,1},{3,0},{4,7},{5,6},{6,5},{7,4},{8,11},{9,10},{10,... | collective-permute-start | bytes 98312 | tf_op jit(solution)/shard_map/ppermute | solution.py:24
  24.6 2.6 %collective-permute-done.5 = f32[4,1,2048]{2,1,0:T(1,128)S(1)} collective-permute-done((f32[4,1,2048]{2,1,0:T(1,128)S(1)}, f32[4,1,2048]{2,1,0:T(1,128)S(1)}, u32[]{:S(2)}, u32[]{:S(2)}) %collective-permute-start.5) | collective-permute-done | bytes 32800 | tf_op jit(solution)/shard_map/ppermute | solution.py:24
  30.1 2.4 %collective-permute-start.8 = (f32[2,1,768]{2,1,0:T(1,128)S(1)}, f32[2,1,768]{2,1,0:T(1,128)S(1)}, u32[]{:S(2)}, u32[]{:S(2)}) collective-permute-start(f32[2,1,768]{2,1,0:T(1,128)S(1)} %add.151), channel_id=1, source_target_pairs={{0,24},{4,28},{8,16},{12,20},{16,8},{20,12},{24,0},{28,4},{1,25},{... | collective-permute-start | bytes 18440 | tf_op jit(solution)/shard_map/ppermute | solution.py:24
  33.2 1.4 %collective-permute-done.8 = f32[2,1,768]{2,1,0:T(1,128)S(1)} collective-permute-done((f32[2,1,768]{2,1,0:T(1,128)S(1)}, f32[2,1,768]{2,1,0:T(1,128)S(1)}, u32[]{:S(2)}, u32[]{:S(2)}) %collective-permute-start.8) | collective-permute-done | bytes 6176 | tf_op jit(solution)/shard_map/ppermute | solution.py:24
  34.6 1.5 %collective-permute-done.9 = f32[2,1,768]{2,1,0:T(1,128)S(1)} collective-permute-done((f32[2,1,768]{2,1,0:T(1,128)S(1)}, f32[2,1,768]{2,1,0:T(1,128)S(1)}, u32[]{:S(2)}, u32[]{:S(2)}) %collective-permute-start.9) | collective-permute-done | bytes 6176 | tf_op jit(solution)/shard_map/ppermute | solution.py:24
  37.3 1.5 %collective-permute-start.11 = (f32[2,1,2048]{2,1,0:T(1,128)S(1)}, f32[2,1,2048]{2,1,0:T(1,128)S(1)}, u32[]{:S(2)}, u32[]{:S(2)}) collective-permute-start(f32[2,1,2048]{2,1,0:T(1,128)S(1)} %row_totals.4), channel_id=1, source_target_pairs={{0,3},{1,2},{2,1},{3,0},{4,7},{5,6},{6,5},{7,4},{8,11},{9,10},{10,... | collective-permute-start | bytes 49160 | tf_op jit(solution)/shard_map/ppermute | solution.py:24
  39.4 2.3 %collective-permute-start.13 = (f32[2,1,2048]{2,1,0:T(1,128)S(1)}, f32[2,1,2048]{2,1,0:T(1,128)S(1)}, u32[]{:S(2)}, u32[]{:S(2)}) collective-permute-start(f32[2,1,2048]{2,1,0:T(1,128)S(1)} %row_totals.4), channel_id=1, source_target_pairs={{0,1},{1,0},{2,3},{3,2},{4,5},{5,4},{6,7},{7,6},{8,9},{9,8},{10,11... | collective-permute-start | bytes 49160 | tf_op jit(solution)/shard_map/ppermute | solution.py:24
  47.8 1.5 %collective-permute-start.17 = (f32[2,1,768]{2,1,0:T(1,128)S(1)}, f32[2,1,768]{2,1,0:T(1,128)S(1)}, u32[]{:S(2)}, u32[]{:S(2)}) collective-permute-start(f32[2,1,768]{2,1,0:T(1,128)S(1)} %add.158), channel_id=1, source_target_pairs={{0,8},{4,12},{8,0},{12,4},{16,24},{20,28},{24,16},{28,20},{1,9},{5... | collective-permute-start | bytes 18440 | tf_op jit(solution)/shard_map/ppermute | solution.py:24
  52.7 2.5 %collective-permute-start.18 = (f32[2,1,2048]{2,1,0:T(1,128)S(1)}, f32[2,1,2048]{2,1,0:T(1,128)S(1)}, u32[]{:S(2)}, u32[]{:S(2)}) collective-permute-start(f32[2,1,2048]{2,1,0:T(1,128)S(1)} %row_totals.5), channel_id=1, source_target_pairs={{0,3},{1,2},{2,1},{3,0},{4,7},{5,6},{6,5},{7,4},{8,11},{9,10},{10,... | collective-permute-start | bytes 49160 | tf_op jit(solution)/shard_map/ppermute | solution.py:24
  58.3 1.5 %collective-permute-done.19 = f32[2,1,2048]{2,1,0:T(1,128)S(1)} collective-permute-done((f32[2,1,2048]{2,1,0:T(1,128)S(1)}, f32[2,1,2048]{2,1,0:T(1,128)S(1)}, u32[]{:S(2)}, u32[]{:S(2)}) %collective-permute-start.19) | collective-permute-done | bytes 16416 | tf_op jit(solution)/shard_map/ppermute | solution.py:24
  60.1 11.0 %gradients.1 = f32[8,168,256]{2,1,0:T(8,128)S(1)} custom-call(bf16[2,2048,512]{2,1,0:T(8,128)(2,1)} %get-tuple-element.20.feats_ref, f32[2,256,2048]{2,1,0:T(8,128)} %get-tuple-element.21.raw_ref, bf16[768,256]{1,0:T(8,128)(2,1)S(1)} %get-tuple-element.22.proto_ref, bf16[256,768]{1,0:T(8,128)(2,1)S(1)} %get-tuple-element.23.turned_ref, ...), custom_call_target="tpu_custom_call" | custom-call | flops 4831838208 | bytes 1048576 | tf_op jit(solution)/shard_map/gradients/pallas_call | solution.py:307
  73.6 1.5 %collective-permute-start.26 = (f32[1,72,256]{2,1,0:T(8,128)S(1)}, f32[1,72,256]{2,1,0:T(8,128)S(1)}, u32[]{:S(2)}, u32[]{:S(2)}) collective-permute-start(f32[1,72,256]{2,1,0:T(8,128)S(1)} %get-tuple-element.32), channel_id=1, source_target_pairs={{0,24},{4,28},{8,16},{12,20},{16,8},{20,12},{24,0},{28,4},{1,25},{... | collective-permute-start | bytes 221192 | tf_op jit(solution)/shard_map/ppermute | solution.py:24
  75.1 1.5 %collective-permute-start.27 = (f32[1,72,256]{2,1,0:T(8,128)S(1)}, f32[1,72,256]{2,1,0:T(8,128)S(1)}, u32[]{:S(2)}, u32[]{:S(2)}) collective-permute-start(f32[1,72,256]{2,1,0:T(8,128)S(1)} %get-tuple-element.33), channel_id=1, source_target_pairs={{0,16},{4,20},{8,24},{12,28},{16,0},{20,4},{24,8},{28,12},{1,17},{... | collective-permute-start | bytes 221192 | tf_op jit(solution)/shard_map/ppermute | solution.py:24
  78.6 1.5 %collective-permute-start.24 = (f32[1,96,256]{2,1,0:T(8,128)S(1)}, f32[1,96,256]{2,1,0:T(8,128)S(1)}, u32[]{:S(2)}, u32[]{:S(2)}) collective-permute-start(f32[1,96,256]{2,1,0:T(8,128)S(1)} %get-tuple-element.30), channel_id=1, source_target_pairs={{0,16},{4,20},{8,24},{12,28},{16,0},{20,4},{24,8},{28,12},{1,17},{... | collective-permute-start | bytes 294920 | tf_op jit(solution)/shard_map/ppermute | solution.py:24
  81.5 1.5 %collective-permute-start.29 = (f32[72,256]{1,0:T(8,128)S(1)}, f32[72,256]{1,0:T(8,128)S(1)}, u32[]{:S(2)}, u32[]{:S(2)}) collective-permute-start(f32[72,256]{1,0:T(8,128)S(1)} %add_bitcast_fusion), channel_id=1, source_target_pairs={{0,3},{1,2},{2,1},{3,0},{4,7},{5,6},{6,5},{7,4},{8,11},{9,10},{10,... | collective-permute-start | bytes 221192 | tf_op jit(solution)/shard_map/ppermute | solution.py:24
  83.9 2.0 %collective-permute-start.31 = (f32[72,256]{1,0:T(8,128)S(1)}, f32[72,256]{1,0:T(8,128)S(1)}, u32[]{:S(2)}, u32[]{:S(2)}) collective-permute-start(f32[72,256]{1,0:T(8,128)S(1)} %add_bitcast_fusion), channel_id=1, source_target_pairs={{0,1},{1,0},{2,3},{3,2},{4,5},{5,4},{6,7},{7,6},{8,9},{9,8},{10,11... | collective-permute-start | bytes 221192 | tf_op jit(solution)/shard_map/ppermute | solution.py:24
  86.2 2.3 %collective-permute-done.29 = f32[72,256]{1,0:T(8,128)S(1)} collective-permute-done((f32[72,256]{1,0:T(8,128)S(1)}, f32[72,256]{1,0:T(8,128)S(1)}, u32[]{:S(2)}, u32[]{:S(2)}) %collective-permute-start.29) | collective-permute-done | bytes 73760 | tf_op jit(solution)/shard_map/ppermute | solution.py:24
  88.5 2.5 %collective-permute-done.30 = f32[72,256]{1,0:T(8,128)S(1)} collective-permute-done((f32[72,256]{1,0:T(8,128)S(1)}, f32[72,256]{1,0:T(8,128)S(1)}, u32[]{:S(2)}, u32[]{:S(2)}) %collective-permute-start.30) | collective-permute-done | bytes 73760 | tf_op jit(solution)/shard_map/ppermute | solution.py:24
  91.0 1.5 %collective-permute-start.32 = (bf16[1,160,256]{2,1,0:T(8,128)(2,1)S(1)}, bf16[1,160,256]{2,1,0:T(8,128)(2,1)S(1)}, u32[]{:S(2)}, u32[]{:S(2)}) collective-permute-start(bf16[1,160,256]{2,1,0:T(8,128)(2,1)S(1)} %pad_maximum_fusion), channel_id=1, source_target_pairs={{0,24},{4,28},{8,16},{12,20},{16,8},{20,12},{24,0},{28,4},{1,25},{... | collective-permute-start | bytes 245768 | tf_op jit(solution)/shard_map/ppermute | solution.py:24
  93.0 1.6 %collective-permute-start.34 = (bf16[1,160,256]{2,1,0:T(8,128)(2,1)S(1)}, bf16[1,160,256]{2,1,0:T(8,128)(2,1)S(1)}, u32[]{:S(2)}, u32[]{:S(2)}) collective-permute-start(bf16[1,160,256]{2,1,0:T(8,128)(2,1)S(1)} %pad_maximum_fusion), channel_id=1, source_target_pairs={{0,8},{4,12},{8,0},{12,4},{16,24},{20,28},{24,16},{28,20},{1,9},{5... | collective-permute-start | bytes 245768 | tf_op jit(solution)/shard_map/ppermute | solution.py:24
  94.6 2.7 %collective-permute-done.32 = bf16[1,160,256]{2,1,0:T(8,128)(2,1)S(1)} collective-permute-done((bf16[1,160,256]{2,1,0:T(8,128)(2,1)S(1)}, bf16[1,160,256]{2,1,0:T(8,128)(2,1)S(1)}, u32[]{:S(2)}, u32[]{:S(2)}) %collective-permute-start.32) | collective-permute-done | bytes 81952 | tf_op jit(solution)/shard_map/ppermute | solution.py:24
  (91 shorter events, 35.0 us)
Async XLA Ops:
  9.6 5.5 %collective-permute-start.1 = (f32[2,1,768]{2,1,0:T(1,128)S(1)}, f32[2,1,768]{2,1,0:T(1,128)S(1)}, u32[]{:S(2)}, u32[]{:S(2)}) collective-permute-start(f32[2,1,768]{2,1,0:T(1,128)S(1)} %add.144), channel_id=1, source_target_pairs={{0,24},{4,28},{8,16},{12,20},{16,8},{20,12},{24,0},{28,4},{1,25},{... | collective-permute-start | bytes 18440 | tf_op jit(solution)/shard_map/ppermute | solution.py:24
  18.8 5.9 %collective-permute-start.4 = (f32[4,1,2048]{2,1,0:T(1,128)S(1)}, f32[4,1,2048]{2,1,0:T(1,128)S(1)}, u32[]{:S(2)}, u32[]{:S(2)}) collective-permute-start(f32[4,1,2048]{2,1,0:T(1,128)S(1)} %pad_maximum_fusion.1), channel_id=1, source_target_pairs={{0,3},{1,2},{2,1},{3,0},{4,7},{5,6},{6,5},{7,4},{8,11},{9,10},{10,... | collective-permute-start | bytes 98312 | tf_op jit(solution)/shard_map/ppermute | solution.py:24
  22.4 4.8 %collective-permute-start.5 = (f32[4,1,2048]{2,1,0:T(1,128)S(1)}, f32[4,1,2048]{2,1,0:T(1,128)S(1)}, u32[]{:S(2)}, u32[]{:S(2)}) collective-permute-start(f32[4,1,2048]{2,1,0:T(1,128)S(1)} %pad_maximum_fusion.1), channel_id=1, source_target_pairs={{0,2},{1,3},{2,0},{3,1},{4,6},{5,7},{6,4},{7,5},{8,10},{9,11},{10,... | collective-permute-start | bytes 98312 | tf_op jit(solution)/shard_map/ppermute | solution.py:24
  22.4 4.8 %collective-permute-start.6 = (f32[4,1,2048]{2,1,0:T(1,128)S(1)}, f32[4,1,2048]{2,1,0:T(1,128)S(1)}, u32[]{:S(2)}, u32[]{:S(2)}) collective-permute-start(f32[4,1,2048]{2,1,0:T(1,128)S(1)} %pad_maximum_fusion.1), channel_id=1, source_target_pairs={{0,1},{1,0},{2,3},{3,2},{4,5},{5,4},{6,7},{7,6},{8,9},{9,8},{10,11... | collective-permute-start | bytes 98312 | tf_op jit(solution)/shard_map/ppermute | solution.py:24
  30.1 4.5 %collective-permute-start.8 = (f32[2,1,768]{2,1,0:T(1,128)S(1)}, f32[2,1,768]{2,1,0:T(1,128)S(1)}, u32[]{:S(2)}, u32[]{:S(2)}) collective-permute-start(f32[2,1,768]{2,1,0:T(1,128)S(1)} %add.151), channel_id=1, source_target_pairs={{0,24},{4,28},{8,16},{12,20},{16,8},{20,12},{24,0},{28,4},{1,25},{... | collective-permute-start | bytes 18440 | tf_op jit(solution)/shard_map/ppermute | solution.py:24
  37.3 5.6 %collective-permute-start.11 = (f32[2,1,2048]{2,1,0:T(1,128)S(1)}, f32[2,1,2048]{2,1,0:T(1,128)S(1)}, u32[]{:S(2)}, u32[]{:S(2)}) collective-permute-start(f32[2,1,2048]{2,1,0:T(1,128)S(1)} %row_totals.4), channel_id=1, source_target_pairs={{0,3},{1,2},{2,1},{3,0},{4,7},{5,6},{6,5},{7,4},{8,11},{9,10},{10,... | collective-permute-start | bytes 49160 | tf_op jit(solution)/shard_map/ppermute | solution.py:24
  38.8 4.7 %collective-permute-start.12 = (f32[2,1,2048]{2,1,0:T(1,128)S(1)}, f32[2,1,2048]{2,1,0:T(1,128)S(1)}, u32[]{:S(2)}, u32[]{:S(2)}) collective-permute-start(f32[2,1,2048]{2,1,0:T(1,128)S(1)} %row_totals.4), channel_id=1, source_target_pairs={{0,2},{1,3},{2,0},{3,1},{4,6},{5,7},{6,4},{7,5},{8,10},{9,11},{10,... | collective-permute-start | bytes 49160 | tf_op jit(solution)/shard_map/ppermute | solution.py:24
  39.4 4.2 %collective-permute-start.13 = (f32[2,1,2048]{2,1,0:T(1,128)S(1)}, f32[2,1,2048]{2,1,0:T(1,128)S(1)}, u32[]{:S(2)}, u32[]{:S(2)}) collective-permute-start(f32[2,1,2048]{2,1,0:T(1,128)S(1)} %row_totals.4), channel_id=1, source_target_pairs={{0,1},{1,0},{2,3},{3,2},{4,5},{5,4},{6,7},{7,6},{8,9},{9,8},{10,11... | collective-permute-start | bytes 49160 | tf_op jit(solution)/shard_map/ppermute | solution.py:24
  45.8 4.6 %collective-permute-start.15 = (f32[2,1,768]{2,1,0:T(1,128)S(1)}, f32[2,1,768]{2,1,0:T(1,128)S(1)}, u32[]{:S(2)}, u32[]{:S(2)}) collective-permute-start(f32[2,1,768]{2,1,0:T(1,128)S(1)} %add.158), channel_id=1, source_target_pairs={{0,24},{4,28},{8,16},{12,20},{16,8},{20,12},{24,0},{28,4},{1,25},{... | collective-permute-start | bytes 18440 | tf_op jit(solution)/shard_map/ppermute | solution.py:24
  52.7 5.6 %collective-permute-start.18 = (f32[2,1,2048]{2,1,0:T(1,128)S(1)}, f32[2,1,2048]{2,1,0:T(1,128)S(1)}, u32[]{:S(2)}, u32[]{:S(2)}) collective-permute-start(f32[2,1,2048]{2,1,0:T(1,128)S(1)} %row_totals.5), channel_id=1, source_target_pairs={{0,3},{1,2},{2,1},{3,0},{4,7},{5,6},{6,5},{7,4},{8,11},{9,10},{10,... | collective-permute-start | bytes 49160 | tf_op jit(solution)/shard_map/ppermute | solution.py:24
  55.2 4.7 %collective-permute-start.19 = (f32[2,1,2048]{2,1,0:T(1,128)S(1)}, f32[2,1,2048]{2,1,0:T(1,128)S(1)}, u32[]{:S(2)}, u32[]{:S(2)}) collective-permute-start(f32[2,1,2048]{2,1,0:T(1,128)S(1)} %row_totals.5), channel_id=1, source_target_pairs={{0,2},{1,3},{2,0},{3,1},{4,6},{5,7},{6,4},{7,5},{8,10},{9,11},{10,... | collective-permute-start | bytes 49160 | tf_op jit(solution)/shard_map/ppermute | solution.py:24
  56.1 3.9 %collective-permute-start.20 = (f32[2,1,2048]{2,1,0:T(1,128)S(1)}, f32[2,1,2048]{2,1,0:T(1,128)S(1)}, u32[]{:S(2)}, u32[]{:S(2)}) collective-permute-start(f32[2,1,2048]{2,1,0:T(1,128)S(1)} %row_totals.5), channel_id=1, source_target_pairs={{0,1},{1,0},{2,3},{3,2},{4,5},{5,4},{6,7},{7,6},{8,9},{9,8},{10,11... | collective-permute-start | bytes 49160 | tf_op jit(solution)/shard_map/ppermute | solution.py:24
  73.6 6.5 %collective-permute-start.26 = (f32[1,72,256]{2,1,0:T(8,128)S(1)}, f32[1,72,256]{2,1,0:T(8,128)S(1)}, u32[]{:S(2)}, u32[]{:S(2)}) collective-permute-start(f32[1,72,256]{2,1,0:T(8,128)S(1)} %get-tuple-element.32), channel_id=1, source_target_pairs={{0,24},{4,28},{8,16},{12,20},{16,8},{20,12},{24,0},{28,4},{1,25},{... | collective-permute-start | bytes 221192 | tf_op jit(solution)/shard_map/ppermute | solution.py:24
  75.1 6.2 %collective-permute-start.27 = (f32[1,72,256]{2,1,0:T(8,128)S(1)}, f32[1,72,256]{2,1,0:T(8,128)S(1)}, u32[]{:S(2)}, u32[]{:S(2)}) collective-permute-start(f32[1,72,256]{2,1,0:T(8,128)S(1)} %get-tuple-element.33), channel_id=1, source_target_pairs={{0,16},{4,20},{8,24},{12,28},{16,0},{20,4},{24,8},{28,12},{1,17},{... | collective-permute-start | bytes 221192 | tf_op jit(solution)/shard_map/ppermute | solution.py:24
  76.6 4.8 %collective-permute-start.28 = (f32[1,72,256]{2,1,0:T(8,128)S(1)}, f32[1,72,256]{2,1,0:T(8,128)S(1)}, u32[]{:S(2)}, u32[]{:S(2)}) collective-permute-start(f32[1,72,256]{2,1,0:T(8,128)S(1)} %get-tuple-element.34), channel_id=1, source_target_pairs={{0,8},{4,12},{8,0},{12,4},{16,24},{20,28},{24,16},{28,20},{1,9},{5... | collective-permute-start | bytes 221192 | tf_op jit(solution)/shard_map/ppermute | solution.py:24
  77.2 6.7 %collective-permute-start.23 = (f32[1,96,256]{2,1,0:T(8,128)S(1)}, f32[1,96,256]{2,1,0:T(8,128)S(1)}, u32[]{:S(2)}, u32[]{:S(2)}) collective-permute-start(f32[1,96,256]{2,1,0:T(8,128)S(1)} %get-tuple-element.29), channel_id=1, source_target_pairs={{0,24},{4,28},{8,16},{12,20},{16,8},{20,12},{24,0},{28,4},{1,25},{... | collective-permute-start | bytes 294920 | tf_op jit(solution)/shard_map/ppermute | solution.py:24
  78.6 7.3 %collective-permute-start.24 = (f32[1,96,256]{2,1,0:T(8,128)S(1)}, f32[1,96,256]{2,1,0:T(8,128)S(1)}, u32[]{:S(2)}, u32[]{:S(2)}) collective-permute-start(f32[1,96,256]{2,1,0:T(8,128)S(1)} %get-tuple-element.30), channel_id=1, source_target_pairs={{0,16},{4,20},{8,24},{12,28},{16,0},{20,4},{24,8},{28,12},{1,17},{... | collective-permute-start | bytes 294920 | tf_op jit(solution)/shard_map/ppermute | solution.py:24
  80.1 5.8 %collective-permute-start.25 = (f32[1,96,256]{2,1,0:T(8,128)S(1)}, f32[1,96,256]{2,1,0:T(8,128)S(1)}, u32[]{:S(2)}, u32[]{:S(2)}) collective-permute-start(f32[1,96,256]{2,1,0:T(8,128)S(1)} %get-tuple-element.31), channel_id=1, source_target_pairs={{0,8},{4,12},{8,0},{12,4},{16,24},{20,28},{24,16},{28,20},{1,9},{5... | collective-permute-start | bytes 294920 | tf_op jit(solution)/shard_map/ppermute | solution.py:24
  81.5 7.0 %collective-permute-start.29 = (f32[72,256]{1,0:T(8,128)S(1)}, f32[72,256]{1,0:T(8,128)S(1)}, u32[]{:S(2)}, u32[]{:S(2)}) collective-permute-start(f32[72,256]{1,0:T(8,128)S(1)} %add_bitcast_fusion), channel_id=1, source_target_pairs={{0,3},{1,2},{2,1},{3,0},{4,7},{5,6},{6,5},{7,4},{8,11},{9,10},{10,... | collective-permute-start | bytes 221192 | tf_op jit(solution)/shard_map/ppermute | solution.py:24
  82.9 8.0 %collective-permute-start.30 = (f32[72,256]{1,0:T(8,128)S(1)}, f32[72,256]{1,0:T(8,128)S(1)}, u32[]{:S(2)}, u32[]{:S(2)}) collective-permute-start(f32[72,256]{1,0:T(8,128)S(1)} %add_bitcast_fusion), channel_id=1, source_target_pairs={{0,2},{1,3},{2,0},{3,1},{4,6},{5,7},{6,4},{7,5},{8,10},{9,11},{10,... | collective-permute-start | bytes 221192 | tf_op jit(solution)/shard_map/ppermute | solution.py:24
  83.9 7.1 %collective-permute-start.31 = (f32[72,256]{1,0:T(8,128)S(1)}, f32[72,256]{1,0:T(8,128)S(1)}, u32[]{:S(2)}, u32[]{:S(2)}) collective-permute-start(f32[72,256]{1,0:T(8,128)S(1)} %add_bitcast_fusion), channel_id=1, source_target_pairs={{0,1},{1,0},{2,3},{3,2},{4,5},{5,4},{6,7},{7,6},{8,9},{9,8},{10,11... | collective-permute-start | bytes 221192 | tf_op jit(solution)/shard_map/ppermute | solution.py:24
  91.0 6.2 %collective-permute-start.32 = (bf16[1,160,256]{2,1,0:T(8,128)(2,1)S(1)}, bf16[1,160,256]{2,1,0:T(8,128)(2,1)S(1)}, u32[]{:S(2)}, u32[]{:S(2)}) collective-permute-start(bf16[1,160,256]{2,1,0:T(8,128)(2,1)S(1)} %pad_maximum_fusion), channel_id=1, source_target_pairs={{0,24},{4,28},{8,16},{12,20},{16,8},{20,12},{24,0},{28,4},{1,25},{... | collective-permute-start | bytes 245768 | tf_op jit(solution)/shard_map/ppermute | solution.py:24
  92.5 5.1 %collective-permute-start.33 = (bf16[1,160,256]{2,1,0:T(8,128)(2,1)S(1)}, bf16[1,160,256]{2,1,0:T(8,128)(2,1)S(1)}, u32[]{:S(2)}, u32[]{:S(2)}) collective-permute-start(bf16[1,160,256]{2,1,0:T(8,128)(2,1)S(1)} %pad_maximum_fusion), channel_id=1, source_target_pairs={{0,16},{4,20},{8,24},{12,28},{16,0},{20,4},{24,8},{28,12},{1,17},{... | collective-permute-start | bytes 245768 | tf_op jit(solution)/shard_map/ppermute | solution.py:24
  93.0 4.6 %collective-permute-start.34 = (bf16[1,160,256]{2,1,0:T(8,128)(2,1)S(1)}, bf16[1,160,256]{2,1,0:T(8,128)(2,1)S(1)}, u32[]{:S(2)}, u32[]{:S(2)}) collective-permute-start(bf16[1,160,256]{2,1,0:T(8,128)(2,1)S(1)} %pad_maximum_fusion), channel_id=1, source_target_pairs={{0,8},{4,12},{8,0},{12,4},{16,24},{20,28},{24,16},{28,20},{1,9},{5... | collective-permute-start | bytes 245768 | tf_op jit(solution)/shard_map/ppermute | solution.py:24
  (13 other events, 32.3 us)

commit v7 on v6

--- a/solution.py
+++ b/solution.py
@@ -16,7 +16,7 @@
 LANES = 128
 CHUNK = 256
 WIDE = 1024
-FINAL_TYPE = jnp.bfloat16
+FINAL_TYPE = jnp.float32
 VMEM_LIMIT = 22 * 1024 * 1024
 
 

time: 102 us -> 106 us (1.039)
  waiting for transfers between devices: 30.3 us -> 34.2 us
    ppermute x36, waiting for transfers between devices: 30.3 us -> 34.2 us  [swap(): return lax.ppermute(values, axis, [(i, i ^ offset) for i in range(size)])]
where the time goes in v7:
time: 106 us
  starting transfers between devices  41.8 us (39%)
  waiting for transfers between devices  34.2 us (32%)
  Pallas kernels  25 us (24%)
  between operations  2.68 us (3%)
  local copies, waits for them, and re-layouts  1.2 us (1%)
    ppermute x36, starting transfers between devices, swap(): return lax.ppermute(values, axis, [(i, i ^ offset) for i in range(size)])  41.8 us
    ppermute x36, waiting for transfers between devices, swap(): return lax.ppermute(values, axis, [(i, i ^ offset) for i in range(size)])  34.2 us
    pallas_call x7, Pallas kernels, call(): pl.pallas_call(kernel, in_specs=[IN_HBM if at in far_in else IN_VMEM for...  23.8 us
  transfers between devices with their start and end apart: 36, of which 29 were waited for; matrix products, arithmetic and copies ran while one was open for 1% of the time, Pallas kernels for 0%

profile of v7, /device:TPU:0, one launch (start us, length us, event | category | flops | bytes accessed | tf_op | source)
XLA Modules:
  0.0 105.6 jit_solution(5473028174622697286)
XLA Ops:
  0.6 7.7 %first_totals.1 = (f32[2,768,2048]{2,1,0:T(8,128)S(1)}, f32[2,1,768]{2,1,0:T(1,128)S(1)}, f32[2,1,2048]{2,1,0:T(1,128)S(1)}, bf16[768,256]{1,0:T(8,128)(2,1)S(1)...) custom-call(bf16[2048,2,512]{2,1,0:T(2,128)(2,1)} %feats_ref.1, ...), custom_call_target="tpu_custom_call" | custom-call | flops 1610612736 | bytes 1048576 | tf_op jit(solution)/shard_map/first_totals/pallas_call | solution.py:307
  9.6 3.9 %collective-permute-start.1 = (f32[2,1,768]{2,1,0:T(1,128)S(1)}, f32[2,1,768]{2,1,0:T(1,128)S(1)}, u32[]{:S(2)}, u32[]{:S(2)}) collective-permute-start(f32[2,1,768]{2,1,0:T(1,128)S(1)} %add.144), channel_id=1, source_target_pairs={{0,24},{4,28},{8,16},{12,20},{16,8},{20,12},{24,0},{28,4},{1,25},{... | collective-permute-start | bytes 18440 | tf_op jit(solution)/shard_map/ppermute | solution.py:24
  15.1 2.0 %collective-permute-done.2 = f32[2,1,768]{2,1,0:T(1,128)S(1)} collective-permute-done((f32[2,1,768]{2,1,0:T(1,128)S(1)}, f32[2,1,768]{2,1,0:T(1,128)S(1)}, u32[]{:S(2)}, u32[]{:S(2)}) %collective-permute-start.2) | collective-permute-done | bytes 6176 | tf_op jit(solution)/shard_map/ppermute | solution.py:24
  18.8 3.7 %collective-permute-start.4 = (f32[4,1,2048]{2,1,0:T(1,128)S(1)}, f32[4,1,2048]{2,1,0:T(1,128)S(1)}, u32[]{:S(2)}, u32[]{:S(2)}) collective-permute-start(f32[4,1,2048]{2,1,0:T(1,128)S(1)} %pad_maximum_fusion), channel_id=1, source_target_pairs={{0,3},{1,2},{2,1},{3,0},{4,7},{5,6},{6,5},{7,4},{8,11},{9,10},{10,... | collective-permute-start | bytes 98312 | tf_op jit(solution)/shard_map/ppermute | solution.py:24
  24.6 2.6 %collective-permute-done.5 = f32[4,1,2048]{2,1,0:T(1,128)S(1)} collective-permute-done((f32[4,1,2048]{2,1,0:T(1,128)S(1)}, f32[4,1,2048]{2,1,0:T(1,128)S(1)}, u32[]{:S(2)}, u32[]{:S(2)}) %collective-permute-start.5) | collective-permute-done | bytes 32800 | tf_op jit(solution)/shard_map/ppermute | solution.py:24
  30.1 2.4 %collective-permute-start.8 = (f32[2,1,768]{2,1,0:T(1,128)S(1)}, f32[2,1,768]{2,1,0:T(1,128)S(1)}, u32[]{:S(2)}, u32[]{:S(2)}) collective-permute-start(f32[2,1,768]{2,1,0:T(1,128)S(1)} %add.151), channel_id=1, source_target_pairs={{0,24},{4,28},{8,16},{12,20},{16,8},{20,12},{24,0},{28,4},{1,25},{... | collective-permute-start | bytes 18440 | tf_op jit(solution)/shard_map/ppermute | solution.py:24
  34.6 1.5 %collective-permute-done.9 = f32[2,1,768]{2,1,0:T(1,128)S(1)} collective-permute-done((f32[2,1,768]{2,1,0:T(1,128)S(1)}, f32[2,1,768]{2,1,0:T(1,128)S(1)}, u32[]{:S(2)}, u32[]{:S(2)}) %collective-permute-start.9) | collective-permute-done | bytes 6176 | tf_op jit(solution)/shard_map/ppermute | solution.py:24
  37.3 1.5 %collective-permute-start.11 = (f32[2,1,2048]{2,1,0:T(1,128)S(1)}, f32[2,1,2048]{2,1,0:T(1,128)S(1)}, u32[]{:S(2)}, u32[]{:S(2)}) collective-permute-start(f32[2,1,2048]{2,1,0:T(1,128)S(1)} %row_totals.4), channel_id=1, source_target_pairs={{0,3},{1,2},{2,1},{3,0},{4,7},{5,6},{6,5},{7,4},{8,11},{9,10},{10,... | collective-permute-start | bytes 49160 | tf_op jit(solution)/shard_map/ppermute | solution.py:24
  39.4 2.3 %collective-permute-start.13 = (f32[2,1,2048]{2,1,0:T(1,128)S(1)}, f32[2,1,2048]{2,1,0:T(1,128)S(1)}, u32[]{:S(2)}, u32[]{:S(2)}) collective-permute-start(f32[2,1,2048]{2,1,0:T(1,128)S(1)} %row_totals.4), channel_id=1, source_target_pairs={{0,1},{1,0},{2,3},{3,2},{4,5},{5,4},{6,7},{7,6},{8,9},{9,8},{10,11... | collective-permute-start | bytes 49160 | tf_op jit(solution)/shard_map/ppermute | solution.py:24
  47.8 1.5 %collective-permute-start.17 = (f32[2,1,768]{2,1,0:T(1,128)S(1)}, f32[2,1,768]{2,1,0:T(1,128)S(1)}, u32[]{:S(2)}, u32[]{:S(2)}) collective-permute-start(f32[2,1,768]{2,1,0:T(1,128)S(1)} %add.158), channel_id=1, source_target_pairs={{0,8},{4,12},{8,0},{12,4},{16,24},{20,28},{24,16},{28,20},{1,9},{5... | collective-permute-start | bytes 18440 | tf_op jit(solution)/shard_map/ppermute | solution.py:24
  52.7 2.5 %collective-permute-start.18 = (f32[2,1,2048]{2,1,0:T(1,128)S(1)}, f32[2,1,2048]{2,1,0:T(1,128)S(1)}, u32[]{:S(2)}, u32[]{:S(2)}) collective-permute-start(f32[2,1,2048]{2,1,0:T(1,128)S(1)} %row_totals.5), channel_id=1, source_target_pairs={{0,3},{1,2},{2,1},{3,0},{4,7},{5,6},{6,5},{7,4},{8,11},{9,10},{10,... | collective-permute-start | bytes 49160 | tf_op jit(solution)/shard_map/ppermute | solution.py:24
  58.3 1.5 %collective-permute-done.19 = f32[2,1,2048]{2,1,0:T(1,128)S(1)} collective-permute-done((f32[2,1,2048]{2,1,0:T(1,128)S(1)}, f32[2,1,2048]{2,1,0:T(1,128)S(1)}, u32[]{:S(2)}, u32[]{:S(2)}) %collective-permute-start.19) | collective-permute-done | bytes 16416 | tf_op jit(solution)/shard_map/ppermute | solution.py:24
  60.1 11.0 %gradients.1 = f32[8,168,256]{2,1,0:T(8,128)S(1)} custom-call(bf16[2,2048,512]{2,1,0:T(8,128)(2,1)} %get-tuple-element.20.feats_ref, f32[2,256,2048]{2,1,0:T(8,128)} %get-tuple-element.21.raw_ref, bf16[768,256]{1,0:T(8,128)(2,1)S(1)} %get-tuple-element.22.proto_ref, bf16[256,768]{1,0:T(8,128)(2,1)S(1)} %get-tuple-element.23.turned_ref, ...), custom_call_target="tpu_custom_call" | custom-call | flops 4831838208 | bytes 1048576 | tf_op jit(solution)/shard_map/gradients/pallas_call | solution.py:307
  73.6 1.5 %collective-permute-start.26 = (f32[1,72,256]{2,1,0:T(8,128)S(1)}, f32[1,72,256]{2,1,0:T(8,128)S(1)}, u32[]{:S(2)}, u32[]{:S(2)}) collective-permute-start(f32[1,72,256]{2,1,0:T(8,128)S(1)} %get-tuple-element.32), channel_id=1, source_target_pairs={{0,24},{4,28},{8,16},{12,20},{16,8},{20,12},{24,0},{28,4},{1,25},{... | collective-permute-start | bytes 221192 | tf_op jit(solution)/shard_map/ppermute | solution.py:24
  75.1 1.5 %collective-permute-start.27 = (f32[1,72,256]{2,1,0:T(8,128)S(1)}, f32[1,72,256]{2,1,0:T(8,128)S(1)}, u32[]{:S(2)}, u32[]{:S(2)}) collective-permute-start(f32[1,72,256]{2,1,0:T(8,128)S(1)} %get-tuple-element.33), channel_id=1, source_target_pairs={{0,16},{4,20},{8,24},{12,28},{16,0},{20,4},{24,8},{28,12},{1,17},{... | collective-permute-start | bytes 221192 | tf_op jit(solution)/shard_map/ppermute | solution.py:24
  78.6 1.5 %collective-permute-start.24 = (f32[1,96,256]{2,1,0:T(8,128)S(1)}, f32[1,96,256]{2,1,0:T(8,128)S(1)}, u32[]{:S(2)}, u32[]{:S(2)}) collective-permute-start(f32[1,96,256]{2,1,0:T(8,128)S(1)} %get-tuple-element.30), channel_id=1, source_target_pairs={{0,16},{4,20},{8,24},{12,28},{16,0},{20,4},{24,8},{28,12},{1,17},{... | collective-permute-start | bytes 294920 | tf_op jit(solution)/shard_map/ppermute | solution.py:24
  81.5 1.5 %collective-permute-start.29 = (f32[72,256]{1,0:T(8,128)S(1)}, f32[72,256]{1,0:T(8,128)S(1)}, u32[]{:S(2)}, u32[]{:S(2)}) collective-permute-start(f32[72,256]{1,0:T(8,128)S(1)} %add_bitcast_fusion), channel_id=1, source_target_pairs={{0,3},{1,2},{2,1},{3,0},{4,7},{5,6},{6,5},{7,4},{8,11},{9,10},{10,... | collective-permute-start | bytes 221192 | tf_op jit(solution)/shard_map/ppermute | solution.py:24
  83.9 2.0 %collective-permute-start.31 = (f32[72,256]{1,0:T(8,128)S(1)}, f32[72,256]{1,0:T(8,128)S(1)}, u32[]{:S(2)}, u32[]{:S(2)}) collective-permute-start(f32[72,256]{1,0:T(8,128)S(1)} %add_bitcast_fusion), channel_id=1, source_target_pairs={{0,1},{1,0},{2,3},{3,2},{4,5},{5,4},{6,7},{7,6},{8,9},{9,8},{10,11... | collective-permute-start | bytes 221192 | tf_op jit(solution)/shard_map/ppermute | solution.py:24
  86.2 2.3 %collective-permute-done.29 = f32[72,256]{1,0:T(8,128)S(1)} collective-permute-done((f32[72,256]{1,0:T(8,128)S(1)}, f32[72,256]{1,0:T(8,128)S(1)}, u32[]{:S(2)}, u32[]{:S(2)}) %collective-permute-start.29) | collective-permute-done | bytes 73760 | tf_op jit(solution)/shard_map/ppermute | solution.py:24
  88.5 2.5 %collective-permute-done.30 = f32[72,256]{1,0:T(8,128)S(1)} collective-permute-done((f32[72,256]{1,0:T(8,128)S(1)}, f32[72,256]{1,0:T(8,128)S(1)}, u32[]{:S(2)}, u32[]{:S(2)}) %collective-permute-start.30) | collective-permute-done | bytes 73760 | tf_op jit(solution)/shard_map/ppermute | solution.py:24
  91.0 1.5 %collective-permute-start.32 = (f32[1,160,256]{2,1,0:T(8,128)S(1)}, f32[1,160,256]{2,1,0:T(8,128)S(1)}, u32[]{:S(2)}, u32[]{:S(2)}) collective-permute-start(f32[1,160,256]{2,1,0:T(8,128)S(1)} %maximum_bitcast_fusion), channel_id=1, source_target_pairs={{0,24},{4,28},{8,16},{12,20},{16,8},{20,12},{24,0},{28,4},{1,25},{... | collective-permute-start | bytes 491528 | tf_op jit(solution)/shard_map/ppermute | solution.py:24
  93.0 1.6 %collective-permute-start.34 = (f32[1,160,256]{2,1,0:T(8,128)S(1)}, f32[1,160,256]{2,1,0:T(8,128)S(1)}, u32[]{:S(2)}, u32[]{:S(2)}) collective-permute-start(f32[1,160,256]{2,1,0:T(8,128)S(1)} %maximum_bitcast_fusion), channel_id=1, source_target_pairs={{0,8},{4,12},{8,0},{12,4},{16,24},{20,28},{24,16},{28,20},{1,9},{5... | collective-permute-start | bytes 491528 | tf_op jit(solution)/shard_map/ppermute | solution.py:24
  94.6 4.6 %collective-permute-done.32 = f32[1,160,256]{2,1,0:T(8,128)S(1)} collective-permute-done((f32[1,160,256]{2,1,0:T(8,128)S(1)}, f32[1,160,256]{2,1,0:T(8,128)S(1)}, u32[]{:S(2)}, u32[]{:S(2)}) %collective-permute-start.32) | collective-permute-done | bytes 163872 | tf_op jit(solution)/shard_map/ppermute | solution.py:24
  99.2 1.9 %collective-permute-done.33 = f32[1,160,256]{2,1,0:T(8,128)S(1)} collective-permute-done((f32[1,160,256]{2,1,0:T(8,128)S(1)}, f32[1,160,256]{2,1,0:T(8,128)S(1)}, u32[]{:S(2)}, u32[]{:S(2)}) %collective-permute-start.33) | collective-permute-done | bytes 163872 | tf_op jit(solution)/shard_map/ppermute | solution.py:24
  (91 shorter events, 36.6 us)
Async XLA Ops:
  9.6 5.5 %collective-permute-start.1 = (f32[2,1,768]{2,1,0:T(1,128)S(1)}, f32[2,1,768]{2,1,0:T(1,128)S(1)}, u32[]{:S(2)}, u32[]{:S(2)}) collective-permute-start(f32[2,1,768]{2,1,0:T(1,128)S(1)} %add.144), channel_id=1, source_target_pairs={{0,24},{4,28},{8,16},{12,20},{16,8},{20,12},{24,0},{28,4},{1,25},{... | collective-permute-start | bytes 18440 | tf_op jit(solution)/shard_map/ppermute | solution.py:24
  18.8 5.9 %collective-permute-start.4 = (f32[4,1,2048]{2,1,0:T(1,128)S(1)}, f32[4,1,2048]{2,1,0:T(1,128)S(1)}, u32[]{:S(2)}, u32[]{:S(2)}) collective-permute-start(f32[4,1,2048]{2,1,0:T(1,128)S(1)} %pad_maximum_fusion), channel_id=1, source_target_pairs={{0,3},{1,2},{2,1},{3,0},{4,7},{5,6},{6,5},{7,4},{8,11},{9,10},{10,... | collective-permute-start | bytes 98312 | tf_op jit(solution)/shard_map/ppermute | solution.py:24
  22.4 4.8 %collective-permute-start.5 = (f32[4,1,2048]{2,1,0:T(1,128)S(1)}, f32[4,1,2048]{2,1,0:T(1,128)S(1)}, u32[]{:S(2)}, u32[]{:S(2)}) collective-permute-start(f32[4,1,2048]{2,1,0:T(1,128)S(1)} %pad_maximum_fusion), channel_id=1, source_target_pairs={{0,2},{1,3},{2,0},{3,1},{4,6},{5,7},{6,4},{7,5},{8,10},{9,11},{10,... | collective-permute-start | bytes 98312 | tf_op jit(solution)/shard_map/ppermute | solution.py:24
  22.4 4.8 %collective-permute-start.6 = (f32[4,1,2048]{2,1,0:T(1,128)S(1)}, f32[4,1,2048]{2,1,0:T(1,128)S(1)}, u32[]{:S(2)}, u32[]{:S(2)}) collective-permute-start(f32[4,1,2048]{2,1,0:T(1,128)S(1)} %pad_maximum_fusion), channel_id=1, source_target_pairs={{0,1},{1,0},{2,3},{3,2},{4,5},{5,4},{6,7},{7,6},{8,9},{9,8},{10,11... | collective-permute-start | bytes 98312 | tf_op jit(solution)/shard_map/ppermute | solution.py:24
  30.1 4.5 %collective-permute-start.8 = (f32[2,1,768]{2,1,0:T(1,128)S(1)}, f32[2,1,768]{2,1,0:T(1,128)S(1)}, u32[]{:S(2)}, u32[]{:S(2)}) collective-permute-start(f32[2,1,768]{2,1,0:T(1,128)S(1)} %add.151), channel_id=1, source_target_pairs={{0,24},{4,28},{8,16},{12,20},{16,8},{20,12},{24,0},{28,4},{1,25},{... | collective-permute-start | bytes 18440 | tf_op jit(solution)/shard_map/ppermute | solution.py:24
  37.3 5.6 %collective-permute-start.11 = (f32[2,1,2048]{2,1,0:T(1,128)S(1)}, f32[2,1,2048]{2,1,0:T(1,128)S(1)}, u32[]{:S(2)}, u32[]{:S(2)}) collective-permute-start(f32[2,1,2048]{2,1,0:T(1,128)S(1)} %row_totals.4), channel_id=1, source_target_pairs={{0,3},{1,2},{2,1},{3,0},{4,7},{5,6},{6,5},{7,4},{8,11},{9,10},{10,... | collective-permute-start | bytes 49160 | tf_op jit(solution)/shard_map/ppermute | solution.py:24
  38.8 4.7 %collective-permute-start.12 = (f32[2,1,2048]{2,1,0:T(1,128)S(1)}, f32[2,1,2048]{2,1,0:T(1,128)S(1)}, u32[]{:S(2)}, u32[]{:S(2)}) collective-permute-start(f32[2,1,2048]{2,1,0:T(1,128)S(1)} %row_totals.4), channel_id=1, source_target_pairs={{0,2},{1,3},{2,0},{3,1},{4,6},{5,7},{6,4},{7,5},{8,10},{9,11},{10,... | collective-permute-start | bytes 49160 | tf_op jit(solution)/shard_map/ppermute | solution.py:24
  39.4 4.2 %collective-permute-start.13 = (f32[2,1,2048]{2,1,0:T(1,128)S(1)}, f32[2,1,2048]{2,1,0:T(1,128)S(1)}, u32[]{:S(2)}, u32[]{:S(2)}) collective-permute-start(f32[2,1,2048]{2,1,0:T(1,128)S(1)} %row_totals.4), channel_id=1, source_target_pairs={{0,1},{1,0},{2,3},{3,2},{4,5},{5,4},{6,7},{7,6},{8,9},{9,8},{10,11... | collective-permute-start | bytes 49160 | tf_op jit(solution)/shard_map/ppermute | solution.py:24
  45.8 4.6 %collective-permute-start.15 = (f32[2,1,768]{2,1,0:T(1,128)S(1)}, f32[2,1,768]{2,1,0:T(1,128)S(1)}, u32[]{:S(2)}, u32[]{:S(2)}) collective-permute-start(f32[2,1,768]{2,1,0:T(1,128)S(1)} %add.158), channel_id=1, source_target_pairs={{0,24},{4,28},{8,16},{12,20},{16,8},{20,12},{24,0},{28,4},{1,25},{... | collective-permute-start | bytes 18440 | tf_op jit(solution)/shard_map/ppermute | solution.py:24
  52.7 5.6 %collective-permute-start.18 = (f32[2,1,2048]{2,1,0:T(1,128)S(1)}, f32[2,1,2048]{2,1,0:T(1,128)S(1)}, u32[]{:S(2)}, u32[]{:S(2)}) collective-permute-start(f32[2,1,2048]{2,1,0:T(1,128)S(1)} %row_totals.5), channel_id=1, source_target_pairs={{0,3},{1,2},{2,1},{3,0},{4,7},{5,6},{6,5},{7,4},{8,11},{9,10},{10,... | collective-permute-start | bytes 49160 | tf_op jit(solution)/shard_map/ppermute | solution.py:24
  55.2 4.7 %collective-permute-start.19 = (f32[2,1,2048]{2,1,0:T(1,128)S(1)}, f32[2,1,2048]{2,1,0:T(1,128)S(1)}, u32[]{:S(2)}, u32[]{:S(2)}) collective-permute-start(f32[2,1,2048]{2,1,0:T(1,128)S(1)} %row_totals.5), channel_id=1, source_target_pairs={{0,2},{1,3},{2,0},{3,1},{4,6},{5,7},{6,4},{7,5},{8,10},{9,11},{10,... | collective-permute-start | bytes 49160 | tf_op jit(solution)/shard_map/ppermute | solution.py:24
  56.1 3.9 %collective-permute-start.20 = (f32[2,1,2048]{2,1,0:T(1,128)S(1)}, f32[2,1,2048]{2,1,0:T(1,128)S(1)}, u32[]{:S(2)}, u32[]{:S(2)}) collective-permute-start(f32[2,1,2048]{2,1,0:T(1,128)S(1)} %row_totals.5), channel_id=1, source_target_pairs={{0,1},{1,0},{2,3},{3,2},{4,5},{5,4},{6,7},{7,6},{8,9},{9,8},{10,11... | collective-permute-start | bytes 49160 | tf_op jit(solution)/shard_map/ppermute | solution.py:24
  73.6 6.5 %collective-permute-start.26 = (f32[1,72,256]{2,1,0:T(8,128)S(1)}, f32[1,72,256]{2,1,0:T(8,128)S(1)}, u32[]{:S(2)}, u32[]{:S(2)}) collective-permute-start(f32[1,72,256]{2,1,0:T(8,128)S(1)} %get-tuple-element.32), channel_id=1, source_target_pairs={{0,24},{4,28},{8,16},{12,20},{16,8},{20,12},{24,0},{28,4},{1,25},{... | collective-permute-start | bytes 221192 | tf_op jit(solution)/shard_map/ppermute | solution.py:24
  75.1 6.2 %collective-permute-start.27 = (f32[1,72,256]{2,1,0:T(8,128)S(1)}, f32[1,72,256]{2,1,0:T(8,128)S(1)}, u32[]{:S(2)}, u32[]{:S(2)}) collective-permute-start(f32[1,72,256]{2,1,0:T(8,128)S(1)} %get-tuple-element.33), channel_id=1, source_target_pairs={{0,16},{4,20},{8,24},{12,28},{16,0},{20,4},{24,8},{28,12},{1,17},{... | collective-permute-start | bytes 221192 | tf_op jit(solution)/shard_map/ppermute | solution.py:24
  76.6 4.8 %collective-permute-start.28 = (f32[1,72,256]{2,1,0:T(8,128)S(1)}, f32[1,72,256]{2,1,0:T(8,128)S(1)}, u32[]{:S(2)}, u32[]{:S(2)}) collective-permute-start(f32[1,72,256]{2,1,0:T(8,128)S(1)} %get-tuple-element.34), channel_id=1, source_target_pairs={{0,8},{4,12},{8,0},{12,4},{16,24},{20,28},{24,16},{28,20},{1,9},{5... | collective-permute-start | bytes 221192 | tf_op jit(solution)/shard_map/ppermute | solution.py:24
  77.2 6.7 %collective-permute-start.23 = (f32[1,96,256]{2,1,0:T(8,128)S(1)}, f32[1,96,256]{2,1,0:T(8,128)S(1)}, u32[]{:S(2)}, u32[]{:S(2)}) collective-permute-start(f32[1,96,256]{2,1,0:T(8,128)S(1)} %get-tuple-element.29), channel_id=1, source_target_pairs={{0,24},{4,28},{8,16},{12,20},{16,8},{20,12},{24,0},{28,4},{1,25},{... | collective-permute-start | bytes 294920 | tf_op jit(solution)/shard_map/ppermute | solution.py:24
  78.6 7.3 %collective-permute-start.24 = (f32[1,96,256]{2,1,0:T(8,128)S(1)}, f32[1,96,256]{2,1,0:T(8,128)S(1)}, u32[]{:S(2)}, u32[]{:S(2)}) collective-permute-start(f32[1,96,256]{2,1,0:T(8,128)S(1)} %get-tuple-element.30), channel_id=1, source_target_pairs={{0,16},{4,20},{8,24},{12,28},{16,0},{20,4},{24,8},{28,12},{1,17},{... | collective-permute-start | bytes 294920 | tf_op jit(solution)/shard_map/ppermute | solution.py:24
  80.1 5.8 %collective-permute-start.25 = (f32[1,96,256]{2,1,0:T(8,128)S(1)}, f32[1,96,256]{2,1,0:T(8,128)S(1)}, u32[]{:S(2)}, u32[]{:S(2)}) collective-permute-start(f32[1,96,256]{2,1,0:T(8,128)S(1)} %get-tuple-element.31), channel_id=1, source_target_pairs={{0,8},{4,12},{8,0},{12,4},{16,24},{20,28},{24,16},{28,20},{1,9},{5... | collective-permute-start | bytes 294920 | tf_op jit(solution)/shard_map/ppermute | solution.py:24
  81.5 7.0 %collective-permute-start.29 = (f32[72,256]{1,0:T(8,128)S(1)}, f32[72,256]{1,0:T(8,128)S(1)}, u32[]{:S(2)}, u32[]{:S(2)}) collective-permute-start(f32[72,256]{1,0:T(8,128)S(1)} %add_bitcast_fusion), channel_id=1, source_target_pairs={{0,3},{1,2},{2,1},{3,0},{4,7},{5,6},{6,5},{7,4},{8,11},{9,10},{10,... | collective-permute-start | bytes 221192 | tf_op jit(solution)/shard_map/ppermute | solution.py:24
  82.9 8.0 %collective-permute-start.30 = (f32[72,256]{1,0:T(8,128)S(1)}, f32[72,256]{1,0:T(8,128)S(1)}, u32[]{:S(2)}, u32[]{:S(2)}) collective-permute-start(f32[72,256]{1,0:T(8,128)S(1)} %add_bitcast_fusion), channel_id=1, source_target_pairs={{0,2},{1,3},{2,0},{3,1},{4,6},{5,7},{6,4},{7,5},{8,10},{9,11},{10,... | collective-permute-start | bytes 221192 | tf_op jit(solution)/shard_map/ppermute | solution.py:24
  83.9 7.1 %collective-permute-start.31 = (f32[72,256]{1,0:T(8,128)S(1)}, f32[72,256]{1,0:T(8,128)S(1)}, u32[]{:S(2)}, u32[]{:S(2)}) collective-permute-start(f32[72,256]{1,0:T(8,128)S(1)} %add_bitcast_fusion), channel_id=1, source_target_pairs={{0,1},{1,0},{2,3},{3,2},{4,5},{5,4},{6,7},{7,6},{8,9},{9,8},{10,11... | collective-permute-start | bytes 221192 | tf_op jit(solution)/shard_map/ppermute | solution.py:24
  91.0 8.1 %collective-permute-start.32 = (f32[1,160,256]{2,1,0:T(8,128)S(1)}, f32[1,160,256]{2,1,0:T(8,128)S(1)}, u32[]{:S(2)}, u32[]{:S(2)}) collective-permute-start(f32[1,160,256]{2,1,0:T(8,128)S(1)} %maximum_bitcast_fusion), channel_id=1, source_target_pairs={{0,24},{4,28},{8,16},{12,20},{16,8},{20,12},{24,0},{28,4},{1,25},{... | collective-permute-start | bytes 491528 | tf_op jit(solution)/shard_map/ppermute | solution.py:24
  92.5 8.7 %collective-permute-start.33 = (f32[1,160,256]{2,1,0:T(8,128)S(1)}, f32[1,160,256]{2,1,0:T(8,128)S(1)}, u32[]{:S(2)}, u32[]{:S(2)}) collective-permute-start(f32[1,160,256]{2,1,0:T(8,128)S(1)} %maximum_bitcast_fusion), channel_id=1, source_target_pairs={{0,16},{4,20},{8,24},{12,28},{16,0},{20,4},{24,8},{28,12},{1,17},{... | collective-permute-start | bytes 491528 | tf_op jit(solution)/shard_map/ppermute | solution.py:24
  93.0 8.1 %collective-permute-start.34 = (f32[1,160,256]{2,1,0:T(8,128)S(1)}, f32[1,160,256]{2,1,0:T(8,128)S(1)}, u32[]{:S(2)}, u32[]{:S(2)}) collective-permute-start(f32[1,160,256]{2,1,0:T(8,128)S(1)} %maximum_bitcast_fusion), channel_id=1, source_target_pairs={{0,8},{4,12},{8,0},{12,4},{16,24},{20,28},{24,16},{28,20},{1,9},{5... | collective-permute-start | bytes 491528 | tf_op jit(solution)/shard_map/ppermute | solution.py:24
  (13 other events, 32.8 us)

commit v8 on v6

--- a/solution.py
+++ b/solution.py
@@ -15,6 +15,7 @@
 LOG2_E = 1.4426950408889634
 LANES = 128
 CHUNK = 256
+GRAD_CHUNK = 384
 WIDE = 1024
 FINAL_TYPE = jnp.bfloat16
 VMEM_LIMIT = 22 * 1024 * 1024
@@ -34,10 +35,12 @@
     return groups
 
 
-def sum_over(values, axis, first):
+def sum_over(values, axis, first, wire=jnp.float32):
     size = lax.axis_size(axis)
     for low, width in stages(size, first):
-        parts = [swap(values, axis, size, k << low) for k in reversed(range(1, 1 << width))]
+        sent = values.astype(wire)
+        order = (2, 3, 1) if width == 2 and axis == "mp" else reversed(range(1, 1 << width))
+        parts = [swap(sent, axis, size, k << low).astype(values.dtype) for k in order]
         values = functools.reduce(jnp.add, parts, values)
     return values
 
@@ -244,16 +247,18 @@
         raw = jnp.concatenate([raw_in_ref[view, :, lanes] for view in range(2)], axis=1)
         unit, inverse = unit_columns(raw)
         halves = unit.astype(jnp.bfloat16)
-        for start in range(0, proto_ref.shape[0], CHUNK):
-            part = slice(start, start + CHUNK)
+        row_scales = [factor / row_ref[view, :, lanes] for view in range(2)]
+        denom_scales = [factor / denom_ref[view, :, lanes] for view in range(2)]
+        for start in range(0, proto_ref.shape[0], GRAD_CHUNK):
+            part = slice(start, start + GRAD_CHUNK)
             logits = [product(proto_ref[part], halves[:, side], NN) for side in sides]
             softs = [jnp.exp2(logits[view] * (LOG2_E / SOFTMAX_TEMPER)) for view in range(2)]
             for view in range(2):
                 other = 1 - view
                 target = softs[other] * softs[other] * widen(scale_ref[other, part], width)
-                target = target * (factor / row_ref[other, :, lanes])
+                target = target * row_scales[other]
                 loss = loss + jnp.sum((logits[view] * target).reshape(-1, 8, width), axis=0)
-                grad = softs[view] * (factor / denom_ref[view, :, lanes]) - target
+                grad = softs[view] * denom_scales[view] - target
                 grad_ref[part, sides[view]] = grad.astype(jnp.bfloat16)
         proto_part = product(grad_ref[...], halves, NT)
         grad_unit = product(turned_ref[...], grad_ref[...], NN)
@@ -360,7 +365,8 @@
     row_sums, denoms = both[:2], both[2:]
     for iteration in range(1, ITERS):
         col_sums = sum_over(col_call(row_sums)[0], "dp", 1)
-        row_sums = sum_over(row_call(col_sums)[0], "mp", 2)
+        wire = single if iteration == ITERS - 1 else half_type
+        row_sums = sum_over(row_call(col_sums)[0], "mp", 2, wire)
 
     parts = call(
         functools.partial(grad_kernel, valid, 1024, factor), "gradients",

time: 102 us -> 101 us (level)
  starting transfers between devices: 41.8 us -> 38.9 us
  waiting for transfers between devices: 30.3 us -> 32.7 us
    ppermute x36, starting transfers between devices: 41.8 us -> 38.9 us  [swap(): return lax.ppermute(values, axis, [(i, i ^ offset) for i in range(size)])]
    ppermute x36, waiting for transfers between devices: 30.3 us -> 32.7 us  [swap(): return lax.ppermute(values, axis, [(i, i ^ offset) for i in range(size)])]
where the time goes in v8:
time: 101 us
  starting transfers between devices  38.9 us (39%)
  waiting for transfers between devices  32.7 us (32%)
  Pallas kernels  24.9 us (25%)
  between operations  2.68 us (3%)
  local copies, waits for them, and re-layouts  1.16 us (1%)
    ppermute x36, starting transfers between devices, swap(): return lax.ppermute(values, axis, [(i, i ^ offset) for i in range(size)])  38.9 us
    ppermute x36, waiting for transfers between devices, swap(): return lax.ppermute(values, axis, [(i, i ^ offset) for i in range(size)])  32.7 us
    pallas_call x7, Pallas kernels, call(): pl.pallas_call(kernel, in_specs=[IN_HBM if at in far_in else IN_VMEM for...  23.8 us
  transfers between devices with their start and end apart: 36, of which 29 were waited for; matrix products, arithmetic and copies ran while one was open for 1% of the time, Pallas kernels for 0%

profile of v8, /device:TPU:0, one launch (start us, length us, event | category | flops | bytes accessed | tf_op | source)
XLA Modules:
  0.0 101.1 jit_solution(12791724787703884603)
XLA Ops:
  0.6 7.7 %first_totals.1 = (f32[2,768,2048]{2,1,0:T(8,128)S(1)}, f32[2,1,768]{2,1,0:T(1,128)S(1)}, f32[2,1,2048]{2,1,0:T(1,128)S(1)}, bf16[768,256]{1,0:T(8,128)(2,1)S(1)...) custom-call(bf16[2048,2,512]{2,1,0:T(2,128)(2,1)} %feats_ref.1, ...), custom_call_target="tpu_custom_call" | custom-call | flops 1610612736 | bytes 1048576 | tf_op jit(solution)/shard_map/first_totals/pallas_call | solution.py:312
  9.6 3.9 %collective-permute-start.1 = (f32[2,1,768]{2,1,0:T(1,128)S(1)}, f32[2,1,768]{2,1,0:T(1,128)S(1)}, u32[]{:S(2)}, u32[]{:S(2)}) collective-permute-start(f32[2,1,768]{2,1,0:T(1,128)S(1)} %add.144), channel_id=1, source_target_pairs={{0,24},{4,28},{8,16},{12,20},{16,8},{20,12},{24,0},{28,4},{1,25},{... | collective-permute-start | bytes 18440 | tf_op jit(solution)/shard_map/ppermute | solution.py:25
  15.1 2.0 %collective-permute-done.2 = f32[2,1,768]{2,1,0:T(1,128)S(1)} collective-permute-done((f32[2,1,768]{2,1,0:T(1,128)S(1)}, f32[2,1,768]{2,1,0:T(1,128)S(1)}, u32[]{:S(2)}, u32[]{:S(2)}) %collective-permute-start.2) | collective-permute-done | bytes 6176 | tf_op jit(solution)/shard_map/ppermute | solution.py:25
  18.8 2.7 %collective-permute-start.4 = (f32[4,1,2048]{2,1,0:T(1,128)S(1)}, f32[4,1,2048]{2,1,0:T(1,128)S(1)}, u32[]{:S(2)}, u32[]{:S(2)}) collective-permute-start(f32[4,1,2048]{2,1,0:T(1,128)S(1)} %pad_maximum_fusion.1), channel_id=1, source_target_pairs={{0,2},{1,3},{2,0},{3,1},{4,6},{5,7},{6,4},{7,5},{8,10},{9,11},{10,... | collective-permute-start | bytes 98312 | tf_op jit(solution)/shard_map/ppermute | solution.py:25
  21.4 1.3 %collective-permute-start.5 = (f32[4,1,2048]{2,1,0:T(1,128)S(1)}, f32[4,1,2048]{2,1,0:T(1,128)S(1)}, u32[]{:S(2)}, u32[]{:S(2)}) collective-permute-start(f32[4,1,2048]{2,1,0:T(1,128)S(1)} %pad_maximum_fusion.1), channel_id=1, source_target_pairs={{0,3},{1,2},{2,1},{3,0},{4,7},{5,6},{6,5},{7,4},{8,11},{9,10},{10,... | collective-permute-start | bytes 98312 | tf_op jit(solution)/shard_map/ppermute | solution.py:25
  24.0 3.2 %collective-permute-done.5 = f32[4,1,2048]{2,1,0:T(1,128)S(1)} collective-permute-done((f32[4,1,2048]{2,1,0:T(1,128)S(1)}, f32[4,1,2048]{2,1,0:T(1,128)S(1)}, u32[]{:S(2)}, u32[]{:S(2)}) %collective-permute-start.5) | collective-permute-done | bytes 32800 | tf_op jit(solution)/shard_map/ppermute | solution.py:25
  30.0 2.4 %collective-permute-start.8 = (f32[2,1,768]{2,1,0:T(1,128)S(1)}, f32[2,1,768]{2,1,0:T(1,128)S(1)}, u32[]{:S(2)}, u32[]{:S(2)}) collective-permute-start(f32[2,1,768]{2,1,0:T(1,128)S(1)} %add.151), channel_id=1, source_target_pairs={{0,24},{4,28},{8,16},{12,20},{16,8},{20,12},{24,0},{28,4},{1,25},{... | collective-permute-start | bytes 18440 | tf_op jit(solution)/shard_map/ppermute | solution.py:25
  33.1 1.4 %collective-permute-done.8 = f32[2,1,768]{2,1,0:T(1,128)S(1)} collective-permute-done((f32[2,1,768]{2,1,0:T(1,128)S(1)}, f32[2,1,768]{2,1,0:T(1,128)S(1)}, u32[]{:S(2)}, u32[]{:S(2)}) %collective-permute-start.8) | collective-permute-done | bytes 6176 | tf_op jit(solution)/shard_map/ppermute | solution.py:25
  34.5 1.5 %collective-permute-done.9 = f32[2,1,768]{2,1,0:T(1,128)S(1)} collective-permute-done((f32[2,1,768]{2,1,0:T(1,128)S(1)}, f32[2,1,768]{2,1,0:T(1,128)S(1)}, u32[]{:S(2)}, u32[]{:S(2)}) %collective-permute-start.9) | collective-permute-done | bytes 6176 | tf_op jit(solution)/shard_map/ppermute | solution.py:25
  37.2 1.3 %collective-permute-start.11 = (bf16[2,1,2048]{2,1,0:T(2,128)(2,1)S(1)}, bf16[2,1,2048]{2,1,0:T(2,128)(2,1)S(1)}, u32[]{:S(2)}, u32[]{:S(2)}) collective-permute-start(bf16[2,1,2048]{2,1,0:T(2,128)(2,1)S(1)} %convert_element_type.23), channel_id=1, source_target_pairs={{0,2},{1,3},{2,0},{3,1},{4,6},{5,7},{6,4},{7,5},{8,10},{9,11},{10,... | collective-permute-start | bytes 24584 | tf_op jit(solution)/shard_map/ppermute | solution.py:25
  41.9 2.1 %collective-permute-done.12 = bf16[2,1,2048]{2,1,0:T(2,128)(2,1)S(1)} collective-permute-done((bf16[2,1,2048]{2,1,0:T(2,128)(2,1)S(1)}, bf16[2,1,2048]{2,1,0:T(2,128)(2,1)S(1)}, u32[]{:S(2)}, u32[]{:S(2)}) %collective-permute-start.12) | collective-permute-done | bytes 8224 | tf_op jit(solution)/shard_map/ppermute | solution.py:25
  48.3 1.5 %collective-permute-start.17 = (f32[2,1,768]{2,1,0:T(1,128)S(1)}, f32[2,1,768]{2,1,0:T(1,128)S(1)}, u32[]{:S(2)}, u32[]{:S(2)}) collective-permute-start(f32[2,1,768]{2,1,0:T(1,128)S(1)} %add.158), channel_id=1, source_target_pairs={{0,8},{4,12},{8,0},{12,4},{16,24},{20,28},{24,16},{28,20},{1,9},{5... | collective-permute-start | bytes 18440 | tf_op jit(solution)/shard_map/ppermute | solution.py:25
  54.2 1.8 %collective-permute-start.19 = (f32[2,1,2048]{2,1,0:T(1,128)S(1)}, f32[2,1,2048]{2,1,0:T(1,128)S(1)}, u32[]{:S(2)}, u32[]{:S(2)}) collective-permute-start(f32[2,1,2048]{2,1,0:T(1,128)S(1)} %row_totals.5), channel_id=1, source_target_pairs={{0,3},{1,2},{2,1},{3,0},{4,7},{5,6},{6,5},{7,4},{8,11},{9,10},{10,... | collective-permute-start | bytes 49160 | tf_op jit(solution)/shard_map/ppermute | solution.py:25
  56.7 1.3 %collective-permute-done.18 = f32[2,1,2048]{2,1,0:T(1,128)S(1)} collective-permute-done((f32[2,1,2048]{2,1,0:T(1,128)S(1)}, f32[2,1,2048]{2,1,0:T(1,128)S(1)}, u32[]{:S(2)}, u32[]{:S(2)}) %collective-permute-start.18) | collective-permute-done | bytes 16416 | tf_op jit(solution)/shard_map/ppermute | solution.py:25
  58.0 1.8 %collective-permute-done.19 = f32[2,1,2048]{2,1,0:T(1,128)S(1)} collective-permute-done((f32[2,1,2048]{2,1,0:T(1,128)S(1)}, f32[2,1,2048]{2,1,0:T(1,128)S(1)}, u32[]{:S(2)}, u32[]{:S(2)}) %collective-permute-start.19) | collective-permute-done | bytes 16416 | tf_op jit(solution)/shard_map/ppermute | solution.py:25
  60.0 10.9 %gradients.1 = f32[8,168,256]{2,1,0:T(8,128)S(1)} custom-call(bf16[2,2048,512]{2,1,0:T(8,128)(2,1)} %get-tuple-element.20.feats_ref, f32[2,256,2048]{2,1,0:T(8,128)} %get-tuple-element.21.raw_ref, bf16[768,256]{1,0:T(8,128)(2,1)S(1)} %get-tuple-element.22.proto_ref, bf16[256,768]{1,0:T(8,128)(2,1)S(1)} %get-tuple-element.23.turned_ref, ...), custom_call_target="tpu_custom_call" | custom-call | flops 4831838208 | bytes 1048576 | tf_op jit(solution)/shard_map/gradients/pallas_call | solution.py:312
  73.5 1.5 %collective-permute-start.26 = (f32[1,72,256]{2,1,0:T(8,128)S(1)}, f32[1,72,256]{2,1,0:T(8,128)S(1)}, u32[]{:S(2)}, u32[]{:S(2)}) collective-permute-start(f32[1,72,256]{2,1,0:T(8,128)S(1)} %get-tuple-element.32), channel_id=1, source_target_pairs={{0,24},{4,28},{8,16},{12,20},{16,8},{20,12},{24,0},{28,4},{1,25},{... | collective-permute-start | bytes 221192 | tf_op jit(solution)/shard_map/ppermute | solution.py:25
  75.0 1.5 %collective-permute-start.27 = (f32[1,72,256]{2,1,0:T(8,128)S(1)}, f32[1,72,256]{2,1,0:T(8,128)S(1)}, u32[]{:S(2)}, u32[]{:S(2)}) collective-permute-start(f32[1,72,256]{2,1,0:T(8,128)S(1)} %get-tuple-element.33), channel_id=1, source_target_pairs={{0,16},{4,20},{8,24},{12,28},{16,0},{20,4},{24,8},{28,12},{1,17},{... | collective-permute-start | bytes 221192 | tf_op jit(solution)/shard_map/ppermute | solution.py:25
  77.0 1.4 %collective-permute-start.23 = (f32[1,96,256]{2,1,0:T(8,128)S(1)}, f32[1,96,256]{2,1,0:T(8,128)S(1)}, u32[]{:S(2)}, u32[]{:S(2)}) collective-permute-start(f32[1,96,256]{2,1,0:T(8,128)S(1)} %get-tuple-element.29), channel_id=1, source_target_pairs={{0,24},{4,28},{8,16},{12,20},{16,8},{20,12},{24,0},{28,4},{1,25},{... | collective-permute-start | bytes 294920 | tf_op jit(solution)/shard_map/ppermute | solution.py:25
  78.5 1.5 %collective-permute-start.24 = (f32[1,96,256]{2,1,0:T(8,128)S(1)}, f32[1,96,256]{2,1,0:T(8,128)S(1)}, u32[]{:S(2)}, u32[]{:S(2)}) collective-permute-start(f32[1,96,256]{2,1,0:T(8,128)S(1)} %get-tuple-element.30), channel_id=1, source_target_pairs={{0,16},{4,20},{8,24},{12,28},{16,0},{20,4},{24,8},{28,12},{1,17},{... | collective-permute-start | bytes 294920 | tf_op jit(solution)/shard_map/ppermute | solution.py:25
  82.4 1.8 %collective-permute-start.30 = (f32[72,256]{1,0:T(8,128)S(1)}, f32[72,256]{1,0:T(8,128)S(1)}, u32[]{:S(2)}, u32[]{:S(2)}) collective-permute-start(f32[72,256]{1,0:T(8,128)S(1)} %add_bitcast_fusion), channel_id=1, source_target_pairs={{0,3},{1,2},{2,1},{3,0},{4,7},{5,6},{6,5},{7,4},{8,11},{9,10},{10,... | collective-permute-start | bytes 221192 | tf_op jit(solution)/shard_map/ppermute | solution.py:25
  85.2 4.7 %collective-permute-done.29 = f32[72,256]{1,0:T(8,128)S(1)} collective-permute-done((f32[72,256]{1,0:T(8,128)S(1)}, f32[72,256]{1,0:T(8,128)S(1)}, u32[]{:S(2)}, u32[]{:S(2)}) %collective-permute-start.29) | collective-permute-done | bytes 73760 | tf_op jit(solution)/shard_map/ppermute | solution.py:25
  90.0 1.7 %collective-permute-start.32 = (bf16[1,160,256]{2,1,0:T(8,128)(2,1)S(1)}, bf16[1,160,256]{2,1,0:T(8,128)(2,1)S(1)}, u32[]{:S(2)}, u32[]{:S(2)}) collective-permute-start(bf16[1,160,256]{2,1,0:T(8,128)(2,1)S(1)} %pad_maximum_fusion), channel_id=1, source_target_pairs={{0,24},{4,28},{8,16},{12,20},{16,8},{20,12},{24,0},{28,4},{1,25},{... | collective-permute-start | bytes 245768 | tf_op jit(solution)/shard_map/ppermute | solution.py:25
  93.6 2.7 %collective-permute-done.32 = bf16[1,160,256]{2,1,0:T(8,128)(2,1)S(1)} collective-permute-done((bf16[1,160,256]{2,1,0:T(8,128)(2,1)S(1)}, bf16[1,160,256]{2,1,0:T(8,128)(2,1)S(1)}, u32[]{:S(2)}, u32[]{:S(2)}) %collective-permute-start.32) | collective-permute-done | bytes 81952 | tf_op jit(solution)/shard_map/ppermute | solution.py:25
  (92 shorter events, 34.7 us)
Async XLA Ops:
  9.6 5.5 %collective-permute-start.1 = (f32[2,1,768]{2,1,0:T(1,128)S(1)}, f32[2,1,768]{2,1,0:T(1,128)S(1)}, u32[]{:S(2)}, u32[]{:S(2)}) collective-permute-start(f32[2,1,768]{2,1,0:T(1,128)S(1)} %add.144), channel_id=1, source_target_pairs={{0,24},{4,28},{8,16},{12,20},{16,8},{20,12},{24,0},{28,4},{1,25},{... | collective-permute-start | bytes 18440 | tf_op jit(solution)/shard_map/ppermute | solution.py:25
  18.8 5.2 %collective-permute-start.4 = (f32[4,1,2048]{2,1,0:T(1,128)S(1)}, f32[4,1,2048]{2,1,0:T(1,128)S(1)}, u32[]{:S(2)}, u32[]{:S(2)}) collective-permute-start(f32[4,1,2048]{2,1,0:T(1,128)S(1)} %pad_maximum_fusion.1), channel_id=1, source_target_pairs={{0,2},{1,3},{2,0},{3,1},{4,6},{5,7},{6,4},{7,5},{8,10},{9,11},{10,... | collective-permute-start | bytes 98312 | tf_op jit(solution)/shard_map/ppermute | solution.py:25
  21.4 5.7 %collective-permute-start.5 = (f32[4,1,2048]{2,1,0:T(1,128)S(1)}, f32[4,1,2048]{2,1,0:T(1,128)S(1)}, u32[]{:S(2)}, u32[]{:S(2)}) collective-permute-start(f32[4,1,2048]{2,1,0:T(1,128)S(1)} %pad_maximum_fusion.1), channel_id=1, source_target_pairs={{0,3},{1,2},{2,1},{3,0},{4,7},{5,6},{6,5},{7,4},{8,11},{9,10},{10,... | collective-permute-start | bytes 98312 | tf_op jit(solution)/shard_map/ppermute | solution.py:25
  22.8 4.4 %collective-permute-start.6 = (f32[4,1,2048]{2,1,0:T(1,128)S(1)}, f32[4,1,2048]{2,1,0:T(1,128)S(1)}, u32[]{:S(2)}, u32[]{:S(2)}) collective-permute-start(f32[4,1,2048]{2,1,0:T(1,128)S(1)} %pad_maximum_fusion.1), channel_id=1, source_target_pairs={{0,1},{1,0},{2,3},{3,2},{4,5},{5,4},{6,7},{7,6},{8,9},{9,8},{10,11... | collective-permute-start | bytes 98312 | tf_op jit(solution)/shard_map/ppermute | solution.py:25
  30.0 4.5 %collective-permute-start.8 = (f32[2,1,768]{2,1,0:T(1,128)S(1)}, f32[2,1,768]{2,1,0:T(1,128)S(1)}, u32[]{:S(2)}, u32[]{:S(2)}) collective-permute-start(f32[2,1,768]{2,1,0:T(1,128)S(1)} %add.151), channel_id=1, source_target_pairs={{0,24},{4,28},{8,16},{12,20},{16,8},{20,12},{24,0},{28,4},{1,25},{... | collective-permute-start | bytes 18440 | tf_op jit(solution)/shard_map/ppermute | solution.py:25
  37.2 4.7 %collective-permute-start.11 = (bf16[2,1,2048]{2,1,0:T(2,128)(2,1)S(1)}, bf16[2,1,2048]{2,1,0:T(2,128)(2,1)S(1)}, u32[]{:S(2)}, u32[]{:S(2)}) collective-permute-start(bf16[2,1,2048]{2,1,0:T(2,128)(2,1)S(1)} %convert_element_type.23), channel_id=1, source_target_pairs={{0,2},{1,3},{2,0},{3,1},{4,6},{5,7},{6,4},{7,5},{8,10},{9,11},{10,... | collective-permute-start | bytes 24584 | tf_op jit(solution)/shard_map/ppermute | solution.py:25
  38.5 5.5 %collective-permute-start.12 = (bf16[2,1,2048]{2,1,0:T(2,128)(2,1)S(1)}, bf16[2,1,2048]{2,1,0:T(2,128)(2,1)S(1)}, u32[]{:S(2)}, u32[]{:S(2)}) collective-permute-start(bf16[2,1,2048]{2,1,0:T(2,128)(2,1)S(1)} %convert_element_type.23), channel_id=1, source_target_pairs={{0,3},{1,2},{2,1},{3,0},{4,7},{5,6},{6,5},{7,4},{8,11},{9,10},{10,... | collective-permute-start | bytes 24584 | tf_op jit(solution)/shard_map/ppermute | solution.py:25
  39.5 4.5 %collective-permute-start.13 = (bf16[2,1,2048]{2,1,0:T(2,128)(2,1)S(1)}, bf16[2,1,2048]{2,1,0:T(2,128)(2,1)S(1)}, u32[]{:S(2)}, u32[]{:S(2)}) collective-permute-start(bf16[2,1,2048]{2,1,0:T(2,128)(2,1)S(1)} %convert_element_type.23), channel_id=1, source_target_pairs={{0,1},{1,0},{2,3},{3,2},{4,5},{5,4},{6,7},{7,6},{8,9},{9,8},{10,11... | collective-permute-start | bytes 24584 | tf_op jit(solution)/shard_map/ppermute | solution.py:25
  46.2 4.6 %collective-permute-start.15 = (f32[2,1,768]{2,1,0:T(1,128)S(1)}, f32[2,1,768]{2,1,0:T(1,128)S(1)}, u32[]{:S(2)}, u32[]{:S(2)}) collective-permute-start(f32[2,1,768]{2,1,0:T(1,128)S(1)} %add.158), channel_id=1, source_target_pairs={{0,24},{4,28},{8,16},{12,20},{16,8},{20,12},{24,0},{28,4},{1,25},{... | collective-permute-start | bytes 18440 | tf_op jit(solution)/shard_map/ppermute | solution.py:25
  53.2 4.8 %collective-permute-start.18 = (f32[2,1,2048]{2,1,0:T(1,128)S(1)}, f32[2,1,2048]{2,1,0:T(1,128)S(1)}, u32[]{:S(2)}, u32[]{:S(2)}) collective-permute-start(f32[2,1,2048]{2,1,0:T(1,128)S(1)} %row_totals.5), channel_id=1, source_target_pairs={{0,2},{1,3},{2,0},{3,1},{4,6},{5,7},{6,4},{7,5},{8,10},{9,11},{10,... | collective-permute-start | bytes 49160 | tf_op jit(solution)/shard_map/ppermute | solution.py:25
  54.2 5.6 %collective-permute-start.19 = (f32[2,1,2048]{2,1,0:T(1,128)S(1)}, f32[2,1,2048]{2,1,0:T(1,128)S(1)}, u32[]{:S(2)}, u32[]{:S(2)}) collective-permute-start(f32[2,1,2048]{2,1,0:T(1,128)S(1)} %row_totals.5), channel_id=1, source_target_pairs={{0,3},{1,2},{2,1},{3,0},{4,7},{5,6},{6,5},{7,4},{8,11},{9,10},{10,... | collective-permute-start | bytes 49160 | tf_op jit(solution)/shard_map/ppermute | solution.py:25
  56.0 3.9 %collective-permute-start.20 = (f32[2,1,2048]{2,1,0:T(1,128)S(1)}, f32[2,1,2048]{2,1,0:T(1,128)S(1)}, u32[]{:S(2)}, u32[]{:S(2)}) collective-permute-start(f32[2,1,2048]{2,1,0:T(1,128)S(1)} %row_totals.5), channel_id=1, source_target_pairs={{0,1},{1,0},{2,3},{3,2},{4,5},{5,4},{6,7},{7,6},{8,9},{9,8},{10,11... | collective-permute-start | bytes 49160 | tf_op jit(solution)/shard_map/ppermute | solution.py:25
  73.5 6.5 %collective-permute-start.26 = (f32[1,72,256]{2,1,0:T(8,128)S(1)}, f32[1,72,256]{2,1,0:T(8,128)S(1)}, u32[]{:S(2)}, u32[]{:S(2)}) collective-permute-start(f32[1,72,256]{2,1,0:T(8,128)S(1)} %get-tuple-element.32), channel_id=1, source_target_pairs={{0,24},{4,28},{8,16},{12,20},{16,8},{20,12},{24,0},{28,4},{1,25},{... | collective-permute-start | bytes 221192 | tf_op jit(solution)/shard_map/ppermute | solution.py:25
  75.0 6.2 %collective-permute-start.27 = (f32[1,72,256]{2,1,0:T(8,128)S(1)}, f32[1,72,256]{2,1,0:T(8,128)S(1)}, u32[]{:S(2)}, u32[]{:S(2)}) collective-permute-start(f32[1,72,256]{2,1,0:T(8,128)S(1)} %get-tuple-element.33), channel_id=1, source_target_pairs={{0,16},{4,20},{8,24},{12,28},{16,0},{20,4},{24,8},{28,12},{1,17},{... | collective-permute-start | bytes 221192 | tf_op jit(solution)/shard_map/ppermute | solution.py:25
  76.5 4.8 %collective-permute-start.28 = (f32[1,72,256]{2,1,0:T(8,128)S(1)}, f32[1,72,256]{2,1,0:T(8,128)S(1)}, u32[]{:S(2)}, u32[]{:S(2)}) collective-permute-start(f32[1,72,256]{2,1,0:T(8,128)S(1)} %get-tuple-element.34), channel_id=1, source_target_pairs={{0,8},{4,12},{8,0},{12,4},{16,24},{20,28},{24,16},{28,20},{1,9},{5... | collective-permute-start | bytes 221192 | tf_op jit(solution)/shard_map/ppermute | solution.py:25
  77.0 7.2 %collective-permute-start.23 = (f32[1,96,256]{2,1,0:T(8,128)S(1)}, f32[1,96,256]{2,1,0:T(8,128)S(1)}, u32[]{:S(2)}, u32[]{:S(2)}) collective-permute-start(f32[1,96,256]{2,1,0:T(8,128)S(1)} %get-tuple-element.29), channel_id=1, source_target_pairs={{0,24},{4,28},{8,16},{12,20},{16,8},{20,12},{24,0},{28,4},{1,25},{... | collective-permute-start | bytes 294920 | tf_op jit(solution)/shard_map/ppermute | solution.py:25
  78.5 6.4 %collective-permute-start.24 = (f32[1,96,256]{2,1,0:T(8,128)S(1)}, f32[1,96,256]{2,1,0:T(8,128)S(1)}, u32[]{:S(2)}, u32[]{:S(2)}) collective-permute-start(f32[1,96,256]{2,1,0:T(8,128)S(1)} %get-tuple-element.30), channel_id=1, source_target_pairs={{0,16},{4,20},{8,24},{12,28},{16,0},{20,4},{24,8},{28,12},{1,17},{... | collective-permute-start | bytes 294920 | tf_op jit(solution)/shard_map/ppermute | solution.py:25
  80.0 4.9 %collective-permute-start.25 = (f32[1,96,256]{2,1,0:T(8,128)S(1)}, f32[1,96,256]{2,1,0:T(8,128)S(1)}, u32[]{:S(2)}, u32[]{:S(2)}) collective-permute-start(f32[1,96,256]{2,1,0:T(8,128)S(1)} %get-tuple-element.31), channel_id=1, source_target_pairs={{0,8},{4,12},{8,0},{12,4},{16,24},{20,28},{24,16},{28,20},{1,9},{5... | collective-permute-start | bytes 294920 | tf_op jit(solution)/shard_map/ppermute | solution.py:25
  81.3 8.5 %collective-permute-start.29 = (f32[72,256]{1,0:T(8,128)S(1)}, f32[72,256]{1,0:T(8,128)S(1)}, u32[]{:S(2)}, u32[]{:S(2)}) collective-permute-start(f32[72,256]{1,0:T(8,128)S(1)} %add_bitcast_fusion), channel_id=1, source_target_pairs={{0,2},{1,3},{2,0},{3,1},{4,6},{5,7},{6,4},{7,5},{8,10},{9,11},{10,... | collective-permute-start | bytes 221192 | tf_op jit(solution)/shard_map/ppermute | solution.py:25
  82.4 7.4 %collective-permute-start.30 = (f32[72,256]{1,0:T(8,128)S(1)}, f32[72,256]{1,0:T(8,128)S(1)}, u32[]{:S(2)}, u32[]{:S(2)}) collective-permute-start(f32[72,256]{1,0:T(8,128)S(1)} %add_bitcast_fusion), channel_id=1, source_target_pairs={{0,3},{1,2},{2,1},{3,0},{4,7},{5,6},{6,5},{7,4},{8,11},{9,10},{10,... | collective-permute-start | bytes 221192 | tf_op jit(solution)/shard_map/ppermute | solution.py:25
  84.2 5.8 %collective-permute-start.31 = (f32[72,256]{1,0:T(8,128)S(1)}, f32[72,256]{1,0:T(8,128)S(1)}, u32[]{:S(2)}, u32[]{:S(2)}) collective-permute-start(f32[72,256]{1,0:T(8,128)S(1)} %add_bitcast_fusion), channel_id=1, source_target_pairs={{0,1},{1,0},{2,3},{3,2},{4,5},{5,4},{6,7},{7,6},{8,9},{9,8},{10,11... | collective-permute-start | bytes 221192 | tf_op jit(solution)/shard_map/ppermute | solution.py:25
  90.0 6.3 %collective-permute-start.32 = (bf16[1,160,256]{2,1,0:T(8,128)(2,1)S(1)}, bf16[1,160,256]{2,1,0:T(8,128)(2,1)S(1)}, u32[]{:S(2)}, u32[]{:S(2)}) collective-permute-start(bf16[1,160,256]{2,1,0:T(8,128)(2,1)S(1)} %pad_maximum_fusion), channel_id=1, source_target_pairs={{0,24},{4,28},{8,16},{12,20},{16,8},{20,12},{24,0},{28,4},{1,25},{... | collective-permute-start | bytes 245768 | tf_op jit(solution)/shard_map/ppermute | solution.py:25
  91.8 4.9 %collective-permute-start.33 = (bf16[1,160,256]{2,1,0:T(8,128)(2,1)S(1)}, bf16[1,160,256]{2,1,0:T(8,128)(2,1)S(1)}, u32[]{:S(2)}, u32[]{:S(2)}) collective-permute-start(bf16[1,160,256]{2,1,0:T(8,128)(2,1)S(1)} %pad_maximum_fusion), channel_id=1, source_target_pairs={{0,16},{4,20},{8,24},{12,28},{16,0},{20,4},{24,8},{28,12},{1,17},{... | collective-permute-start | bytes 245768 | tf_op jit(solution)/shard_map/ppermute | solution.py:25
  92.7 4.4 %collective-permute-start.34 = (bf16[1,160,256]{2,1,0:T(8,128)(2,1)S(1)}, bf16[1,160,256]{2,1,0:T(8,128)(2,1)S(1)}, u32[]{:S(2)}, u32[]{:S(2)}) collective-permute-start(bf16[1,160,256]{2,1,0:T(8,128)(2,1)S(1)} %pad_maximum_fusion), channel_id=1, source_target_pairs={{0,8},{4,12},{8,0},{12,4},{16,24},{20,28},{24,16},{28,20},{1,9},{5... | collective-permute-start | bytes 245768 | tf_op jit(solution)/shard_map/ppermute | solution.py:25
  (13 other events, 32.3 us)
